TPU v7x, 256 devices: a whole 4x4x8 slice. The times are simulated.
256 devices in a mesh: layer: 2 (over core), row: 32 (over x, z), col: 4 (over y).
Axes of the slice: x: 4, y: 4, z: 8, core: 2. Of those that a mesh axis runs over, the one named last changes fastest.
Arguments:
- tile_values: bfloat16 [2, 32, 4, 256, 128, 128], P('layer', 'row', 'col'), may hold values from -0.5 to 0.5
- tile_rows: int32 [2, 32, 4, 256], P('layer', 'row', 'col'), may hold values from 0 to 31
- tile_cols: int32 [2, 32, 4, 256], P('layer', 'row', 'col'), may hold values from 0 to 63
- tile_count: int32 [2, 32, 4], P('layer', 'row', 'col'), may hold values from 64 to 256, as said below
- start_panel: bfloat16 [32768, 128], P('col'), may hold values from -6 to 6
Outputs:
- caller_panel: bfloat16 [32, 4096, 128], P('row', ('layer', 'col'))
- dest_panel: bfloat16 [4, 8192, 128], P('col', ('layer', 'row'))
Inputs may be any that keep to these rules, and one draw needn't show every extreme that they name: tile_count reaches 256 on some device.
All inputs are finite; a program needn't handle non-finite values.
Results may differ from a plain program's by a relative error of at most 0.0049.
Values may be sent and summed in bfloat16 or wider, within the bound.
No kernel may reach another device: no remote copies, remote signals or barrier semaphores. Data moves between devices by JAX's collectives and lax.ppermute only.
A program may use at most 128 MiB of HBM per device.

v0:
```python
import functools

import jax
import jax.numpy as jnp
from jax import lax
from jax.experimental import pallas as pl
from jax.experimental.pallas import tpu as pltpu
from jax.sharding import Mesh
from jax.sharding import PartitionSpec as P

TILE = 128
RANK = 128
CTILES = 32
DTILES = 64
NX = 4
NZ = 8
NCOL = 4
NDST = 32768
N_SLOTS = 256
SLOT_BITS, ROW_BITS, COL_BITS = 8, 5, 6
BLOCK = 64
UNROLL = 16
STEPS = 4
EPS = 1e-06

F32 = jnp.float32
BF16 = jnp.bfloat16
CORE, XPOS, COL = 0, 1, 2

SMEM = pl.BlockSpec(memory_space=pltpu.SMEM)
VMEM = pl.BlockSpec(memory_space=pltpu.VMEM)
HBM = pl.BlockSpec(memory_space=pltpu.HBM)
PARAMS = pltpu.CompilerParams(vmem_limit_bytes=40 * 2**20)


def tiles_of(n, dtype):
    return jax.ShapeDtypeStruct((n, TILE, RANK), dtype)


def each(n, body):
    whole = n // STEPS

    def step(i, carry):
        for j in range(STEPS):
            body(i * STEPS + j)
        return carry

    if whole > 1:
        lax.fori_loop(0, whole, step, 0)
    for i in range(whole * STEPS if whole > 1 else 0, n):
        body(i)


def accumulate(lo, hi, live, order, tiles, panel, acc, by_row, keep):
    dump = acc.shape[0] - 1

    def group(g, carry):
        for j in range(UNROLL):
            k = g * UNROLL + j
            code = order[N_SLOTS - 1 - k] if keep else order[k]
            row, col = (code >> SLOT_BITS) & (CTILES - 1), code >> (SLOT_BITS + ROW_BITS)
            dst, src = (row, col) if by_row else (col, row)
            tile, block = tiles[code & (N_SLOTS - 1)], panel[src]
            a, b = (tile, block) if by_row else (block, tile)
            acc[jnp.where(k < live, dst & (dump - 1), dump)] += jnp.dot(a, b, preferred_element_type=F32)
        return carry

    lax.fori_loop(lo, hi, group, 0)


def groups(n):
    return (n + UNROLL - 1) // UNROLL


def zero(acc):
    def one(i):
        acc[i] = jnp.zeros((TILE, RANK), F32)

    each(acc.shape[0], one)


def narrow(acc, out):
    def one(i):
        out[i] = acc[i].astype(BF16)

    each(out.shape[0], one)


def sort_slots(first, size, rows, cols, live, core, by_row, by_col, counts):
    def one(i, carry):
        row_sends, row_keeps, col_sends, col_keeps = carry
        t = first + i
        row, col = rows[t], cols[t]
        code = t + (row << SLOT_BITS) + (col << (SLOT_BITS + ROW_BITS))
        used = t < live
        row_own = jnp.where(jnp.logical_and(used, row >> (ROW_BITS - 1) == core), 1, 0)
        col_own = jnp.where(jnp.logical_and(used, col >> (COL_BITS - 1) == core), 1, 0)
        by_row[jnp.where(row_own == 1, N_SLOTS - 1 - row_keeps, row_sends)] = code
        by_col[jnp.where(col_own == 1, N_SLOTS - 1 - col_keeps, col_sends)] = code
        return row_sends + 1 - row_own, row_keeps + row_own, col_sends + 1 - col_own, col_keeps + col_own

    return lax.fori_loop(0, size, one, counts, unroll=4)


def place(ids, parts, panel, axis, n, per):
    core, me = ids[CORE], ids[axis]
    for side in range(2):
        base = jnp.where(side == 0, core, 1 - core) * (n * per)
        for k in range(n):
            at = base + lax.rem(me + n - k, n) * per
            part = parts[side * n + k]

            def one(i):
                panel[at + i] = part[i]

            each(per, one)


def first_send_kernel(
    rows_hbm, cols_hbm, count, ids, tiles_hbm, panel_hbm, send, by_row, by_col, numbers, tiles, panel, rows, cols, acc, sems
):
    lists = [
        pltpu.make_async_copy(rows_hbm, rows, sems.at[0]),
        pltpu.make_async_copy(cols_hbm, cols, sems.at[1]),
    ]
    start = pltpu.make_async_copy(panel_hbm, panel, sems.at[2])
    blocks = [
        pltpu.make_async_copy(
            tiles_hbm.at[pl.ds(i * BLOCK, BLOCK)], tiles.at[pl.ds(i * BLOCK, BLOCK)], sems.at[3 + i]
        )
        for i in range(N_SLOTS // BLOCK)
    ]
    for copy in lists + [start] + blocks:
        copy.start()
    zero(acc)
    for copy in lists:
        copy.wait()
    live, core = count[0], ids[CORE]
    counts, done, last = (0, 0, 0, 0), 0, N_SLOTS // BLOCK - 1
    for i in range(last + 1):
        counts = sort_slots(i * BLOCK, BLOCK, rows, cols, live, core, by_row, by_col, counts)
        sends = jnp.minimum(live, (i + 1) * BLOCK) - counts[1]
        if i == 0:
            start.wait()
        blocks[i].wait()
        until = groups(sends) if i == last else sends // UNROLL
        accumulate(done, until, sends, by_row, tiles, panel, acc, True, False)
        done = until
    numbers[0] = live - counts[1]
    numbers[1] = counts[1]
    numbers[2] = live - counts[3]
    numbers[3] = counts[3]
    narrow(acc, send)


def in_hbm(value):
    return pltpu.with_memory_space_constraint(value, pltpu.HBM)


def first_send(rows, cols, count, ids, tiles, start):
    n = rows.shape[0]
    words = lambda k: jax.ShapeDtypeStruct((k,), jnp.int32)
    return pl.pallas_call(
        first_send_kernel,
        in_specs=[HBM, HBM, SMEM, SMEM, HBM, HBM],
        out_specs=[VMEM, SMEM, SMEM, SMEM, VMEM, VMEM],
        out_shape=[tiles_of(CTILES // 2, BF16), words(n), words(n), words(4), tiles_of(n, BF16), tiles_of(DTILES, BF16)],
        scratch_shapes=[
            pltpu.SMEM((n,), jnp.int32),
            pltpu.SMEM((n,), jnp.int32),
            pltpu.VMEM((CTILES // 2 + 1, TILE, RANK), F32),
            pltpu.SemaphoreType.DMA((3 + n // BLOCK,)),
        ],
        compiler_params=PARAMS,
        name="first_send",
    )(*(in_hbm(v) for v in (rows, cols)), count, ids, *(in_hbm(v) for v in (tiles, start)))


def send_kernel(order, numbers, ids, tiles, *refs, by_row, axis, n, per):
    parts, (send, panel, acc) = refs[: 2 * n], refs[2 * n :]
    zero(acc)
    place(ids, parts, panel, axis, n, per)
    sends = numbers[0 if by_row else 2]
    accumulate(0, groups(sends), sends, order, tiles, panel, acc, by_row, False)
    narrow(acc, send)


def send_part(order, numbers, ids, tiles, parts, by_row, axis, name):
    n = len(parts) // 2
    per = parts[0].shape[0]
    half = (CTILES if by_row else DTILES) // 2
    return pl.pallas_call(
        functools.partial(send_kernel, by_row=by_row, axis=axis, n=n, per=per),
        in_specs=[SMEM] * 3 + [VMEM] * (1 + len(parts)),
        out_specs=[VMEM, VMEM],
        out_shape=[tiles_of(half, BF16), tiles_of(2 * n * per, BF16)],
        scratch_shapes=[pltpu.VMEM((half + 1, TILE, RANK), F32)],
        compiler_params=PARAMS,
        name=name,
    )(order, numbers, ids, tiles, *parts)


def keep_kernel(order, numbers, tiles, panel, keep, *squares, by_row):
    zero(keep)
    keeps = numbers[1 if by_row else 3]
    accumulate(0, groups(keeps), keeps, order, tiles, panel, keep, by_row, True)
    if squares:

        def one(i, total):
            block = panel[i].astype(F32)
            return total + jnp.sum((block * block).reshape(4, TILE // 4, RANK), axis=0)

        squares[0][...] = lax.fori_loop(0, DTILES, one, jnp.zeros((TILE // 4, RANK), F32))


def keep_part(order, numbers, tiles, panel, by_row, extra, name):
    half = (CTILES if by_row else DTILES) // 2
    work = 2 * N_SLOTS * TILE * TILE * RANK
    return pl.pallas_call(
        functools.partial(keep_kernel, by_row=by_row),
        in_specs=[SMEM, SMEM, VMEM, VMEM],
        out_specs=[VMEM] * (1 + len(extra)),
        out_shape=[tiles_of(half + 1, F32)] + extra,
        compiler_params=PARAMS,
        cost_estimate=pl.CostEstimate(flops=work, bytes_accessed=10 * 2**20, transcendentals=0),
        name=name,
    )(order, numbers, tiles, panel)


def pair_kernel(ids, keep, got, own, *sends, axis, n, per):
    me = ids[axis]
    for k in range(n):
        base = lax.rem(me + k, n) * per

        def one(i):
            total = keep[base + i] + got[base + i].astype(F32)
            if k == 0:
                own[i] = total
            else:
                sends[k - 1][i] = total.astype(BF16)

        each(per, one)


def pair_sum(ids, keep, got, axis, n, per, name):
    return pl.pallas_call(
        functools.partial(pair_kernel, axis=axis, n=n, per=per),
        in_specs=[SMEM, VMEM, VMEM],
        out_specs=[VMEM] * n,
        out_shape=[tiles_of(per, F32)] + [tiles_of(per, BF16)] * (n - 1),
        compiler_params=PARAMS,
        name=name,
    )(ids, keep, got)


def caller_kernel(own, a, b, c, out):
    def one(i):
        total = own[i] + a[i].astype(F32) + b[i].astype(F32) + c[i].astype(F32)
        out[i] = total.astype(BF16).astype(F32).T.astype(BF16)

    each(own.shape[0], one)


def row_kernel(own, a, b, c, out):
    def one(i):
        total = own[i] + a[i].astype(F32) + b[i].astype(F32) + c[i].astype(F32)
        out[i] = total.astype(BF16)

    each(own.shape[0], one)


def four_sum(kernel, own, got, name):
    return pl.pallas_call(
        kernel,
        in_specs=[VMEM] * 4,
        out_specs=VMEM,
        out_shape=tiles_of(own.shape[0], BF16),
        compiler_params=PARAMS,
        name=name,
    )(own, *got)


def share_kernel(got, share, copies):
    total = got[0].astype(F32)
    for k in range(1, NZ):
        total += got[k].astype(F32)
    total = total.T
    share[...] = total
    for k in range(NZ):
        copies[k] = total.astype(BF16)


def last_pair_kernel(ids, keep, got, squares, own, *sends):
    me = ids[COL]
    per = CTILES // 2 // NCOL
    total = jnp.sum(squares[...], axis=0, keepdims=True)
    high = total.astype(BF16).astype(F32)
    middle = (total - high).astype(BF16).astype(F32)
    low = total - high - middle
    row = lax.broadcasted_iota(jnp.int32, (16, RANK), 0)
    coded = jnp.where(row == 0, high, jnp.where(row == 1, middle, jnp.where(row == 2, low, 0.0)))
    for k in range(NCOL):
        base = lax.rem(me + k, NCOL) * per
        if k:
            sends[k - 1][pl.ds(per * TILE, 16), :] = coded.astype(BF16)
        for i in range(per):
            part = keep[base + i] + got[base + i].astype(F32)
            if k == 0:
                own[i] = part
            else:
                sends[k - 1][pl.ds(i * TILE, TILE), :] = part.astype(BF16)


def final_kernel(own, squares, share, a, b, c, caller, dest):
    per = CTILES // 2 // NCOL
    total = jnp.sum(squares[...], axis=0, keepdims=True)
    for got in (a, b, c):
        total += jnp.sum(got[pl.ds(per * TILE, 16), :].astype(F32), axis=0, keepdims=True)
    scale = lax.rsqrt(total / NDST + EPS)
    dest[...] = (share[...] * scale).astype(BF16)
    for i in range(per):
        at = pl.ds(i * TILE, TILE)
        part = own[i] + a[at, :].astype(F32) + b[at, :].astype(F32) + c[at, :].astype(F32)
        caller[at, :] = (part * scale).astype(BF16)


def shifted(value, axis, k, n):
    return lax.ppermute(value, axis, [(i, (i + k) % n) for i in range(n)])


def swap(value):
    return lax.ppermute(value, "layer", [(0, 1), (1, 0)])


def exchange(values, axis, n):
    return [shifted(v, axis, k + 1, n) for k, v in enumerate(values)]


def gather(value, axis, n):
    mine = [value] + [shifted(value, axis, k, n) for k in range(1, n)]
    return mine + [swap(v) for v in mine]


def on_device(tile_values, tile_rows, tile_cols, tile_count, start_panel):
    tiles = tile_values[0, 0, 0]
    rows = tile_rows[0, 0, 0]
    cols = tile_cols[0, 0, 0]
    count = tile_count[0, 0]
    ids = jnp.stack([lax.axis_index(a) for a in ("layer", "x", "col")]).astype(jnp.int32)
    start = start_panel.reshape(DTILES, TILE, RANK)
    quarter = CTILES // 2 // NCOL

    send, by_row, by_col, numbers, tiles, panel = first_send(rows, cols, count, ids, tiles, start)
    got = swap(send)
    [keep] = keep_part(by_row, numbers, tiles, panel, True, [], "first_keep")
    own, *sends = pair_sum(ids, keep, got, COL, NCOL, quarter, "first_pair")
    part = four_sum(caller_kernel, own, exchange(sends, "col", NCOL), "first_sum")
    parts = gather(part, "col", NCOL)

    send, panel = send_part(by_col, numbers, ids, tiles, parts, False, COL, "back_send")
    got = swap(send)
    [keep] = keep_part(by_col, numbers, tiles, panel, False, [], "back_keep")
    own, *sends = pair_sum(ids, keep, got, XPOS, NX, NZ, "back_pair")
    part = four_sum(row_kernel, own, exchange(sends, "x", NX), "back_sum")
    got = lax.all_to_all(part, "z", split_axis=0, concat_axis=0, tiled=True)
    share, copies = pl.pallas_call(
        share_kernel,
        in_specs=[VMEM],
        out_specs=[VMEM, VMEM],
        out_shape=[jax.ShapeDtypeStruct((TILE, RANK), F32), tiles_of(NZ, BF16)],
        compiler_params=PARAMS,
        name="share_sum",
    )(got)
    part = lax.all_to_all(copies, "z", split_axis=0, concat_axis=0, tiled=True)
    parts = gather(part, "x", NX)

    send, panel = send_part(by_row, numbers, ids, tiles, parts, True, XPOS, "last_send")
    got = swap(send)
    keep, squares = keep_part(
        by_row, numbers, tiles, panel, True, [jax.ShapeDtypeStruct((TILE // 4, RANK), F32)], "last_keep"
    )
    chunk = jax.ShapeDtypeStruct((quarter * TILE + 16, RANK), BF16)
    own, *sends = pl.pallas_call(
        last_pair_kernel,
        in_specs=[SMEM, VMEM, VMEM, VMEM],
        out_specs=[VMEM] * NCOL,
        out_shape=[tiles_of(quarter, F32)] + [chunk] * (NCOL - 1),
        compiler_params=PARAMS,
        name="last_pair",
    )(ids, keep, got, squares)
    got = exchange(sends, "col", NCOL)
    caller, dest = pl.pallas_call(
        final_kernel,
        in_specs=[VMEM] * 6,
        out_specs=[VMEM, VMEM],
        out_shape=[
            jax.ShapeDtypeStruct((quarter * TILE, RANK), BF16),
            jax.ShapeDtypeStruct((TILE, RANK), BF16),
        ],
        compiler_params=PARAMS,
        name="final",
    )(own, squares, share, *got)
    return caller[None], dest[None]


def solution(mesh):
    fine = Mesh(mesh.devices.reshape(2, NX, NZ, NCOL), ("layer", "x", "z", "col"))
    row = ("x", "z")
    placed = (
        P("layer", row, "col", None, None, None),
        P("layer", row, "col", None),
        P("layer", row, "col", None),
        P("layer", row, "col"),
        P("col", None),
    )
    return jax.shard_map(
        on_device,
        mesh=fine,
        in_specs=placed,
        out_specs=(P(row, ("layer", "col"), None), P("col", ("layer", "x", "z"), None)),
        check_vma=False,
    )
```

profile of v0, /device:TPU:1, one launch (start us, length us, event | category | flops | bytes accessed | tf_op | source)
XLA Modules:
  0.0 127.6 jit_solution(12505910987765193851)
XLA Ops:
  1.4 8.3 %first_send.1 = (bf16[16,128,128]{2,1,0:T(8,128)(2,1)S(1)}, s32[256]{0:T(256)S(1)}, s32[256]{0:T(256)S(1)}, s32[4]{0:T(128)S(1)}, bf16[256,128,128]{2,1,0:T(8,128)(2,1)S(1)}, /*index=5*/bf16[64,128,128]{2,1,0:T(8,128)(2,1)S(1)}) custom-call(s32[256]{0:T(256)} %bitcast.13, s32[256]{0:T(256)} %bitcast.14, s32[1]{0:T(128)} %bitcast.10.count, ...), custom_call_target="tpu_custom_call" | custom-call | tf_op jit(solution)/shard_map/first_send/pallas_call | solution.py:163
  9.7 2.1 %collective-permute-start = (bf16[16,128,128]{2,1,0:T(8,128)(2,1)S(1)}, bf16[16,128,128]{2,1,0:T(8,128)(2,1)S(1)}, u32[]{:S(2)}, u32[]{:S(2)}) collective-permute-start(bf16[16,128,128]{2,1,0:T(8,128)(2,1)S(1)} %get-tuple-element.35), channel_id=1, source_target_pairs={{0,128},{128,0},{1,129},{129,1},{2,130},{130,2},{3,131},{131,3},{4... | collective-permute-start | bytes 1572872 | tf_op jit(solution)/shard_map/ppermute | solution.py:332
  11.8 2.8 %first_keep.1.keep = f32[17,128,128]{2,1,0:T(8,128)S(1)} custom-call(s32[256]{0:T(256)S(1)} %get-tuple-element.30.order, s32[4]{0:T(128)S(1)} %get-tuple-element.31.numbers, bf16[256,128,128]{2,1,0:T(8,128)(2,1)S(1)} %get-tuple-element.32.tiles, bf16[64,128,128]{2,1,0:T(8,128)(2,1)S(1)} %get-tuple-element.34.panel), custom_call_target="tpu_custom_call" | custom-call | flops 1073741824 | bytes 10485760 | tf_op jit(solution)/shard_map/first_keep/pallas_call | solution.py:219
  15.4 1.5 %collective-permute-start.2 = (bf16[4,128,128]{2,1,0:T(8,128)(2,1)S(1)}, bf16[4,128,128]{2,1,0:T(8,128)(2,1)S(1)}, u32[]{:S(2)}, u32[]{:S(2)}) collective-permute-start(bf16[4,128,128]{2,1,0:T(8,128)(2,1)S(1)} %get-tuple-element.38), channel_id=1, source_target_pairs={{0,2},{1,3},{2,0},{3,1},{4,6},{5,7},{6,4},{7,5},{8,10},{9,11},{10,... | collective-permute-start | bytes 393224 | tf_op jit(solution)/shard_map/ppermute | solution.py:328
  16.9 2.0 %collective-permute-start.3 = (bf16[4,128,128]{2,1,0:T(8,128)(2,1)S(1)}, bf16[4,128,128]{2,1,0:T(8,128)(2,1)S(1)}, u32[]{:S(2)}, u32[]{:S(2)}) collective-permute-start(bf16[4,128,128]{2,1,0:T(8,128)(2,1)S(1)} %get-tuple-element.39), channel_id=1, source_target_pairs={{0,3},{1,0},{2,1},{3,2},{4,7},{5,4},{6,5},{7,6},{8,11},{9,8},{10,9... | collective-permute-start | bytes 393224 | tf_op jit(solution)/shard_map/ppermute | solution.py:328
  18.9 5.9 %collective-permute-done.1.a = bf16[4,128,128]{2,1,0:T(8,128)(2,1)S(1)} collective-permute-done((bf16[4,128,128]{2,1,0:T(8,128)(2,1)S(1)}, bf16[4,128,128]{2,1,0:T(8,128)(2,1)S(1)}, u32[]{:S(2)}, u32[]{:S(2)}) %collective-permute-start.1) | collective-permute-done | bytes 131104 | tf_op jit(solution)/shard_map/ppermute | solution.py:328
  25.3 2.7 %collective-permute-start.6 = (bf16[4,128,128]{2,1,0:T(8,128)(2,1)S(1)}, bf16[4,128,128]{2,1,0:T(8,128)(2,1)S(1)}, u32[]{:S(2)}, u32[]{:S(2)}) collective-permute-start(bf16[4,128,128]{2,1,0:T(8,128)(2,1)S(1)} %first_sum.1.refs_0_), channel_id=1, source_target_pairs={{0,3},{1,0},{2,1},{3,2},{4,7},{5,4},{6,5},{7,6},{8,11},{9,8},{10,9... | collective-permute-start | bytes 393224 | tf_op jit(solution)/shard_map/ppermute | solution.py:328
  29.7 3.6 %collective-permute-done.6.refs_3_ = bf16[4,128,128]{2,1,0:T(8,128)(2,1)S(1)} collective-permute-done((bf16[4,128,128]{2,1,0:T(8,128)(2,1)S(1)}, bf16[4,128,128]{2,1,0:T(8,128)(2,1)S(1)}, u32[]{:S(2)}, u32[]{:S(2)}) %collective-permute-start.6) | collective-permute-done | bytes 131104 | tf_op jit(solution)/shard_map/ppermute | solution.py:328
  34.5 2.2 %collective-permute-start.9 = (bf16[4,128,128]{2,1,0:T(8,128)(2,1)S(1)}, bf16[4,128,128]{2,1,0:T(8,128)(2,1)S(1)}, u32[]{:S(2)}, u32[]{:S(2)}) collective-permute-start(bf16[4,128,128]{2,1,0:T(8,128)(2,1)S(1)} %collective-permute-done.5.refs_2_), channel_id=1, source_target_pairs={{0,128},{128,0},{1,129},{129,1},{2,130},{130,2},{3,131},{131,3},{4... | collective-permute-start | bytes 393224 | tf_op jit(solution)/shard_map/ppermute | solution.py:332
  39.2 3.4 %back_send.1 = (bf16[32,128,128]{2,1,0:T(8,128)(2,1)S(1)}, bf16[32,128,128]{2,1,0:T(8,128)(2,1)S(1)}) custom-call(s32[256]{0:T(256)S(1)} %get-tuple-element.33.order, s32[4]{0:T(128)S(1)} %get-tuple-element.31.numbers, s32[3]{0:T(128)S(1)} %pad_add_fusion.ids, bf16[256,128,128]{2,1,0:T(8,128)(2,1)S(1)} %get-tuple-element.32.tiles, ...), custom_call_target="tpu_custom_call" | custom-call | tf_op jit(solution)/shard_map/back_send/pallas_call | solution.py:192
  42.7 3.2 %back_keep.1.keep = f32[33,128,128]{2,1,0:T(8,128)S(1)} custom-call(s32[256]{0:T(256)S(1)} %get-tuple-element.33.order, s32[4]{0:T(128)S(1)} %get-tuple-element.31.numbers, bf16[256,128,128]{2,1,0:T(8,128)(2,1)S(1)} %get-tuple-element.32.tiles, bf16[32,128,128]{2,1,0:T(8,128)(2,1)S(1)} %get-tuple-element.40.panel), custom_call_target="tpu_custom_call" | custom-call | flops 1073741824 | bytes 10485760 | tf_op jit(solution)/shard_map/back_keep/pallas_call | solution.py:219
  49.4 12.4 %collective-permute-done.12.a = bf16[8,128,128]{2,1,0:T(8,128)(2,1)S(1)} collective-permute-done((bf16[8,128,128]{2,1,0:T(8,128)(2,1)S(1)}, bf16[8,128,128]{2,1,0:T(8,128)(2,1)S(1)}, u32[]{:S(2)}, u32[]{:S(2)}) %collective-permute-start.12) | collective-permute-done | bytes 262176 | tf_op jit(solution)/shard_map/ppermute | solution.py:328
  62.4 15.6 %all_to_all.10.got = bf16[8,128,128]{2,1,0:T(8,128)(2,1)S(1)} all-to-all(bf16[8,128,128]{2,1,0:T(8,128)(2,1)S(1)} %back_sum.1), channel_id=1, replica_groups=mesh['layer'=2,'x'=4,'z'=8,'col'=4] {'z'}, dimensions={0} | all-to-all | bytes 524288 | tf_op jit(solution)/shard_map/all_to_all | solution.py:365
  78.0 12.0 %all_to_all.11.refs_0_ = bf16[8,128,128]{2,1,0:T(8,128)(2,1)S(1)} all-to-all(bf16[8,128,128]{2,1,0:T(8,128)(2,1)S(1)} %get-tuple-element.46), channel_id=1, replica_groups=mesh['layer'=2,'x'=4,'z'=8,'col'=4] {'z'}, dimensions={0} | all-to-all | bytes 524288 | tf_op jit(solution)/shard_map/all_to_all | solution.py:374
  90.0 2.9 %collective-permute-start.17 = (bf16[8,128,128]{2,1,0:T(8,128)(2,1)S(1)}, bf16[8,128,128]{2,1,0:T(8,128)(2,1)S(1)}, u32[]{:S(2)}, u32[]{:S(2)}) collective-permute-start(bf16[8,128,128]{2,1,0:T(8,128)(2,1)S(1)} %all_to_all.11.refs_0_), channel_id=1, source_target_pairs={{0,96},{32,0},{64,32},{96,64},{1,97},{33,1},{65,33},{97,65},{2,98}... | collective-permute-start | bytes 786440 | tf_op jit(solution)/shard_map/ppermute | solution.py:328
  93.5 4.1 %collective-permute-start.18 = (bf16[8,128,128]{2,1,0:T(8,128)(2,1)S(1)}, bf16[8,128,128]{2,1,0:T(8,128)(2,1)S(1)}, u32[]{:S(2)}, u32[]{:S(2)}) collective-permute-start(bf16[8,128,128]{2,1,0:T(8,128)(2,1)S(1)} %all_to_all.11.refs_0_), channel_id=1, source_target_pairs={{0,128},{128,0},{1,129},{129,1},{2,130},{130,2},{3,131},{131,3},{4... | collective-permute-start | bytes 786440 | tf_op jit(solution)/shard_map/ppermute | solution.py:332
  97.6 2.1 %collective-permute-done.17.refs_3_ = bf16[8,128,128]{2,1,0:T(8,128)(2,1)S(1)} collective-permute-done((bf16[8,128,128]{2,1,0:T(8,128)(2,1)S(1)}, bf16[8,128,128]{2,1,0:T(8,128)(2,1)S(1)}, u32[]{:S(2)}, u32[]{:S(2)}) %collective-permute-start.17) | collective-permute-done | bytes 262176 | tf_op jit(solution)/shard_map/ppermute | solution.py:328
  99.7 5.3 %collective-permute-start.21 = (bf16[8,128,128]{2,1,0:T(8,128)(2,1)S(1)}, bf16[8,128,128]{2,1,0:T(8,128)(2,1)S(1)}, u32[]{:S(2)}, u32[]{:S(2)}) collective-permute-start(bf16[8,128,128]{2,1,0:T(8,128)(2,1)S(1)} %collective-permute-done.17.refs_3_), channel_id=1, source_target_pairs={{0,128},{128,0},{1,129},{129,1},{2,130},{130,2},{3,131},{131,3},{4... | collective-permute-start | bytes 786440 | tf_op jit(solution)/shard_map/ppermute | solution.py:332
  106.3 2.1 %collective-permute-start.19 = (bf16[8,128,128]{2,1,0:T(8,128)(2,1)S(1)}, bf16[8,128,128]{2,1,0:T(8,128)(2,1)S(1)}, u32[]{:S(2)}, u32[]{:S(2)}) collective-permute-start(bf16[8,128,128]{2,1,0:T(8,128)(2,1)S(1)} %collective-permute-done.15.refs_1_), channel_id=1, source_target_pairs={{0,128},{128,0},{1,129},{129,1},{2,130},{130,2},{3,131},{131,3},{4... | collective-permute-start | bytes 786440 | tf_op jit(solution)/shard_map/ppermute | solution.py:332
  109.6 3.6 %last_send.1 = (bf16[16,128,128]{2,1,0:T(8,128)(2,1)S(1)}, bf16[64,128,128]{2,1,0:T(8,128)(2,1)S(1)}) custom-call(s32[256]{0:T(256)S(1)} %get-tuple-element.30.order, s32[4]{0:T(128)S(1)} %get-tuple-element.31.numbers, s32[3]{0:T(128)S(1)} %pad_add_fusion.ids, bf16[256,128,128]{2,1,0:T(8,128)(2,1)S(1)} %get-tuple-element.32.tiles, ...), custom_call_target="tpu_custom_call" | custom-call | tf_op jit(solution)/shard_map/last_send/pallas_call | solution.py:192
  113.3 3.3 %last_keep.1 = (f32[17,128,128]{2,1,0:T(8,128)S(1)}, f32[32,128]{1,0:T(8,128)S(1)}) custom-call(s32[256]{0:T(256)S(1)} %get-tuple-element.30.order, s32[4]{0:T(128)S(1)} %get-tuple-element.31.numbers, bf16[256,128,128]{2,1,0:T(8,128)(2,1)S(1)} %get-tuple-element.32.tiles, bf16[64,128,128]{2,1,0:T(8,128)(2,1)S(1)} %get-tuple-element.47.panel), custom_call_target="tpu_custom_call" | custom-call | flops 1073741824 | bytes 10485760 | tf_op jit(solution)/shard_map/last_keep/pallas_call | solution.py:219
  117.5 1.6 %collective-permute-start.24 = (bf16[528,128]{1,0:T(8,128)(2,1)S(1)}, bf16[528,128]{1,0:T(8,128)(2,1)S(1)}, u32[]{:S(2)}, u32[]{:S(2)}) collective-permute-start(bf16[528,128]{1,0:T(8,128)(2,1)S(1)} %get-tuple-element.54), channel_id=1, source_target_pairs={{0,2},{1,3},{2,0},{3,1},{4,6},{5,7},{6,4},{7,5},{8,10},{9,11},{10,... | collective-permute-start | bytes 405512 | tf_op jit(solution)/shard_map/ppermute | solution.py:328
  119.1 2.0 %collective-permute-start.25 = (bf16[528,128]{1,0:T(8,128)(2,1)S(1)}, bf16[528,128]{1,0:T(8,128)(2,1)S(1)}, u32[]{:S(2)}, u32[]{:S(2)}) collective-permute-start(bf16[528,128]{1,0:T(8,128)(2,1)S(1)} %get-tuple-element.55), channel_id=1, source_target_pairs={{0,3},{1,0},{2,1},{3,2},{4,7},{5,4},{6,5},{7,6},{8,11},{9,8},{10,9... | collective-permute-start | bytes 405512 | tf_op jit(solution)/shard_map/ppermute | solution.py:328
  121.1 5.6 %collective-permute-done.23.a = bf16[528,128]{1,0:T(8,128)(2,1)S(1)} collective-permute-done((bf16[528,128]{1,0:T(8,128)(2,1)S(1)}, bf16[528,128]{1,0:T(8,128)(2,1)S(1)}, u32[]{:S(2)}, u32[]{:S(2)}) %collective-permute-start.23) | collective-permute-done | bytes 135200 | tf_op jit(solution)/shard_map/ppermute | solution.py:328
  (44 shorter events, 15.7 us)
Async XLA Ops:
  9.7 5.0 %collective-permute-start = (bf16[16,128,128]{2,1,0:T(8,128)(2,1)S(1)}, bf16[16,128,128]{2,1,0:T(8,128)(2,1)S(1)}, u32[]{:S(2)}, u32[]{:S(2)}) collective-permute-start(bf16[16,128,128]{2,1,0:T(8,128)(2,1)S(1)} %get-tuple-element.35), channel_id=1, source_target_pairs={{0,128},{128,0},{1,129},{129,1},{2,130},{130,2},{3,131},{131,3},{4... | collective-permute-start | bytes 1572872 | tf_op jit(solution)/shard_map/ppermute | solution.py:332
  15.3 9.4 %collective-permute-start.1 = (bf16[4,128,128]{2,1,0:T(8,128)(2,1)S(1)}, bf16[4,128,128]{2,1,0:T(8,128)(2,1)S(1)}, u32[]{:S(2)}, u32[]{:S(2)}) collective-permute-start(bf16[4,128,128]{2,1,0:T(8,128)(2,1)S(1)} %get-tuple-element.37), channel_id=1, source_target_pairs={{0,1},{1,2},{2,3},{3,0},{4,5},{5,6},{6,7},{7,4},{8,9},{9,10},{10,1... | collective-permute-start | bytes 393224 | tf_op jit(solution)/shard_map/ppermute | solution.py:328
  15.4 9.4 %collective-permute-start.2 = (bf16[4,128,128]{2,1,0:T(8,128)(2,1)S(1)}, bf16[4,128,128]{2,1,0:T(8,128)(2,1)S(1)}, u32[]{:S(2)}, u32[]{:S(2)}) collective-permute-start(bf16[4,128,128]{2,1,0:T(8,128)(2,1)S(1)} %get-tuple-element.38), channel_id=1, source_target_pairs={{0,2},{1,3},{2,0},{3,1},{4,6},{5,7},{6,4},{7,5},{8,10},{9,11},{10,... | collective-permute-start | bytes 393224 | tf_op jit(solution)/shard_map/ppermute | solution.py:328
  16.9 8.2 %collective-permute-start.3 = (bf16[4,128,128]{2,1,0:T(8,128)(2,1)S(1)}, bf16[4,128,128]{2,1,0:T(8,128)(2,1)S(1)}, u32[]{:S(2)}, u32[]{:S(2)}) collective-permute-start(bf16[4,128,128]{2,1,0:T(8,128)(2,1)S(1)} %get-tuple-element.39), channel_id=1, source_target_pairs={{0,3},{1,0},{2,1},{3,2},{4,7},{5,4},{6,5},{7,6},{8,11},{9,8},{10,9... | collective-permute-start | bytes 393224 | tf_op jit(solution)/shard_map/ppermute | solution.py:328
  25.3 8.0 %collective-permute-start.6 = (bf16[4,128,128]{2,1,0:T(8,128)(2,1)S(1)}, bf16[4,128,128]{2,1,0:T(8,128)(2,1)S(1)}, u32[]{:S(2)}, u32[]{:S(2)}) collective-permute-start(bf16[4,128,128]{2,1,0:T(8,128)(2,1)S(1)} %first_sum.1.refs_0_), channel_id=1, source_target_pairs={{0,3},{1,0},{2,1},{3,2},{4,7},{5,4},{6,5},{7,6},{8,11},{9,8},{10,9... | collective-permute-start | bytes 393224 | tf_op jit(solution)/shard_map/ppermute | solution.py:328
  28.0 6.5 %collective-permute-start.5 = (bf16[4,128,128]{2,1,0:T(8,128)(2,1)S(1)}, bf16[4,128,128]{2,1,0:T(8,128)(2,1)S(1)}, u32[]{:S(2)}, u32[]{:S(2)}) collective-permute-start(bf16[4,128,128]{2,1,0:T(8,128)(2,1)S(1)} %first_sum.1.refs_0_), channel_id=1, source_target_pairs={{0,2},{1,3},{2,0},{3,1},{4,6},{5,7},{6,4},{7,5},{8,10},{9,11},{10,... | collective-permute-start | bytes 393224 | tf_op jit(solution)/shard_map/ppermute | solution.py:328
  28.3 9.4 %collective-permute-start.4 = (bf16[4,128,128]{2,1,0:T(8,128)(2,1)S(1)}, bf16[4,128,128]{2,1,0:T(8,128)(2,1)S(1)}, u32[]{:S(2)}, u32[]{:S(2)}) collective-permute-start(bf16[4,128,128]{2,1,0:T(8,128)(2,1)S(1)} %first_sum.1.refs_0_), channel_id=1, source_target_pairs={{0,1},{1,2},{2,3},{3,0},{4,5},{5,6},{6,7},{7,4},{8,9},{9,10},{10,1... | collective-permute-start | bytes 393224 | tf_op jit(solution)/shard_map/ppermute | solution.py:328
  28.7 9.5 %collective-permute-start.7 = (bf16[4,128,128]{2,1,0:T(8,128)(2,1)S(1)}, bf16[4,128,128]{2,1,0:T(8,128)(2,1)S(1)}, u32[]{:S(2)}, u32[]{:S(2)}) collective-permute-start(bf16[4,128,128]{2,1,0:T(8,128)(2,1)S(1)} %first_sum.1.refs_0_), channel_id=1, source_target_pairs={{0,128},{128,0},{1,129},{129,1},{2,130},{130,2},{3,131},{131,3},{4... | collective-permute-start | bytes 393224 | tf_op jit(solution)/shard_map/ppermute | solution.py:332
  33.4 4.9 %collective-permute-start.10 = (bf16[4,128,128]{2,1,0:T(8,128)(2,1)S(1)}, bf16[4,128,128]{2,1,0:T(8,128)(2,1)S(1)}, u32[]{:S(2)}, u32[]{:S(2)}) collective-permute-start(bf16[4,128,128]{2,1,0:T(8,128)(2,1)S(1)} %collective-permute-done.6.refs_3_), channel_id=1, source_target_pairs={{0,128},{128,0},{1,129},{129,1},{2,130},{130,2},{3,131},{131,3},{4... | collective-permute-start | bytes 393224 | tf_op jit(solution)/shard_map/ppermute | solution.py:332
  34.5 3.7 %collective-permute-start.9 = (bf16[4,128,128]{2,1,0:T(8,128)(2,1)S(1)}, bf16[4,128,128]{2,1,0:T(8,128)(2,1)S(1)}, u32[]{:S(2)}, u32[]{:S(2)}) collective-permute-start(bf16[4,128,128]{2,1,0:T(8,128)(2,1)S(1)} %collective-permute-done.5.refs_2_), channel_id=1, source_target_pairs={{0,128},{128,0},{1,129},{129,1},{2,130},{130,2},{3,131},{131,3},{4... | collective-permute-start | bytes 393224 | tf_op jit(solution)/shard_map/ppermute | solution.py:332
  42.6 3.3 %collective-permute-start.11 = (bf16[32,128,128]{2,1,0:T(8,128)(2,1)S(1)}, bf16[32,128,128]{2,1,0:T(8,128)(2,1)S(1)}, u32[]{:S(2)}, u32[]{:S(2)}) collective-permute-start(bf16[32,128,128]{2,1,0:T(8,128)(2,1)S(1)} %get-tuple-element.41), channel_id=1, source_target_pairs={{0,128},{128,0},{1,129},{129,1},{2,130},{130,2},{3,131},{131,3},{4... | collective-permute-start | bytes 3145736 | tf_op jit(solution)/shard_map/ppermute | solution.py:332
  46.7 15.2 %collective-permute-start.12 = (bf16[8,128,128]{2,1,0:T(8,128)(2,1)S(1)}, bf16[8,128,128]{2,1,0:T(8,128)(2,1)S(1)}, u32[]{:S(2)}, u32[]{:S(2)}) collective-permute-start(bf16[8,128,128]{2,1,0:T(8,128)(2,1)S(1)} %get-tuple-element.43), channel_id=1, source_target_pairs={{0,32},{32,64},{64,96},{96,0},{1,33},{33,65},{65,97},{97,1},{2,34}... | collective-permute-start | bytes 786440 | tf_op jit(solution)/shard_map/ppermute | solution.py:328
  46.8 15.1 %collective-permute-start.13 = (bf16[8,128,128]{2,1,0:T(8,128)(2,1)S(1)}, bf16[8,128,128]{2,1,0:T(8,128)(2,1)S(1)}, u32[]{:S(2)}, u32[]{:S(2)}) collective-permute-start(bf16[8,128,128]{2,1,0:T(8,128)(2,1)S(1)} %get-tuple-element.44), channel_id=1, source_target_pairs={{0,64},{32,96},{64,0},{96,32},{1,65},{33,97},{65,1},{97,33},{2,66}... | collective-permute-start | bytes 786440 | tf_op jit(solution)/shard_map/ppermute | solution.py:328
  48.2 14.0 %collective-permute-start.14 = (bf16[8,128,128]{2,1,0:T(8,128)(2,1)S(1)}, bf16[8,128,128]{2,1,0:T(8,128)(2,1)S(1)}, u32[]{:S(2)}, u32[]{:S(2)}) collective-permute-start(bf16[8,128,128]{2,1,0:T(8,128)(2,1)S(1)} %get-tuple-element.45), channel_id=1, source_target_pairs={{0,96},{32,0},{64,32},{96,64},{1,97},{33,1},{65,33},{97,65},{2,98}... | collective-permute-start | bytes 786440 | tf_op jit(solution)/shard_map/ppermute | solution.py:328
  90.0 9.7 %collective-permute-start.17 = (bf16[8,128,128]{2,1,0:T(8,128)(2,1)S(1)}, bf16[8,128,128]{2,1,0:T(8,128)(2,1)S(1)}, u32[]{:S(2)}, u32[]{:S(2)}) collective-permute-start(bf16[8,128,128]{2,1,0:T(8,128)(2,1)S(1)} %all_to_all.11.refs_0_), channel_id=1, source_target_pairs={{0,96},{32,0},{64,32},{96,64},{1,97},{33,1},{65,33},{97,65},{2,98}... | collective-permute-start | bytes 786440 | tf_op jit(solution)/shard_map/ppermute | solution.py:328
  92.9 12.1 %collective-permute-start.16 = (bf16[8,128,128]{2,1,0:T(8,128)(2,1)S(1)}, bf16[8,128,128]{2,1,0:T(8,128)(2,1)S(1)}, u32[]{:S(2)}, u32[]{:S(2)}) collective-permute-start(bf16[8,128,128]{2,1,0:T(8,128)(2,1)S(1)} %all_to_all.11.refs_0_), channel_id=1, source_target_pairs={{0,64},{32,96},{64,0},{96,32},{1,65},{33,97},{65,1},{97,33},{2,66}... | collective-permute-start | bytes 786440 | tf_op jit(solution)/shard_map/ppermute | solution.py:328
  92.9 13.4 %collective-permute-start.15 = (bf16[8,128,128]{2,1,0:T(8,128)(2,1)S(1)}, bf16[8,128,128]{2,1,0:T(8,128)(2,1)S(1)}, u32[]{:S(2)}, u32[]{:S(2)}) collective-permute-start(bf16[8,128,128]{2,1,0:T(8,128)(2,1)S(1)} %all_to_all.11.refs_0_), channel_id=1, source_target_pairs={{0,32},{32,64},{64,96},{96,0},{1,33},{33,65},{65,97},{97,1},{2,34}... | collective-permute-start | bytes 786440 | tf_op jit(solution)/shard_map/ppermute | solution.py:328
  93.5 15.0 %collective-permute-start.18 = (bf16[8,128,128]{2,1,0:T(8,128)(2,1)S(1)}, bf16[8,128,128]{2,1,0:T(8,128)(2,1)S(1)}, u32[]{:S(2)}, u32[]{:S(2)}) collective-permute-start(bf16[8,128,128]{2,1,0:T(8,128)(2,1)S(1)} %all_to_all.11.refs_0_), channel_id=1, source_target_pairs={{0,128},{128,0},{1,129},{129,1},{2,130},{130,2},{3,131},{131,3},{4... | collective-permute-start | bytes 786440 | tf_op jit(solution)/shard_map/ppermute | solution.py:332
  99.7 8.7 %collective-permute-start.21 = (bf16[8,128,128]{2,1,0:T(8,128)(2,1)S(1)}, bf16[8,128,128]{2,1,0:T(8,128)(2,1)S(1)}, u32[]{:S(2)}, u32[]{:S(2)}) collective-permute-start(bf16[8,128,128]{2,1,0:T(8,128)(2,1)S(1)} %collective-permute-done.17.refs_3_), channel_id=1, source_target_pairs={{0,128},{128,0},{1,129},{129,1},{2,130},{130,2},{3,131},{131,3},{4... | collective-permute-start | bytes 786440 | tf_op jit(solution)/shard_map/ppermute | solution.py:332
  105.0 3.4 %collective-permute-start.20 = (bf16[8,128,128]{2,1,0:T(8,128)(2,1)S(1)}, bf16[8,128,128]{2,1,0:T(8,128)(2,1)S(1)}, u32[]{:S(2)}, u32[]{:S(2)}) collective-permute-start(bf16[8,128,128]{2,1,0:T(8,128)(2,1)S(1)} %collective-permute-done.16.refs_2_), channel_id=1, source_target_pairs={{0,128},{128,0},{1,129},{129,1},{2,130},{130,2},{3,131},{131,3},{4... | collective-permute-start | bytes 786440 | tf_op jit(solution)/shard_map/ppermute | solution.py:332
  113.2 3.5 %collective-permute-start.22 = (bf16[16,128,128]{2,1,0:T(8,128)(2,1)S(1)}, bf16[16,128,128]{2,1,0:T(8,128)(2,1)S(1)}, u32[]{:S(2)}, u32[]{:S(2)}) collective-permute-start(bf16[16,128,128]{2,1,0:T(8,128)(2,1)S(1)} %get-tuple-element.49), channel_id=1, source_target_pairs={{0,128},{128,0},{1,129},{129,1},{2,130},{130,2},{3,131},{131,3},{4... | collective-permute-start | bytes 1572872 | tf_op jit(solution)/shard_map/ppermute | solution.py:332
  117.4 9.3 %collective-permute-start.23 = (bf16[528,128]{1,0:T(8,128)(2,1)S(1)}, bf16[528,128]{1,0:T(8,128)(2,1)S(1)}, u32[]{:S(2)}, u32[]{:S(2)}) collective-permute-start(bf16[528,128]{1,0:T(8,128)(2,1)S(1)} %get-tuple-element.53), channel_id=1, source_target_pairs={{0,1},{1,2},{2,3},{3,0},{4,5},{5,6},{6,7},{7,4},{8,9},{9,10},{10,1... | collective-permute-start | bytes 405512 | tf_op jit(solution)/shard_map/ppermute | solution.py:328
  117.5 9.2 %collective-permute-start.24 = (bf16[528,128]{1,0:T(8,128)(2,1)S(1)}, bf16[528,128]{1,0:T(8,128)(2,1)S(1)}, u32[]{:S(2)}, u32[]{:S(2)}) collective-permute-start(bf16[528,128]{1,0:T(8,128)(2,1)S(1)} %get-tuple-element.54), channel_id=1, source_target_pairs={{0,2},{1,3},{2,0},{3,1},{4,6},{5,7},{6,4},{7,5},{8,10},{9,11},{10,... | collective-permute-start | bytes 405512 | tf_op jit(solution)/shard_map/ppermute | solution.py:328
  119.1 7.7 %collective-permute-start.25 = (bf16[528,128]{1,0:T(8,128)(2,1)S(1)}, bf16[528,128]{1,0:T(8,128)(2,1)S(1)}, u32[]{:S(2)}, u32[]{:S(2)}) collective-permute-start(bf16[528,128]{1,0:T(8,128)(2,1)S(1)} %get-tuple-element.55), channel_id=1, source_target_pairs={{0,3},{1,0},{2,1},{3,2},{4,7},{5,4},{6,5},{7,6},{8,11},{9,8},{10,9... | collective-permute-start | bytes 405512 | tf_op jit(solution)/shard_map/ppermute | solution.py:328
  (2 other events, 4.8 us)
where the time goes:
time: 127 us; the launch traced here: 128 us
  starting transfers between devices  36.7 us (29%)
  waiting for transfers between devices  33.9 us (27%)
  Pallas kernels  27.9 us (22%)
  blocking collectives  27.5 us (22%)
  between operations  1.45 us (1%)
    ppermute x15, waiting for transfers between devices, shifted(): return lax.ppermute(value, axis, [(i, (i + k) % n) for i in range(n)])  31.8 us
    ppermute x11, starting transfers between devices, swap(): return lax.ppermute(value, 'layer', [(0, 1), (1, 0)])  19.8 us
    ppermute x15, starting transfers between devices, shifted(): return lax.ppermute(value, axis, [(i, (i + k) % n) for i in range(n)])  16.9 us
    all_to_all x1, blocking collectives, on_device(): got = lax.all_to_all(part, 'z', split_axis=0, concat_axis=0, tiled=True)  15.6 us
    all_to_all x1, blocking collectives, on_device(): part = lax.all_to_all(copies, 'z', split_axis=0, concat_axis=0, tiled=True)  12 us
    pallas_call x3, Pallas kernels, keep_part(): pl.pallas_call(functools.partial(keep_kernel, by_row=by_row), in_specs=[S...  9.35 us
    pallas_call x1, Pallas kernels, first_send(): pl.pallas_call(first_send_kernel, in_specs=[HBM, HBM, SMEM, SMEM, HBM, HB...  8.32 us
    pallas_call x2, Pallas kernels, send_part(): pl.pallas_call(functools.partial(send_kernel, by_row=by_row, axis=axis, n...  7.01 us
  transfers between devices with their start and end apart: 26, of which 12 were waited for; matrix products, arithmetic and copies ran while one was open for 0% of the time, Pallas kernels for 7%

commit v1 on v0

--- a/solution.py
+++ b/solution.py
@@ -21,6 +21,9 @@
 BLOCK = 64
 UNROLL = 16
 STEPS = 4
+SORT_STEP = 16
+SHIFTS = (0, 2, 1, 3)
+GATHER_SHIFTS = (0, 1, 3, 2)
 EPS = 1e-06
 
 F32 = jnp.float32
@@ -87,19 +90,22 @@
 
 
 def sort_slots(first, size, rows, cols, live, core, by_row, by_col, counts):
-    def one(i, carry):
+    def several(g, carry):
         row_sends, row_keeps, col_sends, col_keeps = carry
-        t = first + i
-        row, col = rows[t], cols[t]
-        code = t + (row << SLOT_BITS) + (col << (SLOT_BITS + ROW_BITS))
-        used = t < live
-        row_own = jnp.where(jnp.logical_and(used, row >> (ROW_BITS - 1) == core), 1, 0)
-        col_own = jnp.where(jnp.logical_and(used, col >> (COL_BITS - 1) == core), 1, 0)
-        by_row[jnp.where(row_own == 1, N_SLOTS - 1 - row_keeps, row_sends)] = code
-        by_col[jnp.where(col_own == 1, N_SLOTS - 1 - col_keeps, col_sends)] = code
-        return row_sends + 1 - row_own, row_keeps + row_own, col_sends + 1 - col_own, col_keeps + col_own
-
-    return lax.fori_loop(0, size, one, counts, unroll=4)
+        slots = [first + g * SORT_STEP + j for j in range(SORT_STEP)]
+        loaded = [(t, rows[t], cols[t]) for t in slots]
+        for t, row, col in loaded:
+            code = t + (row << SLOT_BITS) + (col << (SLOT_BITS + ROW_BITS))
+            used = t < live
+            row_own = jnp.where(jnp.logical_and(used, row >> (ROW_BITS - 1) == core), 1, 0)
+            col_own = jnp.where(jnp.logical_and(used, col >> (COL_BITS - 1) == core), 1, 0)
+            by_row[jnp.where(row_own == 1, N_SLOTS - 1 - row_keeps, row_sends)] = code
+            by_col[jnp.where(col_own == 1, N_SLOTS - 1 - col_keeps, col_sends)] = code
+            row_sends, row_keeps = row_sends + 1 - row_own, row_keeps + row_own
+            col_sends, col_keeps = col_sends + 1 - col_own, col_keeps + col_own
+        return row_sends, row_keeps, col_sends, col_keeps
+
+    return lax.fori_loop(0, size // SORT_STEP, several, counts)
 
 
 def place(ids, parts, panel, axis, n, per):
@@ -107,7 +113,7 @@
     for side in range(2):
         base = jnp.where(side == 0, core, 1 - core) * (n * per)
         for k in range(n):
-            at = base + lax.rem(me + n - k, n) * per
+            at = base + lax.rem(me + n - GATHER_SHIFTS[k], n) * per
             part = parts[side * n + k]
 
             def one(i):
@@ -230,7 +236,7 @@
 def pair_kernel(ids, keep, got, own, *sends, axis, n, per):
     me = ids[axis]
     for k in range(n):
-        base = lax.rem(me + k, n) * per
+        base = lax.rem(me + SHIFTS[k], n) * per
 
         def one(i):
             total = keep[base + i] + got[base + i].astype(F32)
@@ -300,7 +306,7 @@
     row = lax.broadcasted_iota(jnp.int32, (16, RANK), 0)
     coded = jnp.where(row == 0, high, jnp.where(row == 1, middle, jnp.where(row == 2, low, 0.0)))
     for k in range(NCOL):
-        base = lax.rem(me + k, NCOL) * per
+        base = lax.rem(me + SHIFTS[k], NCOL) * per
         if k:
             sends[k - 1][pl.ds(per * TILE, 16), :] = coded.astype(BF16)
         for i in range(per):
@@ -333,11 +339,11 @@
 
 
 def exchange(values, axis, n):
-    return [shifted(v, axis, k + 1, n) for k, v in enumerate(values)]
+    return [shifted(v, axis, k, n) for v, k in zip(values, SHIFTS[1:], strict=True)]
 
 
 def gather(value, axis, n):
-    mine = [value] + [shifted(value, axis, k, n) for k in range(1, n)]
+    mine = [value] + [shifted(value, axis, k, n) for k in GATHER_SHIFTS[1:]]
     return mine + [swap(v) for v in mine]
 
 

time: 127 us -> 125 us (0.984)
  waiting for transfers between devices: 33.9 us -> 24.4 us
  starting transfers between devices: 36.7 us -> 45.8 us
  Pallas kernels: 27.9 us -> 23 us
  blocking collectives: 27.5 us -> 30.5 us
    ppermute x15, waiting for transfers between devices: 31.8 us -> 22.2 us  [shifted(): return lax.ppermute(value, axis, [(i, (i + k) % n) for i in range(n)])]
    ppermute x11, starting transfers between devices: 19.8 us -> 25.4 us  [swap(): return lax.ppermute(value, 'layer', [(0, 1), (1, 0)])]
    ppermute x15, starting transfers between devices: 16.9 us -> 20.4 us  [shifted(): return lax.ppermute(value, axis, [(i, (i + k) % n) for i in range(n)])]
    all_to_all x1, blocking collectives: 15.6 us -> 18.8 us  [on_device(): got = lax.all_to_all(part, 'z', split_axis=0, concat_axis=0, tiled=True)]
    pallas_call x3, Pallas kernels: 9.35 us -> 6.56 us  [keep_part(): pl.pallas_call(functools.partial(keep_kernel, by_row=by_row), in_specs=[S...]
    pallas_call x2, Pallas kernels: 7.01 us -> 5.5 us  [send_part(): pl.pallas_call(functools.partial(send_kernel, by_row=by_row, axis=axis, n...]
  transfers between devices with their start and end apart: 26 -> 26, of which waited for: 12 -> 11; matrix products, arithmetic and copies ran while one was open for 0% -> 0% of each run, Pallas kernels for 7% -> 5%
where the time goes in v1:
time: 125 us
  starting transfers between devices  45.8 us (37%)
  blocking collectives  30.5 us (24%)
  waiting for transfers between devices  24.4 us (20%)
  Pallas kernels  23 us (18%)
  between operations  1.42 us (1%)
    ppermute x11, starting transfers between devices, swap(): return lax.ppermute(value, 'layer', [(0, 1), (1, 0)])  25.4 us
    ppermute x15, waiting for transfers between devices, shifted(): return lax.ppermute(value, axis, [(i, (i + k) % n) for i in range(n)])  22.2 us
    ppermute x15, starting transfers between devices, shifted(): return lax.ppermute(value, axis, [(i, (i + k) % n) for i in range(n)])  20.4 us
    all_to_all x1, blocking collectives, on_device(): got = lax.all_to_all(part, 'z', split_axis=0, concat_axis=0, tiled=True)  18.8 us
    all_to_all x1, blocking collectives, on_device(): part = lax.all_to_all(copies, 'z', split_axis=0, concat_axis=0, tiled=True)  11.7 us
    pallas_call x1, Pallas kernels, first_send(): pl.pallas_call(first_send_kernel, in_specs=[HBM, HBM, SMEM, SMEM, HBM, HB...  7.74 us
    pallas_call x3, Pallas kernels, keep_part(): pl.pallas_call(functools.partial(keep_kernel, by_row=by_row), in_specs=[S...  6.56 us
    pallas_call x2, Pallas kernels, send_part(): pl.pallas_call(functools.partial(send_kernel, by_row=by_row, axis=axis, n...  5.5 us
  transfers between devices with their start and end apart: 26, of which 11 were waited for; matrix products, arithmetic and copies ran while one was open for 0% of the time, Pallas kernels for 5%

profile of v1, /device:TPU:1, one launch (start us, length us, event | category | flops | bytes accessed | tf_op | source)
XLA Modules:
  0.0 125.1 jit_solution(2653049566743170791)
XLA Ops:
  1.4 7.7 %first_send.1 = (bf16[16,128,128]{2,1,0:T(8,128)(2,1)S(1)}, s32[256]{0:T(256)S(1)}, s32[256]{0:T(256)S(1)}, s32[4]{0:T(128)S(1)}, bf16[256,128,128]{2,1,0:T(8,128)(2,1)S(1)}, /*index=5*/bf16[64,128,128]{2,1,0:T(8,128)(2,1)S(1)}) custom-call(s32[256]{0:T(256)} %bitcast.13, s32[256]{0:T(256)} %bitcast.14, s32[1]{0:T(128)} %bitcast.10.count, ...), custom_call_target="tpu_custom_call" | custom-call | tf_op jit(solution)/shard_map/first_send/pallas_call | solution.py:169
  9.1 2.7 %collective-permute-start = (bf16[16,128,128]{2,1,0:T(8,128)(2,1)S(1)}, bf16[16,128,128]{2,1,0:T(8,128)(2,1)S(1)}, u32[]{:S(2)}, u32[]{:S(2)}) collective-permute-start(bf16[16,128,128]{2,1,0:T(8,128)(2,1)S(1)} %get-tuple-element.35), channel_id=1, source_target_pairs={{0,128},{128,0},{1,129},{129,1},{2,130},{130,2},{3,131},{131,3},{4... | collective-permute-start | bytes 1572872 | tf_op jit(solution)/shard_map/ppermute | solution.py:338
  18.0 1.9 %collective-permute-done.1.a = bf16[4,128,128]{2,1,0:T(8,128)(2,1)S(1)} collective-permute-done((bf16[4,128,128]{2,1,0:T(8,128)(2,1)S(1)}, bf16[4,128,128]{2,1,0:T(8,128)(2,1)S(1)}, u32[]{:S(2)}, u32[]{:S(2)}) %collective-permute-start.1) | collective-permute-done | bytes 131104 | tf_op jit(solution)/shard_map/ppermute | solution.py:334
  19.9 2.3 %collective-permute-done.2.b = bf16[4,128,128]{2,1,0:T(8,128)(2,1)S(1)} collective-permute-done((bf16[4,128,128]{2,1,0:T(8,128)(2,1)S(1)}, bf16[4,128,128]{2,1,0:T(8,128)(2,1)S(1)}, u32[]{:S(2)}, u32[]{:S(2)}) %collective-permute-start.2) | collective-permute-done | bytes 131104 | tf_op jit(solution)/shard_map/ppermute | solution.py:334
  23.1 2.0 %collective-permute-start.5 = (bf16[4,128,128]{2,1,0:T(8,128)(2,1)S(1)}, bf16[4,128,128]{2,1,0:T(8,128)(2,1)S(1)}, u32[]{:S(2)}, u32[]{:S(2)}) collective-permute-start(bf16[4,128,128]{2,1,0:T(8,128)(2,1)S(1)} %first_sum.1.refs_0_), channel_id=1, source_target_pairs={{0,3},{1,0},{2,1},{3,2},{4,7},{5,4},{6,5},{7,6},{8,11},{9,8},{10,9... | collective-permute-start | bytes 393224 | tf_op jit(solution)/shard_map/ppermute | solution.py:334
  25.3 3.4 %collective-permute-start.7 = (bf16[4,128,128]{2,1,0:T(8,128)(2,1)S(1)}, bf16[4,128,128]{2,1,0:T(8,128)(2,1)S(1)}, u32[]{:S(2)}, u32[]{:S(2)}) collective-permute-start(bf16[4,128,128]{2,1,0:T(8,128)(2,1)S(1)} %first_sum.1.refs_0_), channel_id=1, source_target_pairs={{0,128},{128,0},{1,129},{129,1},{2,130},{130,2},{3,131},{131,3},{4... | collective-permute-start | bytes 393224 | tf_op jit(solution)/shard_map/ppermute | solution.py:338
  28.6 3.4 %collective-permute-start.10 = (bf16[4,128,128]{2,1,0:T(8,128)(2,1)S(1)}, bf16[4,128,128]{2,1,0:T(8,128)(2,1)S(1)}, u32[]{:S(2)}, u32[]{:S(2)}) collective-permute-start(bf16[4,128,128]{2,1,0:T(8,128)(2,1)S(1)} %collective-permute-done.6.refs_3_), channel_id=1, source_target_pairs={{0,128},{128,0},{1,129},{129,1},{2,130},{130,2},{3,131},{131,3},{4... | collective-permute-start | bytes 393224 | tf_op jit(solution)/shard_map/ppermute | solution.py:338
  35.0 2.5 %back_send.1 = (bf16[32,128,128]{2,1,0:T(8,128)(2,1)S(1)}, bf16[32,128,128]{2,1,0:T(8,128)(2,1)S(1)}) custom-call(s32[256]{0:T(256)S(1)} %get-tuple-element.33.order, s32[4]{0:T(128)S(1)} %get-tuple-element.31.numbers, s32[3]{0:T(128)S(1)} %pad_add_fusion.ids, bf16[256,128,128]{2,1,0:T(8,128)(2,1)S(1)} %get-tuple-element.32.tiles, ...), custom_call_target="tpu_custom_call" | custom-call | tf_op jit(solution)/shard_map/back_send/pallas_call | solution.py:198
  38.6 2.3 %back_keep.1.keep = f32[33,128,128]{2,1,0:T(8,128)S(1)} custom-call(s32[256]{0:T(256)S(1)} %get-tuple-element.33.order, s32[4]{0:T(128)S(1)} %get-tuple-element.31.numbers, bf16[256,128,128]{2,1,0:T(8,128)(2,1)S(1)} %get-tuple-element.32.tiles, bf16[32,128,128]{2,1,0:T(8,128)(2,1)S(1)} %get-tuple-element.40.panel), custom_call_target="tpu_custom_call" | custom-call | flops 1073741824 | bytes 10485760 | tf_op jit(solution)/shard_map/back_keep/pallas_call | solution.py:225
  41.6 2.6 %collective-permute-start.12 = (bf16[8,128,128]{2,1,0:T(8,128)(2,1)S(1)}, bf16[8,128,128]{2,1,0:T(8,128)(2,1)S(1)}, u32[]{:S(2)}, u32[]{:S(2)}) collective-permute-start(bf16[8,128,128]{2,1,0:T(8,128)(2,1)S(1)} %get-tuple-element.43), channel_id=1, source_target_pairs={{0,64},{32,96},{64,0},{96,32},{1,65},{33,97},{65,1},{97,33},{2,66}... | collective-permute-start | bytes 786440 | tf_op jit(solution)/shard_map/ppermute | solution.py:334
  44.3 2.0 %collective-permute-start.13 = (bf16[8,128,128]{2,1,0:T(8,128)(2,1)S(1)}, bf16[8,128,128]{2,1,0:T(8,128)(2,1)S(1)}, u32[]{:S(2)}, u32[]{:S(2)}) collective-permute-start(bf16[8,128,128]{2,1,0:T(8,128)(2,1)S(1)} %get-tuple-element.44), channel_id=1, source_target_pairs={{0,32},{32,64},{64,96},{96,0},{1,33},{33,65},{65,97},{97,1},{2,34}... | collective-permute-start | bytes 786440 | tf_op jit(solution)/shard_map/ppermute | solution.py:334
  47.0 3.5 %collective-permute-done.12.a = bf16[8,128,128]{2,1,0:T(8,128)(2,1)S(1)} collective-permute-done((bf16[8,128,128]{2,1,0:T(8,128)(2,1)S(1)}, bf16[8,128,128]{2,1,0:T(8,128)(2,1)S(1)}, u32[]{:S(2)}, u32[]{:S(2)}) %collective-permute-start.12) | collective-permute-done | bytes 262176 | tf_op jit(solution)/shard_map/ppermute | solution.py:334
  50.5 6.6 %collective-permute-done.13.b = bf16[8,128,128]{2,1,0:T(8,128)(2,1)S(1)} collective-permute-done((bf16[8,128,128]{2,1,0:T(8,128)(2,1)S(1)}, bf16[8,128,128]{2,1,0:T(8,128)(2,1)S(1)}, u32[]{:S(2)}, u32[]{:S(2)}) %collective-permute-start.13) | collective-permute-done | bytes 262176 | tf_op jit(solution)/shard_map/ppermute | solution.py:334
  58.3 18.8 %all_to_all.10.got = bf16[8,128,128]{2,1,0:T(8,128)(2,1)S(1)} all-to-all(bf16[8,128,128]{2,1,0:T(8,128)(2,1)S(1)} %back_sum.1), channel_id=1, replica_groups=mesh['layer'=2,'x'=4,'z'=8,'col'=4] {'z'}, dimensions={0} | all-to-all | bytes 524288 | tf_op jit(solution)/shard_map/all_to_all | solution.py:371
  77.2 11.7 %all_to_all.11.refs_0_ = bf16[8,128,128]{2,1,0:T(8,128)(2,1)S(1)} all-to-all(bf16[8,128,128]{2,1,0:T(8,128)(2,1)S(1)} %get-tuple-element.46), channel_id=1, replica_groups=mesh['layer'=2,'x'=4,'z'=8,'col'=4] {'z'}, dimensions={0} | all-to-all | bytes 524288 | tf_op jit(solution)/shard_map/all_to_all | solution.py:380
  90.4 2.2 %collective-permute-start.16 = (bf16[8,128,128]{2,1,0:T(8,128)(2,1)S(1)}, bf16[8,128,128]{2,1,0:T(8,128)(2,1)S(1)}, u32[]{:S(2)}, u32[]{:S(2)}) collective-permute-start(bf16[8,128,128]{2,1,0:T(8,128)(2,1)S(1)} %all_to_all.11.refs_0_), channel_id=1, source_target_pairs={{0,96},{32,0},{64,32},{96,64},{1,97},{33,1},{65,33},{97,65},{2,98}... | collective-permute-start | bytes 786440 | tf_op jit(solution)/shard_map/ppermute | solution.py:334
  92.5 4.1 %collective-permute-start.18 = (bf16[8,128,128]{2,1,0:T(8,128)(2,1)S(1)}, bf16[8,128,128]{2,1,0:T(8,128)(2,1)S(1)}, u32[]{:S(2)}, u32[]{:S(2)}) collective-permute-start(bf16[8,128,128]{2,1,0:T(8,128)(2,1)S(1)} %all_to_all.11.refs_0_), channel_id=1, source_target_pairs={{0,128},{128,0},{1,129},{129,1},{2,130},{130,2},{3,131},{131,3},{4... | collective-permute-start | bytes 786440 | tf_op jit(solution)/shard_map/ppermute | solution.py:338
  96.7 5.4 %collective-permute-start.21 = (bf16[8,128,128]{2,1,0:T(8,128)(2,1)S(1)}, bf16[8,128,128]{2,1,0:T(8,128)(2,1)S(1)}, u32[]{:S(2)}, u32[]{:S(2)}) collective-permute-start(bf16[8,128,128]{2,1,0:T(8,128)(2,1)S(1)} %collective-permute-done.17.refs_3_), channel_id=1, source_target_pairs={{0,128},{128,0},{1,129},{129,1},{2,130},{130,2},{3,131},{131,3},{4... | collective-permute-start | bytes 786440 | tf_op jit(solution)/shard_map/ppermute | solution.py:338
  102.1 2.5 %collective-permute-start.20 = (bf16[8,128,128]{2,1,0:T(8,128)(2,1)S(1)}, bf16[8,128,128]{2,1,0:T(8,128)(2,1)S(1)}, u32[]{:S(2)}, u32[]{:S(2)}) collective-permute-start(bf16[8,128,128]{2,1,0:T(8,128)(2,1)S(1)} %collective-permute-done.16.refs_2_), channel_id=1, source_target_pairs={{0,128},{128,0},{1,129},{129,1},{2,130},{130,2},{3,131},{131,3},{4... | collective-permute-start | bytes 786440 | tf_op jit(solution)/shard_map/ppermute | solution.py:338
  106.4 3.0 %last_send.1 = (bf16[16,128,128]{2,1,0:T(8,128)(2,1)S(1)}, bf16[64,128,128]{2,1,0:T(8,128)(2,1)S(1)}) custom-call(s32[256]{0:T(256)S(1)} %get-tuple-element.30.order, s32[4]{0:T(128)S(1)} %get-tuple-element.31.numbers, s32[3]{0:T(128)S(1)} %pad_add_fusion.ids, bf16[256,128,128]{2,1,0:T(8,128)(2,1)S(1)} %get-tuple-element.32.tiles, ...), custom_call_target="tpu_custom_call" | custom-call | tf_op jit(solution)/shard_map/last_send/pallas_call | solution.py:198
  109.6 2.4 %last_keep.1 = (f32[17,128,128]{2,1,0:T(8,128)S(1)}, f32[32,128]{1,0:T(8,128)S(1)}) custom-call(s32[256]{0:T(256)S(1)} %get-tuple-element.30.order, s32[4]{0:T(128)S(1)} %get-tuple-element.31.numbers, bf16[256,128,128]{2,1,0:T(8,128)(2,1)S(1)} %get-tuple-element.32.tiles, bf16[64,128,128]{2,1,0:T(8,128)(2,1)S(1)} %get-tuple-element.47.panel), custom_call_target="tpu_custom_call" | custom-call | flops 1073741824 | bytes 10485760 | tf_op jit(solution)/shard_map/last_keep/pallas_call | solution.py:225
  114.2 4.0 %collective-permute-start.24 = (bf16[528,128]{1,0:T(8,128)(2,1)S(1)}, bf16[528,128]{1,0:T(8,128)(2,1)S(1)}, u32[]{:S(2)}, u32[]{:S(2)}) collective-permute-start(bf16[528,128]{1,0:T(8,128)(2,1)S(1)} %get-tuple-element.54), channel_id=1, source_target_pairs={{0,1},{1,2},{2,3},{3,0},{4,5},{5,6},{6,7},{7,4},{8,9},{9,10},{10,1... | collective-permute-start | bytes 405512 | tf_op jit(solution)/shard_map/ppermute | solution.py:334
  118.3 3.8 %collective-permute-done.24.b = bf16[528,128]{1,0:T(8,128)(2,1)S(1)} collective-permute-done((bf16[528,128]{1,0:T(8,128)(2,1)S(1)}, bf16[528,128]{1,0:T(8,128)(2,1)S(1)}, u32[]{:S(2)}, u32[]{:S(2)}) %collective-permute-start.24) | collective-permute-done | bytes 135200 | tf_op jit(solution)/shard_map/ppermute | solution.py:334
  122.1 2.3 %collective-permute-done.25.c = bf16[528,128]{1,0:T(8,128)(2,1)S(1)} collective-permute-done((bf16[528,128]{1,0:T(8,128)(2,1)S(1)}, bf16[528,128]{1,0:T(8,128)(2,1)S(1)}, u32[]{:S(2)}, u32[]{:S(2)}) %collective-permute-start.25) | collective-permute-done | bytes 135200 | tf_op jit(solution)/shard_map/ppermute | solution.py:334
  (44 shorter events, 20.6 us)
Async XLA Ops:
  9.1 4.6 %collective-permute-start = (bf16[16,128,128]{2,1,0:T(8,128)(2,1)S(1)}, bf16[16,128,128]{2,1,0:T(8,128)(2,1)S(1)}, u32[]{:S(2)}, u32[]{:S(2)}) collective-permute-start(bf16[16,128,128]{2,1,0:T(8,128)(2,1)S(1)} %get-tuple-element.35), channel_id=1, source_target_pairs={{0,128},{128,0},{1,129},{129,1},{2,130},{130,2},{3,131},{131,3},{4... | collective-permute-start | bytes 1572872 | tf_op jit(solution)/shard_map/ppermute | solution.py:338
  14.4 5.5 %collective-permute-start.1 = (bf16[4,128,128]{2,1,0:T(8,128)(2,1)S(1)}, bf16[4,128,128]{2,1,0:T(8,128)(2,1)S(1)}, u32[]{:S(2)}, u32[]{:S(2)}) collective-permute-start(bf16[4,128,128]{2,1,0:T(8,128)(2,1)S(1)} %get-tuple-element.37), channel_id=1, source_target_pairs={{0,2},{1,3},{2,0},{3,1},{4,6},{5,7},{6,4},{7,5},{8,10},{9,11},{10,... | collective-permute-start | bytes 393224 | tf_op jit(solution)/shard_map/ppermute | solution.py:334
  15.3 6.9 %collective-permute-start.2 = (bf16[4,128,128]{2,1,0:T(8,128)(2,1)S(1)}, bf16[4,128,128]{2,1,0:T(8,128)(2,1)S(1)}, u32[]{:S(2)}, u32[]{:S(2)}) collective-permute-start(bf16[4,128,128]{2,1,0:T(8,128)(2,1)S(1)} %get-tuple-element.38), channel_id=1, source_target_pairs={{0,1},{1,2},{2,3},{3,0},{4,5},{5,6},{6,7},{7,4},{8,9},{9,10},{10,1... | collective-permute-start | bytes 393224 | tf_op jit(solution)/shard_map/ppermute | solution.py:334
  16.9 5.9 %collective-permute-start.3 = (bf16[4,128,128]{2,1,0:T(8,128)(2,1)S(1)}, bf16[4,128,128]{2,1,0:T(8,128)(2,1)S(1)}, u32[]{:S(2)}, u32[]{:S(2)}) collective-permute-start(bf16[4,128,128]{2,1,0:T(8,128)(2,1)S(1)} %get-tuple-element.39), channel_id=1, source_target_pairs={{0,3},{1,0},{2,1},{3,2},{4,7},{5,4},{6,5},{7,6},{8,11},{9,8},{10,9... | collective-permute-start | bytes 393224 | tf_op jit(solution)/shard_map/ppermute | solution.py:334
  23.0 5.7 %collective-permute-start.6 = (bf16[4,128,128]{2,1,0:T(8,128)(2,1)S(1)}, bf16[4,128,128]{2,1,0:T(8,128)(2,1)S(1)}, u32[]{:S(2)}, u32[]{:S(2)}) collective-permute-start(bf16[4,128,128]{2,1,0:T(8,128)(2,1)S(1)} %first_sum.1.refs_0_), channel_id=1, source_target_pairs={{0,2},{1,3},{2,0},{3,1},{4,6},{5,7},{6,4},{7,5},{8,10},{9,11},{10,... | collective-permute-start | bytes 393224 | tf_op jit(solution)/shard_map/ppermute | solution.py:334
  23.1 8.9 %collective-permute-start.5 = (bf16[4,128,128]{2,1,0:T(8,128)(2,1)S(1)}, bf16[4,128,128]{2,1,0:T(8,128)(2,1)S(1)}, u32[]{:S(2)}, u32[]{:S(2)}) collective-permute-start(bf16[4,128,128]{2,1,0:T(8,128)(2,1)S(1)} %first_sum.1.refs_0_), channel_id=1, source_target_pairs={{0,3},{1,0},{2,1},{3,2},{4,7},{5,4},{6,5},{7,6},{8,11},{9,8},{10,9... | collective-permute-start | bytes 393224 | tf_op jit(solution)/shard_map/ppermute | solution.py:334
  25.1 7.9 %collective-permute-start.4 = (bf16[4,128,128]{2,1,0:T(8,128)(2,1)S(1)}, bf16[4,128,128]{2,1,0:T(8,128)(2,1)S(1)}, u32[]{:S(2)}, u32[]{:S(2)}) collective-permute-start(bf16[4,128,128]{2,1,0:T(8,128)(2,1)S(1)} %first_sum.1.refs_0_), channel_id=1, source_target_pairs={{0,1},{1,2},{2,3},{3,0},{4,5},{5,6},{6,7},{7,4},{8,9},{9,10},{10,1... | collective-permute-start | bytes 393224 | tf_op jit(solution)/shard_map/ppermute | solution.py:334
  25.3 8.8 %collective-permute-start.7 = (bf16[4,128,128]{2,1,0:T(8,128)(2,1)S(1)}, bf16[4,128,128]{2,1,0:T(8,128)(2,1)S(1)}, u32[]{:S(2)}, u32[]{:S(2)}) collective-permute-start(bf16[4,128,128]{2,1,0:T(8,128)(2,1)S(1)} %first_sum.1.refs_0_), channel_id=1, source_target_pairs={{0,128},{128,0},{1,129},{129,1},{2,130},{130,2},{3,131},{131,3},{4... | collective-permute-start | bytes 393224 | tf_op jit(solution)/shard_map/ppermute | solution.py:338
  28.6 5.4 %collective-permute-start.10 = (bf16[4,128,128]{2,1,0:T(8,128)(2,1)S(1)}, bf16[4,128,128]{2,1,0:T(8,128)(2,1)S(1)}, u32[]{:S(2)}, u32[]{:S(2)}) collective-permute-start(bf16[4,128,128]{2,1,0:T(8,128)(2,1)S(1)} %collective-permute-done.6.refs_3_), channel_id=1, source_target_pairs={{0,128},{128,0},{1,129},{129,1},{2,130},{130,2},{3,131},{131,3},{4... | collective-permute-start | bytes 393224 | tf_op jit(solution)/shard_map/ppermute | solution.py:338
  32.0 2.1 %collective-permute-start.9 = (bf16[4,128,128]{2,1,0:T(8,128)(2,1)S(1)}, bf16[4,128,128]{2,1,0:T(8,128)(2,1)S(1)}, u32[]{:S(2)}, u32[]{:S(2)}) collective-permute-start(bf16[4,128,128]{2,1,0:T(8,128)(2,1)S(1)} %collective-permute-done.5.refs_2_), channel_id=1, source_target_pairs={{0,128},{128,0},{1,129},{129,1},{2,130},{130,2},{3,131},{131,3},{4... | collective-permute-start | bytes 393224 | tf_op jit(solution)/shard_map/ppermute | solution.py:338
  37.5 3.4 %collective-permute-start.11 = (bf16[32,128,128]{2,1,0:T(8,128)(2,1)S(1)}, bf16[32,128,128]{2,1,0:T(8,128)(2,1)S(1)}, u32[]{:S(2)}, u32[]{:S(2)}) collective-permute-start(bf16[32,128,128]{2,1,0:T(8,128)(2,1)S(1)} %get-tuple-element.41), channel_id=1, source_target_pairs={{0,128},{128,0},{1,129},{129,1},{2,130},{130,2},{3,131},{131,3},{4... | collective-permute-start | bytes 3145736 | tf_op jit(solution)/shard_map/ppermute | solution.py:338
  41.6 8.8 %collective-permute-start.12 = (bf16[8,128,128]{2,1,0:T(8,128)(2,1)S(1)}, bf16[8,128,128]{2,1,0:T(8,128)(2,1)S(1)}, u32[]{:S(2)}, u32[]{:S(2)}) collective-permute-start(bf16[8,128,128]{2,1,0:T(8,128)(2,1)S(1)} %get-tuple-element.43), channel_id=1, source_target_pairs={{0,64},{32,96},{64,0},{96,32},{1,65},{33,97},{65,1},{97,33},{2,66}... | collective-permute-start | bytes 786440 | tf_op jit(solution)/shard_map/ppermute | solution.py:334
  44.3 12.8 %collective-permute-start.13 = (bf16[8,128,128]{2,1,0:T(8,128)(2,1)S(1)}, bf16[8,128,128]{2,1,0:T(8,128)(2,1)S(1)}, u32[]{:S(2)}, u32[]{:S(2)}) collective-permute-start(bf16[8,128,128]{2,1,0:T(8,128)(2,1)S(1)} %get-tuple-element.44), channel_id=1, source_target_pairs={{0,32},{32,64},{64,96},{96,0},{1,33},{33,65},{65,97},{97,1},{2,34}... | collective-permute-start | bytes 786440 | tf_op jit(solution)/shard_map/ppermute | solution.py:334
  46.2 12.0 %collective-permute-start.14 = (bf16[8,128,128]{2,1,0:T(8,128)(2,1)S(1)}, bf16[8,128,128]{2,1,0:T(8,128)(2,1)S(1)}, u32[]{:S(2)}, u32[]{:S(2)}) collective-permute-start(bf16[8,128,128]{2,1,0:T(8,128)(2,1)S(1)} %get-tuple-element.45), channel_id=1, source_target_pairs={{0,96},{32,0},{64,32},{96,64},{1,97},{33,1},{65,33},{97,65},{2,98}... | collective-permute-start | bytes 786440 | tf_op jit(solution)/shard_map/ppermute | solution.py:334
  88.9 7.7 %collective-permute-start.17 = (bf16[8,128,128]{2,1,0:T(8,128)(2,1)S(1)}, bf16[8,128,128]{2,1,0:T(8,128)(2,1)S(1)}, u32[]{:S(2)}, u32[]{:S(2)}) collective-permute-start(bf16[8,128,128]{2,1,0:T(8,128)(2,1)S(1)} %all_to_all.11.refs_0_), channel_id=1, source_target_pairs={{0,64},{32,96},{64,0},{96,32},{1,65},{33,97},{65,1},{97,33},{2,66}... | collective-permute-start | bytes 786440 | tf_op jit(solution)/shard_map/ppermute | solution.py:334
  90.4 11.7 %collective-permute-start.16 = (bf16[8,128,128]{2,1,0:T(8,128)(2,1)S(1)}, bf16[8,128,128]{2,1,0:T(8,128)(2,1)S(1)}, u32[]{:S(2)}, u32[]{:S(2)}) collective-permute-start(bf16[8,128,128]{2,1,0:T(8,128)(2,1)S(1)} %all_to_all.11.refs_0_), channel_id=1, source_target_pairs={{0,96},{32,0},{64,32},{96,64},{1,97},{33,1},{65,33},{97,65},{2,98}... | collective-permute-start | bytes 786440 | tf_op jit(solution)/shard_map/ppermute | solution.py:334
  92.5 12.0 %collective-permute-start.15 = (bf16[8,128,128]{2,1,0:T(8,128)(2,1)S(1)}, bf16[8,128,128]{2,1,0:T(8,128)(2,1)S(1)}, u32[]{:S(2)}, u32[]{:S(2)}) collective-permute-start(bf16[8,128,128]{2,1,0:T(8,128)(2,1)S(1)} %all_to_all.11.refs_0_), channel_id=1, source_target_pairs={{0,32},{32,64},{64,96},{96,0},{1,33},{33,65},{65,97},{97,1},{2,34}... | collective-permute-start | bytes 786440 | tf_op jit(solution)/shard_map/ppermute | solution.py:334
  92.5 12.7 %collective-permute-start.18 = (bf16[8,128,128]{2,1,0:T(8,128)(2,1)S(1)}, bf16[8,128,128]{2,1,0:T(8,128)(2,1)S(1)}, u32[]{:S(2)}, u32[]{:S(2)}) collective-permute-start(bf16[8,128,128]{2,1,0:T(8,128)(2,1)S(1)} %all_to_all.11.refs_0_), channel_id=1, source_target_pairs={{0,128},{128,0},{1,129},{129,1},{2,130},{130,2},{3,131},{131,3},{4... | collective-permute-start | bytes 786440 | tf_op jit(solution)/shard_map/ppermute | solution.py:338
  96.7 8.6 %collective-permute-start.21 = (bf16[8,128,128]{2,1,0:T(8,128)(2,1)S(1)}, bf16[8,128,128]{2,1,0:T(8,128)(2,1)S(1)}, u32[]{:S(2)}, u32[]{:S(2)}) collective-permute-start(bf16[8,128,128]{2,1,0:T(8,128)(2,1)S(1)} %collective-permute-done.17.refs_3_), channel_id=1, source_target_pairs={{0,128},{128,0},{1,129},{129,1},{2,130},{130,2},{3,131},{131,3},{4... | collective-permute-start | bytes 786440 | tf_op jit(solution)/shard_map/ppermute | solution.py:338
  102.1 3.7 %collective-permute-start.20 = (bf16[8,128,128]{2,1,0:T(8,128)(2,1)S(1)}, bf16[8,128,128]{2,1,0:T(8,128)(2,1)S(1)}, u32[]{:S(2)}, u32[]{:S(2)}) collective-permute-start(bf16[8,128,128]{2,1,0:T(8,128)(2,1)S(1)} %collective-permute-done.16.refs_2_), channel_id=1, source_target_pairs={{0,128},{128,0},{1,129},{129,1},{2,130},{130,2},{3,131},{131,3},{4... | collective-permute-start | bytes 786440 | tf_op jit(solution)/shard_map/ppermute | solution.py:338
  109.5 2.5 %collective-permute-start.22 = (bf16[16,128,128]{2,1,0:T(8,128)(2,1)S(1)}, bf16[16,128,128]{2,1,0:T(8,128)(2,1)S(1)}, u32[]{:S(2)}, u32[]{:S(2)}) collective-permute-start(bf16[16,128,128]{2,1,0:T(8,128)(2,1)S(1)} %get-tuple-element.49), channel_id=1, source_target_pairs={{0,128},{128,0},{1,129},{129,1},{2,130},{130,2},{3,131},{131,3},{4... | collective-permute-start | bytes 1572872 | tf_op jit(solution)/shard_map/ppermute | solution.py:338
  112.7 5.6 %collective-permute-start.23 = (bf16[528,128]{1,0:T(8,128)(2,1)S(1)}, bf16[528,128]{1,0:T(8,128)(2,1)S(1)}, u32[]{:S(2)}, u32[]{:S(2)}) collective-permute-start(bf16[528,128]{1,0:T(8,128)(2,1)S(1)} %get-tuple-element.53), channel_id=1, source_target_pairs={{0,2},{1,3},{2,0},{3,1},{4,6},{5,7},{6,4},{7,5},{8,10},{9,11},{10,... | collective-permute-start | bytes 405512 | tf_op jit(solution)/shard_map/ppermute | solution.py:334
  114.2 7.9 %collective-permute-start.24 = (bf16[528,128]{1,0:T(8,128)(2,1)S(1)}, bf16[528,128]{1,0:T(8,128)(2,1)S(1)}, u32[]{:S(2)}, u32[]{:S(2)}) collective-permute-start(bf16[528,128]{1,0:T(8,128)(2,1)S(1)} %get-tuple-element.54), channel_id=1, source_target_pairs={{0,1},{1,2},{2,3},{3,0},{4,5},{5,6},{6,7},{7,4},{8,9},{9,10},{10,1... | collective-permute-start | bytes 405512 | tf_op jit(solution)/shard_map/ppermute | solution.py:334
  118.3 6.1 %collective-permute-start.25 = (bf16[528,128]{1,0:T(8,128)(2,1)S(1)}, bf16[528,128]{1,0:T(8,128)(2,1)S(1)}, u32[]{:S(2)}, u32[]{:S(2)}) collective-permute-start(bf16[528,128]{1,0:T(8,128)(2,1)S(1)} %get-tuple-element.55), channel_id=1, source_target_pairs={{0,3},{1,0},{2,1},{3,2},{4,7},{5,4},{6,5},{7,6},{8,11},{9,8},{10,9... | collective-permute-start | bytes 405512 | tf_op jit(solution)/shard_map/ppermute | solution.py:334
  (2 other events, 3.9 us)

commit v2 on v1

--- a/solution.py
+++ b/solution.py
@@ -19,7 +19,7 @@
 N_SLOTS = 256
 SLOT_BITS, ROW_BITS, COL_BITS = 8, 5, 6
 BLOCK = 64
-UNROLL = 16
+UNROLL = 32
 STEPS = 4
 SORT_STEP = 16
 SHIFTS = (0, 2, 1, 3)
@@ -89,23 +89,42 @@
     each(out.shape[0], one)
 
 
-def sort_slots(first, size, rows, cols, live, core, by_row, by_col, counts):
+def sort_slots(first, size, rows, cols, live, core, order, by_row, counts):
+    bits = ROW_BITS if by_row else COL_BITS
+
     def several(g, carry):
-        row_sends, row_keeps, col_sends, col_keeps = carry
+        sends, keeps = carry
         slots = [first + g * SORT_STEP + j for j in range(SORT_STEP)]
         loaded = [(t, rows[t], cols[t]) for t in slots]
         for t, row, col in loaded:
             code = t + (row << SLOT_BITS) + (col << (SLOT_BITS + ROW_BITS))
-            used = t < live
-            row_own = jnp.where(jnp.logical_and(used, row >> (ROW_BITS - 1) == core), 1, 0)
-            col_own = jnp.where(jnp.logical_and(used, col >> (COL_BITS - 1) == core), 1, 0)
-            by_row[jnp.where(row_own == 1, N_SLOTS - 1 - row_keeps, row_sends)] = code
-            by_col[jnp.where(col_own == 1, N_SLOTS - 1 - col_keeps, col_sends)] = code
-            row_sends, row_keeps = row_sends + 1 - row_own, row_keeps + row_own
-            col_sends, col_keeps = col_sends + 1 - col_own, col_keeps + col_own
-        return row_sends, row_keeps, col_sends, col_keeps
+            dst = row if by_row else col
+            own = jnp.where(jnp.logical_and(t < live, dst >> (bits - 1) == core), 1, 0)
+            order[jnp.where(own == 1, N_SLOTS - 1 - keeps, sends)] = code
+            sends, keeps = sends + 1 - own, keeps + own
+        return sends, keeps
 
     return lax.fori_loop(0, size // SORT_STEP, several, counts)
+
+
+def sort_kernel(rows, cols, count, ids, after, order, numbers):
+    live = count[0]
+    counts = sort_slots(0, N_SLOTS, rows, cols, live, ids[CORE], order, False, (0, 0))
+    numbers[0] = live - counts[1]
+    numbers[1] = counts[1]
+
+
+def sort_by_col(rows, cols, count, ids, after):
+    words = lambda k: jax.ShapeDtypeStruct((k,), jnp.int32)
+    return pl.pallas_call(
+        sort_kernel,
+        in_specs=[SMEM] * 4 + [pl.BlockSpec(memory_space=pl.ANY)],
+        out_specs=[SMEM, SMEM],
+        out_shape=[words(N_SLOTS), words(2)],
+        cost_estimate=pl.CostEstimate(flops=2 * 10**9, bytes_accessed=4096, transcendentals=0),
+        compiler_params=PARAMS,
+        name="sort_by_col",
+    )(rows, cols, count, ids, after)
 
 
 def place(ids, parts, panel, axis, n, per):
@@ -123,7 +142,7 @@
 
 
 def first_send_kernel(
-    rows_hbm, cols_hbm, count, ids, tiles_hbm, panel_hbm, send, by_row, by_col, numbers, tiles, panel, rows, cols, acc, sems
+    rows_hbm, cols_hbm, count, ids, tiles_hbm, panel_hbm, send, by_row, numbers, tiles, panel, rows, cols, acc, sems
 ):
     lists = [
         pltpu.make_async_copy(rows_hbm, rows, sems.at[0]),
@@ -142,9 +161,9 @@
     for copy in lists:
         copy.wait()
     live, core = count[0], ids[CORE]
-    counts, done, last = (0, 0, 0, 0), 0, N_SLOTS // BLOCK - 1
+    counts, done, last = (0, 0), 0, N_SLOTS // BLOCK - 1
     for i in range(last + 1):
-        counts = sort_slots(i * BLOCK, BLOCK, rows, cols, live, core, by_row, by_col, counts)
+        counts = sort_slots(i * BLOCK, BLOCK, rows, cols, live, core, by_row, True, counts)
         sends = jnp.minimum(live, (i + 1) * BLOCK) - counts[1]
         if i == 0:
             start.wait()
@@ -154,8 +173,6 @@
         done = until
     numbers[0] = live - counts[1]
     numbers[1] = counts[1]
-    numbers[2] = live - counts[3]
-    numbers[3] = counts[3]
     narrow(acc, send)
 
 
@@ -169,8 +186,8 @@
     return pl.pallas_call(
         first_send_kernel,
         in_specs=[HBM, HBM, SMEM, SMEM, HBM, HBM],
-        out_specs=[VMEM, SMEM, SMEM, SMEM, VMEM, VMEM],
-        out_shape=[tiles_of(CTILES // 2, BF16), words(n), words(n), words(4), tiles_of(n, BF16), tiles_of(DTILES, BF16)],
+        out_specs=[VMEM, SMEM, SMEM, VMEM, VMEM],
+        out_shape=[tiles_of(CTILES // 2, BF16), words(n), words(2), tiles_of(n, BF16), tiles_of(DTILES, BF16)],
         scratch_shapes=[
             pltpu.SMEM((n,), jnp.int32),
             pltpu.SMEM((n,), jnp.int32),
@@ -186,7 +203,7 @@
     parts, (send, panel, acc) = refs[: 2 * n], refs[2 * n :]
     zero(acc)
     place(ids, parts, panel, axis, n, per)
-    sends = numbers[0 if by_row else 2]
+    sends = numbers[0]
     accumulate(0, groups(sends), sends, order, tiles, panel, acc, by_row, False)
     narrow(acc, send)
 
@@ -208,7 +225,7 @@
 
 def keep_kernel(order, numbers, tiles, panel, keep, *squares, by_row):
     zero(keep)
-    keeps = numbers[1 if by_row else 3]
+    keeps = numbers[1]
     accumulate(0, groups(keeps), keeps, order, tiles, panel, keep, by_row, True)
     if squares:
 
@@ -259,7 +276,7 @@
     )(ids, keep, got)
 
 
-def caller_kernel(own, a, b, c, out):
+def caller_kernel(sorted_first, own, a, b, c, out):
     def one(i):
         total = own[i] + a[i].astype(F32) + b[i].astype(F32) + c[i].astype(F32)
         out[i] = total.astype(BF16).astype(F32).T.astype(BF16)
@@ -356,16 +373,24 @@
     start = start_panel.reshape(DTILES, TILE, RANK)
     quarter = CTILES // 2 // NCOL
 
-    send, by_row, by_col, numbers, tiles, panel = first_send(rows, cols, count, ids, tiles, start)
+    send, by_row, row_numbers, tiles, panel = first_send(rows, cols, count, ids, tiles, start)
     got = swap(send)
-    [keep] = keep_part(by_row, numbers, tiles, panel, True, [], "first_keep")
+    [keep] = keep_part(by_row, row_numbers, tiles, panel, True, [], "first_keep")
     own, *sends = pair_sum(ids, keep, got, COL, NCOL, quarter, "first_pair")
-    part = four_sum(caller_kernel, own, exchange(sends, "col", NCOL), "first_sum")
+    by_col, col_numbers = sort_by_col(rows, cols, count, ids, own)
+    part = pl.pallas_call(
+        caller_kernel,
+        in_specs=[SMEM] + [VMEM] * NCOL,
+        out_specs=VMEM,
+        out_shape=tiles_of(quarter, BF16),
+        compiler_params=PARAMS,
+        name="first_sum",
+    )(col_numbers, own, *exchange(sends, "col", NCOL))
     parts = gather(part, "col", NCOL)
 
-    send, panel = send_part(by_col, numbers, ids, tiles, parts, False, COL, "back_send")
+    send, panel = send_part(by_col, col_numbers, ids, tiles, parts, False, COL, "back_send")
     got = swap(send)
-    [keep] = keep_part(by_col, numbers, tiles, panel, False, [], "back_keep")
+    [keep] = keep_part(by_col, col_numbers, tiles, panel, False, [], "back_keep")
     own, *sends = pair_sum(ids, keep, got, XPOS, NX, NZ, "back_pair")
     part = four_sum(row_kernel, own, exchange(sends, "x", NX), "back_sum")
     got = lax.all_to_all(part, "z", split_axis=0, concat_axis=0, tiled=True)
@@ -380,10 +405,10 @@
     part = lax.all_to_all(copies, "z", split_axis=0, concat_axis=0, tiled=True)
     parts = gather(part, "x", NX)
 
-    send, panel = send_part(by_row, numbers, ids, tiles, parts, True, XPOS, "last_send")
+    send, panel = send_part(by_row, row_numbers, ids, tiles, parts, True, XPOS, "last_send")
     got = swap(send)
     keep, squares = keep_part(
-        by_row, numbers, tiles, panel, True, [jax.ShapeDtypeStruct((TILE // 4, RANK), F32)], "last_keep"
+        by_row, row_numbers, tiles, panel, True, [jax.ShapeDtypeStruct((TILE // 4, RANK), F32)], "last_keep"
     )
     chunk = jax.ShapeDtypeStruct((quarter * TILE + 16, RANK), BF16)
     own, *sends = pl.pallas_call(

time: 125 us -> 124 us (level)
  waiting for transfers between devices: 24.4 us -> 21.1 us
  starting transfers between devices: 45.8 us -> 49 us
    ppermute x15, starting transfers between devices: 20.4 us -> 26.3 us  [shifted(): return lax.ppermute(value, axis, [(i, (i + k) % n) for i in range(n)])]
    ppermute x15, waiting for transfers between devices: 22.2 us -> 18.3 us  [shifted(): return lax.ppermute(value, axis, [(i, (i + k) % n) for i in range(n)])]
    pallas_call x0 -> x2, Pallas kernels: none -> 3.81 us  [the longest x1 3.13 us: sort_by_col(): pl.pallas_call(sort_kernel, in_specs=[SMEM] * 4 + [pl.BlockSpec(memory_sp...]
    ppermute x11, starting transfers between devices: 25.4 us -> 22.7 us  [swap(): return lax.ppermute(value, 'layer', [(0, 1), (1, 0)])]
    pallas_call x1, Pallas kernels: 7.74 us -> 5.91 us  [first_send(): pl.pallas_call(first_send_kernel, in_specs=[HBM, HBM, SMEM, SMEM, HBM, HB...]
    pallas_call x2, Pallas kernels: 5.5 us -> 3.72 us  [send_part(): pl.pallas_call(functools.partial(send_kernel, by_row=by_row, axis=axis, n...]
  transfers between devices with their start and end apart: 26 -> 26, of which waited for: 11 -> 12; matrix products, arithmetic and copies ran while one was open for 0% -> 0% of each run, Pallas kernels for 5% -> 7%
where the time goes in v2:
time: 124 us; the launch traced here: 123 us
  starting transfers between devices  49 us (40%)
  blocking collectives  29.6 us (24%)
  Pallas kernels  22 us (18%)
  waiting for transfers between devices  21.1 us (17%)
  between operations  1.42 us (1%)
    ppermute x15, starting transfers between devices, shifted(): return lax.ppermute(value, axis, [(i, (i + k) % n) for i in range(n)])  26.3 us
    ppermute x11, starting transfers between devices, swap(): return lax.ppermute(value, 'layer', [(0, 1), (1, 0)])  22.7 us
    ppermute x15, waiting for transfers between devices, shifted(): return lax.ppermute(value, axis, [(i, (i + k) % n) for i in range(n)])  18.3 us
    all_to_all x1, blocking collectives, on_device(): got = lax.all_to_all(part, 'z', split_axis=0, concat_axis=0, tiled=True)  17.7 us
    all_to_all x1, blocking collectives, on_device(): part = lax.all_to_all(copies, 'z', split_axis=0, concat_axis=0, tiled=True)  12 us
    pallas_call x1, Pallas kernels, first_send(): pl.pallas_call(first_send_kernel, in_specs=[HBM, HBM, SMEM, SMEM, HBM, HB...  5.91 us
    pallas_call x3, Pallas kernels, keep_part(): pl.pallas_call(functools.partial(keep_kernel, by_row=by_row), in_specs=[S...  5.45 us
    pallas_call x2, Pallas kernels, send_part(): pl.pallas_call(functools.partial(send_kernel, by_row=by_row, axis=axis, n...  3.72 us
  transfers between devices with their start and end apart: 26, of which 12 were waited for; matrix products, arithmetic and copies ran while one was open for 0% of the time, Pallas kernels for 7%

profile of v2, /device:TPU:1, one launch (start us, length us, event | category | flops | bytes accessed | tf_op | source)
XLA Modules:
  0.0 123.2 jit_solution(3784832504947026180)
XLA Ops:
  1.4 5.9 %first_send.1 = (bf16[16,128,128]{2,1,0:T(8,128)(2,1)S(1)}, s32[256]{0:T(256)S(1)}, s32[2]{0:T(128)S(1)}, bf16[256,128,128]{2,1,0:T(8,128)(2,1)S(1)}, bf16[64,128,128]{2,1,0:T(8,128)(2,1)S(1)}) custom-call(s32[256]{0:T(256)} %bitcast.12, s32[256]{0:T(256)} %bitcast.14, s32[1]{0:T(128)} %bitcast.10.count, s32[3]{0:T(128)S(1)} %pad_add_fusion.ids, ...), custom_call_target="tpu_custom_call" | custom-call | tf_op jit(solution)/shard_map/first_send/pallas_call | solution.py:186
  7.3 3.2 %collective-permute-start = (bf16[16,128,128]{2,1,0:T(8,128)(2,1)S(1)}, bf16[16,128,128]{2,1,0:T(8,128)(2,1)S(1)}, u32[]{:S(2)}, u32[]{:S(2)}) collective-permute-start(bf16[16,128,128]{2,1,0:T(8,128)(2,1)S(1)} %get-tuple-element.35), channel_id=1, source_target_pairs={{0,128},{128,0},{1,129},{129,1},{2,130},{130,2},{3,131},{131,3},{4... | collective-permute-start | bytes 1572872 | tf_op jit(solution)/shard_map/ppermute | solution.py:355
  12.8 3.1 %collective-permute-start.1 = (bf16[4,128,128]{2,1,0:T(8,128)(2,1)S(1)}, bf16[4,128,128]{2,1,0:T(8,128)(2,1)S(1)}, u32[]{:S(2)}, u32[]{:S(2)}) collective-permute-start(bf16[4,128,128]{2,1,0:T(8,128)(2,1)S(1)} %get-tuple-element.39), channel_id=1, source_target_pairs={{0,2},{1,3},{2,0},{3,1},{4,6},{5,7},{6,4},{7,5},{8,10},{9,11},{10,... | collective-permute-start | bytes 393224 | tf_op jit(solution)/shard_map/ppermute | solution.py:351
  16.2 2.3 %collective-permute-start.3 = (bf16[4,128,128]{2,1,0:T(8,128)(2,1)S(1)}, bf16[4,128,128]{2,1,0:T(8,128)(2,1)S(1)}, u32[]{:S(2)}, u32[]{:S(2)}) collective-permute-start(bf16[4,128,128]{2,1,0:T(8,128)(2,1)S(1)} %get-tuple-element.41), channel_id=1, source_target_pairs={{0,3},{1,0},{2,1},{3,2},{4,7},{5,4},{6,5},{7,6},{8,11},{9,8},{10,9... | collective-permute-start | bytes 393224 | tf_op jit(solution)/shard_map/ppermute | solution.py:351
  18.5 3.1 %sort_by_col.1 = (s32[256]{0:T(256)S(1)}, s32[2]{0:T(128)S(1)}) custom-call(s32[256]{0:T(256)S(1)} %bitcast.13, s32[256]{0:T(256)S(1)} %bitcast.15, s32[1]{0:T(128)} %bitcast.11.count, s32[3]{0:T(128)S(1)} %pad_add_fusion.ids, f32[4,128,128]{2,1,0:T(8,128)S(1)} %get-tuple-element.36.after.own), custom_call_target="tpu_custom_call" | custom-call | flops 2000000000 | bytes 4096 | tf_op jit(solution)/shard_map/sort_by_col/pallas_call | solution.py:119
  23.8 1.6 %collective-permute-start.6 = (bf16[4,128,128]{2,1,0:T(8,128)(2,1)S(1)}, bf16[4,128,128]{2,1,0:T(8,128)(2,1)S(1)}, u32[]{:S(2)}, u32[]{:S(2)}) collective-permute-start(bf16[4,128,128]{2,1,0:T(8,128)(2,1)S(1)} %first_sum.1.refs_0_), channel_id=1, source_target_pairs={{0,2},{1,3},{2,0},{3,1},{4,6},{5,7},{6,4},{7,5},{8,10},{9,11},{10,... | collective-permute-start | bytes 393224 | tf_op jit(solution)/shard_map/ppermute | solution.py:351
  28.4 1.7 %collective-permute-done.6.refs_3_ = bf16[4,128,128]{2,1,0:T(8,128)(2,1)S(1)} collective-permute-done((bf16[4,128,128]{2,1,0:T(8,128)(2,1)S(1)}, bf16[4,128,128]{2,1,0:T(8,128)(2,1)S(1)}, u32[]{:S(2)}, u32[]{:S(2)}) %collective-permute-start.6) | collective-permute-done | bytes 131104 | tf_op jit(solution)/shard_map/ppermute | solution.py:351
  30.0 2.1 %collective-permute-start.10 = (bf16[4,128,128]{2,1,0:T(8,128)(2,1)S(1)}, bf16[4,128,128]{2,1,0:T(8,128)(2,1)S(1)}, u32[]{:S(2)}, u32[]{:S(2)}) collective-permute-start(bf16[4,128,128]{2,1,0:T(8,128)(2,1)S(1)} %collective-permute-done.6.refs_3_), channel_id=1, source_target_pairs={{0,128},{128,0},{1,129},{129,1},{2,130},{130,2},{3,131},{131,3},{4... | collective-permute-start | bytes 393224 | tf_op jit(solution)/shard_map/ppermute | solution.py:355
  35.5 1.9 %back_send.1 = (bf16[32,128,128]{2,1,0:T(8,128)(2,1)S(1)}, bf16[32,128,128]{2,1,0:T(8,128)(2,1)S(1)}) custom-call(s32[256]{0:T(256)S(1)} %get-tuple-element.37.order, s32[2]{0:T(128)S(1)} %get-tuple-element.38.sorted_first.numbers, s32[3]{0:T(128)S(1)} %pad_add_fusion.ids, bf16[256,128,128]{2,1,0:T(8,128)(2,1)S(1)} %get-tuple-element.33.tiles, ...), custom_call_target="tpu_custom_call" | custom-call | tf_op jit(solution)/shard_map/back_send/pallas_call | solution.py:215
  37.8 1.7 %back_keep.1.keep = f32[33,128,128]{2,1,0:T(8,128)S(1)} custom-call(s32[256]{0:T(256)S(1)} %get-tuple-element.37.order, s32[2]{0:T(128)S(1)} %get-tuple-element.38.sorted_first.numbers, bf16[256,128,128]{2,1,0:T(8,128)(2,1)S(1)} %get-tuple-element.33.tiles, bf16[32,128,128]{2,1,0:T(8,128)(2,1)S(1)} %get-tuple-element.42.panel), custom_call_target="tpu_custom_call" | custom-call | flops 1073741824 | bytes 10485760 | tf_op jit(solution)/shard_map/back_keep/pallas_call | solution.py:242
  40.9 4.5 %collective-permute-start.12 = (bf16[8,128,128]{2,1,0:T(8,128)(2,1)S(1)}, bf16[8,128,128]{2,1,0:T(8,128)(2,1)S(1)}, u32[]{:S(2)}, u32[]{:S(2)}) collective-permute-start(bf16[8,128,128]{2,1,0:T(8,128)(2,1)S(1)} %get-tuple-element.45), channel_id=1, source_target_pairs={{0,64},{32,96},{64,0},{96,32},{1,65},{33,97},{65,1},{97,33},{2,66}... | collective-permute-start | bytes 786440 | tf_op jit(solution)/shard_map/ppermute | solution.py:351
  45.5 2.7 %collective-permute-start.14 = (bf16[8,128,128]{2,1,0:T(8,128)(2,1)S(1)}, bf16[8,128,128]{2,1,0:T(8,128)(2,1)S(1)}, u32[]{:S(2)}, u32[]{:S(2)}) collective-permute-start(bf16[8,128,128]{2,1,0:T(8,128)(2,1)S(1)} %get-tuple-element.47), channel_id=1, source_target_pairs={{0,96},{32,0},{64,32},{96,64},{1,97},{33,1},{65,33},{97,65},{2,98}... | collective-permute-start | bytes 786440 | tf_op jit(solution)/shard_map/ppermute | solution.py:351
  48.1 3.9 %collective-permute-done.12.a = bf16[8,128,128]{2,1,0:T(8,128)(2,1)S(1)} collective-permute-done((bf16[8,128,128]{2,1,0:T(8,128)(2,1)S(1)}, bf16[8,128,128]{2,1,0:T(8,128)(2,1)S(1)}, u32[]{:S(2)}, u32[]{:S(2)}) %collective-permute-start.12) | collective-permute-done | bytes 262176 | tf_op jit(solution)/shard_map/ppermute | solution.py:351
  52.1 5.8 %collective-permute-done.13.b = bf16[8,128,128]{2,1,0:T(8,128)(2,1)S(1)} collective-permute-done((bf16[8,128,128]{2,1,0:T(8,128)(2,1)S(1)}, bf16[8,128,128]{2,1,0:T(8,128)(2,1)S(1)}, u32[]{:S(2)}, u32[]{:S(2)}) %collective-permute-start.13) | collective-permute-done | bytes 262176 | tf_op jit(solution)/shard_map/ppermute | solution.py:351
  58.0 17.7 %all_to_all.10.got = bf16[8,128,128]{2,1,0:T(8,128)(2,1)S(1)} all-to-all(bf16[8,128,128]{2,1,0:T(8,128)(2,1)S(1)} %back_sum.1), channel_id=1, replica_groups=mesh['layer'=2,'x'=4,'z'=8,'col'=4] {'z'}, dimensions={0} | all-to-all | bytes 524288 | tf_op jit(solution)/shard_map/all_to_all | solution.py:396
  75.8 12.0 %all_to_all.11.refs_0_ = bf16[8,128,128]{2,1,0:T(8,128)(2,1)S(1)} all-to-all(bf16[8,128,128]{2,1,0:T(8,128)(2,1)S(1)} %get-tuple-element.48), channel_id=1, replica_groups=mesh['layer'=2,'x'=4,'z'=8,'col'=4] {'z'}, dimensions={0} | all-to-all | bytes 524288 | tf_op jit(solution)/shard_map/all_to_all | solution.py:405
  89.0 3.1 %collective-permute-start.16 = (bf16[8,128,128]{2,1,0:T(8,128)(2,1)S(1)}, bf16[8,128,128]{2,1,0:T(8,128)(2,1)S(1)}, u32[]{:S(2)}, u32[]{:S(2)}) collective-permute-start(bf16[8,128,128]{2,1,0:T(8,128)(2,1)S(1)} %all_to_all.11.refs_0_), channel_id=1, source_target_pairs={{0,96},{32,0},{64,32},{96,64},{1,97},{33,1},{65,33},{97,65},{2,98}... | collective-permute-start | bytes 786440 | tf_op jit(solution)/shard_map/ppermute | solution.py:351
  92.0 4.1 %collective-permute-start.18 = (bf16[8,128,128]{2,1,0:T(8,128)(2,1)S(1)}, bf16[8,128,128]{2,1,0:T(8,128)(2,1)S(1)}, u32[]{:S(2)}, u32[]{:S(2)}) collective-permute-start(bf16[8,128,128]{2,1,0:T(8,128)(2,1)S(1)} %all_to_all.11.refs_0_), channel_id=1, source_target_pairs={{0,128},{128,0},{1,129},{129,1},{2,130},{130,2},{3,131},{131,3},{4... | collective-permute-start | bytes 786440 | tf_op jit(solution)/shard_map/ppermute | solution.py:355
  96.1 4.8 %collective-permute-start.21 = (bf16[8,128,128]{2,1,0:T(8,128)(2,1)S(1)}, bf16[8,128,128]{2,1,0:T(8,128)(2,1)S(1)}, u32[]{:S(2)}, u32[]{:S(2)}) collective-permute-start(bf16[8,128,128]{2,1,0:T(8,128)(2,1)S(1)} %collective-permute-done.17.refs_3_), channel_id=1, source_target_pairs={{0,128},{128,0},{1,129},{129,1},{2,130},{130,2},{3,131},{131,3},{4... | collective-permute-start | bytes 786440 | tf_op jit(solution)/shard_map/ppermute | solution.py:355
  100.9 2.8 %collective-permute-start.20 = (bf16[8,128,128]{2,1,0:T(8,128)(2,1)S(1)}, bf16[8,128,128]{2,1,0:T(8,128)(2,1)S(1)}, u32[]{:S(2)}, u32[]{:S(2)}) collective-permute-start(bf16[8,128,128]{2,1,0:T(8,128)(2,1)S(1)} %collective-permute-done.16.refs_2_), channel_id=1, source_target_pairs={{0,128},{128,0},{1,129},{129,1},{2,130},{130,2},{3,131},{131,3},{4... | collective-permute-start | bytes 786440 | tf_op jit(solution)/shard_map/ppermute | solution.py:355
  105.9 1.9 %last_send.1 = (bf16[16,128,128]{2,1,0:T(8,128)(2,1)S(1)}, bf16[64,128,128]{2,1,0:T(8,128)(2,1)S(1)}) custom-call(s32[256]{0:T(256)S(1)} %get-tuple-element.31.order, s32[2]{0:T(128)S(1)} %get-tuple-element.32.numbers, s32[3]{0:T(128)S(1)} %pad_add_fusion.ids, bf16[256,128,128]{2,1,0:T(8,128)(2,1)S(1)} %get-tuple-element.33.tiles, ...), custom_call_target="tpu_custom_call" | custom-call | tf_op jit(solution)/shard_map/last_send/pallas_call | solution.py:215
  108.2 2.2 %last_keep.1 = (f32[17,128,128]{2,1,0:T(8,128)S(1)}, f32[32,128]{1,0:T(8,128)S(1)}) custom-call(s32[256]{0:T(256)S(1)} %get-tuple-element.31.order, s32[2]{0:T(128)S(1)} %get-tuple-element.32.numbers, bf16[256,128,128]{2,1,0:T(8,128)(2,1)S(1)} %get-tuple-element.33.tiles, bf16[64,128,128]{2,1,0:T(8,128)(2,1)S(1)} %get-tuple-element.49.panel), custom_call_target="tpu_custom_call" | custom-call | flops 1073741824 | bytes 10485760 | tf_op jit(solution)/shard_map/last_keep/pallas_call | solution.py:242
  111.1 3.2 %collective-permute-start.23 = (bf16[528,128]{1,0:T(8,128)(2,1)S(1)}, bf16[528,128]{1,0:T(8,128)(2,1)S(1)}, u32[]{:S(2)}, u32[]{:S(2)}) collective-permute-start(bf16[528,128]{1,0:T(8,128)(2,1)S(1)} %get-tuple-element.55), channel_id=1, source_target_pairs={{0,2},{1,3},{2,0},{3,1},{4,6},{5,7},{6,4},{7,5},{8,10},{9,11},{10,... | collective-permute-start | bytes 405512 | tf_op jit(solution)/shard_map/ppermute | solution.py:351
  118.2 2.6 %collective-permute-done.24.b = bf16[528,128]{1,0:T(8,128)(2,1)S(1)} collective-permute-done((bf16[528,128]{1,0:T(8,128)(2,1)S(1)}, bf16[528,128]{1,0:T(8,128)(2,1)S(1)}, u32[]{:S(2)}, u32[]{:S(2)}) %collective-permute-start.24) | collective-permute-done | bytes 135200 | tf_op jit(solution)/shard_map/ppermute | solution.py:351
  (49 shorter events, 24.1 us)
Async XLA Ops:
  7.3 4.8 %collective-permute-start = (bf16[16,128,128]{2,1,0:T(8,128)(2,1)S(1)}, bf16[16,128,128]{2,1,0:T(8,128)(2,1)S(1)}, u32[]{:S(2)}, u32[]{:S(2)}) collective-permute-start(bf16[16,128,128]{2,1,0:T(8,128)(2,1)S(1)} %get-tuple-element.35), channel_id=1, source_target_pairs={{0,128},{128,0},{1,129},{129,1},{2,130},{130,2},{3,131},{131,3},{4... | collective-permute-start | bytes 1572872 | tf_op jit(solution)/shard_map/ppermute | solution.py:355
  12.8 8.9 %collective-permute-start.1 = (bf16[4,128,128]{2,1,0:T(8,128)(2,1)S(1)}, bf16[4,128,128]{2,1,0:T(8,128)(2,1)S(1)}, u32[]{:S(2)}, u32[]{:S(2)}) collective-permute-start(bf16[4,128,128]{2,1,0:T(8,128)(2,1)S(1)} %get-tuple-element.39), channel_id=1, source_target_pairs={{0,2},{1,3},{2,0},{3,1},{4,6},{5,7},{6,4},{7,5},{8,10},{9,11},{10,... | collective-permute-start | bytes 393224 | tf_op jit(solution)/shard_map/ppermute | solution.py:351
  15.8 6.8 %collective-permute-start.2 = (bf16[4,128,128]{2,1,0:T(8,128)(2,1)S(1)}, bf16[4,128,128]{2,1,0:T(8,128)(2,1)S(1)}, u32[]{:S(2)}, u32[]{:S(2)}) collective-permute-start(bf16[4,128,128]{2,1,0:T(8,128)(2,1)S(1)} %get-tuple-element.40), channel_id=1, source_target_pairs={{0,1},{1,2},{2,3},{3,0},{4,5},{5,6},{6,7},{7,4},{8,9},{9,10},{10,1... | collective-permute-start | bytes 393224 | tf_op jit(solution)/shard_map/ppermute | solution.py:351
  16.2 6.9 %collective-permute-start.3 = (bf16[4,128,128]{2,1,0:T(8,128)(2,1)S(1)}, bf16[4,128,128]{2,1,0:T(8,128)(2,1)S(1)}, u32[]{:S(2)}, u32[]{:S(2)}) collective-permute-start(bf16[4,128,128]{2,1,0:T(8,128)(2,1)S(1)} %get-tuple-element.41), channel_id=1, source_target_pairs={{0,3},{1,0},{2,1},{3,2},{4,7},{5,4},{6,5},{7,6},{8,11},{9,8},{10,9... | collective-permute-start | bytes 393224 | tf_op jit(solution)/shard_map/ppermute | solution.py:351
  23.8 6.3 %collective-permute-start.6 = (bf16[4,128,128]{2,1,0:T(8,128)(2,1)S(1)}, bf16[4,128,128]{2,1,0:T(8,128)(2,1)S(1)}, u32[]{:S(2)}, u32[]{:S(2)}) collective-permute-start(bf16[4,128,128]{2,1,0:T(8,128)(2,1)S(1)} %first_sum.1.refs_0_), channel_id=1, source_target_pairs={{0,2},{1,3},{2,0},{3,1},{4,6},{5,7},{6,4},{7,5},{8,10},{9,11},{10,... | collective-permute-start | bytes 393224 | tf_op jit(solution)/shard_map/ppermute | solution.py:351
  25.4 6.7 %collective-permute-start.5 = (bf16[4,128,128]{2,1,0:T(8,128)(2,1)S(1)}, bf16[4,128,128]{2,1,0:T(8,128)(2,1)S(1)}, u32[]{:S(2)}, u32[]{:S(2)}) collective-permute-start(bf16[4,128,128]{2,1,0:T(8,128)(2,1)S(1)} %first_sum.1.refs_0_), channel_id=1, source_target_pairs={{0,3},{1,0},{2,1},{3,2},{4,7},{5,4},{6,5},{7,6},{8,11},{9,8},{10,9... | collective-permute-start | bytes 393224 | tf_op jit(solution)/shard_map/ppermute | solution.py:351
  26.9 6.3 %collective-permute-start.4 = (bf16[4,128,128]{2,1,0:T(8,128)(2,1)S(1)}, bf16[4,128,128]{2,1,0:T(8,128)(2,1)S(1)}, u32[]{:S(2)}, u32[]{:S(2)}) collective-permute-start(bf16[4,128,128]{2,1,0:T(8,128)(2,1)S(1)} %first_sum.1.refs_0_), channel_id=1, source_target_pairs={{0,1},{1,2},{2,3},{3,0},{4,5},{5,6},{6,7},{7,4},{8,9},{9,10},{10,1... | collective-permute-start | bytes 393224 | tf_op jit(solution)/shard_map/ppermute | solution.py:351
  26.9 7.6 %collective-permute-start.7 = (bf16[4,128,128]{2,1,0:T(8,128)(2,1)S(1)}, bf16[4,128,128]{2,1,0:T(8,128)(2,1)S(1)}, u32[]{:S(2)}, u32[]{:S(2)}) collective-permute-start(bf16[4,128,128]{2,1,0:T(8,128)(2,1)S(1)} %first_sum.1.refs_0_), channel_id=1, source_target_pairs={{0,128},{128,0},{1,129},{129,1},{2,130},{130,2},{3,131},{131,3},{4... | collective-permute-start | bytes 393224 | tf_op jit(solution)/shard_map/ppermute | solution.py:355
  30.0 4.5 %collective-permute-start.10 = (bf16[4,128,128]{2,1,0:T(8,128)(2,1)S(1)}, bf16[4,128,128]{2,1,0:T(8,128)(2,1)S(1)}, u32[]{:S(2)}, u32[]{:S(2)}) collective-permute-start(bf16[4,128,128]{2,1,0:T(8,128)(2,1)S(1)} %collective-permute-done.6.refs_3_), channel_id=1, source_target_pairs={{0,128},{128,0},{1,129},{129,1},{2,130},{130,2},{3,131},{131,3},{4... | collective-permute-start | bytes 393224 | tf_op jit(solution)/shard_map/ppermute | solution.py:355
  32.1 2.4 %collective-permute-start.9 = (bf16[4,128,128]{2,1,0:T(8,128)(2,1)S(1)}, bf16[4,128,128]{2,1,0:T(8,128)(2,1)S(1)}, u32[]{:S(2)}, u32[]{:S(2)}) collective-permute-start(bf16[4,128,128]{2,1,0:T(8,128)(2,1)S(1)} %collective-permute-done.5.refs_2_), channel_id=1, source_target_pairs={{0,128},{128,0},{1,129},{129,1},{2,130},{130,2},{3,131},{131,3},{4... | collective-permute-start | bytes 393224 | tf_op jit(solution)/shard_map/ppermute | solution.py:355
  37.4 2.7 %collective-permute-start.11 = (bf16[32,128,128]{2,1,0:T(8,128)(2,1)S(1)}, bf16[32,128,128]{2,1,0:T(8,128)(2,1)S(1)}, u32[]{:S(2)}, u32[]{:S(2)}) collective-permute-start(bf16[32,128,128]{2,1,0:T(8,128)(2,1)S(1)} %get-tuple-element.43), channel_id=1, source_target_pairs={{0,128},{128,0},{1,129},{129,1},{2,130},{130,2},{3,131},{131,3},{4... | collective-permute-start | bytes 3145736 | tf_op jit(solution)/shard_map/ppermute | solution.py:355
  40.9 11.1 %collective-permute-start.12 = (bf16[8,128,128]{2,1,0:T(8,128)(2,1)S(1)}, bf16[8,128,128]{2,1,0:T(8,128)(2,1)S(1)}, u32[]{:S(2)}, u32[]{:S(2)}) collective-permute-start(bf16[8,128,128]{2,1,0:T(8,128)(2,1)S(1)} %get-tuple-element.45), channel_id=1, source_target_pairs={{0,64},{32,96},{64,0},{96,32},{1,65},{33,97},{65,1},{97,33},{2,66}... | collective-permute-start | bytes 786440 | tf_op jit(solution)/shard_map/ppermute | solution.py:351
  45.5 12.4 %collective-permute-start.13 = (bf16[8,128,128]{2,1,0:T(8,128)(2,1)S(1)}, bf16[8,128,128]{2,1,0:T(8,128)(2,1)S(1)}, u32[]{:S(2)}, u32[]{:S(2)}) collective-permute-start(bf16[8,128,128]{2,1,0:T(8,128)(2,1)S(1)} %get-tuple-element.46), channel_id=1, source_target_pairs={{0,32},{32,64},{64,96},{96,0},{1,33},{33,65},{65,97},{97,1},{2,34}... | collective-permute-start | bytes 786440 | tf_op jit(solution)/shard_map/ppermute | solution.py:351
  45.5 12.4 %collective-permute-start.14 = (bf16[8,128,128]{2,1,0:T(8,128)(2,1)S(1)}, bf16[8,128,128]{2,1,0:T(8,128)(2,1)S(1)}, u32[]{:S(2)}, u32[]{:S(2)}) collective-permute-start(bf16[8,128,128]{2,1,0:T(8,128)(2,1)S(1)} %get-tuple-element.47), channel_id=1, source_target_pairs={{0,96},{32,0},{64,32},{96,64},{1,97},{33,1},{65,33},{97,65},{2,98}... | collective-permute-start | bytes 786440 | tf_op jit(solution)/shard_map/ppermute | solution.py:351
  87.8 8.4 %collective-permute-start.17 = (bf16[8,128,128]{2,1,0:T(8,128)(2,1)S(1)}, bf16[8,128,128]{2,1,0:T(8,128)(2,1)S(1)}, u32[]{:S(2)}, u32[]{:S(2)}) collective-permute-start(bf16[8,128,128]{2,1,0:T(8,128)(2,1)S(1)} %all_to_all.11.refs_0_), channel_id=1, source_target_pairs={{0,64},{32,96},{64,0},{96,32},{1,65},{33,97},{65,1},{97,33},{2,66}... | collective-permute-start | bytes 786440 | tf_op jit(solution)/shard_map/ppermute | solution.py:351
  89.0 11.9 %collective-permute-start.16 = (bf16[8,128,128]{2,1,0:T(8,128)(2,1)S(1)}, bf16[8,128,128]{2,1,0:T(8,128)(2,1)S(1)}, u32[]{:S(2)}, u32[]{:S(2)}) collective-permute-start(bf16[8,128,128]{2,1,0:T(8,128)(2,1)S(1)} %all_to_all.11.refs_0_), channel_id=1, source_target_pairs={{0,96},{32,0},{64,32},{96,64},{1,97},{33,1},{65,33},{97,65},{2,98}... | collective-permute-start | bytes 786440 | tf_op jit(solution)/shard_map/ppermute | solution.py:351
  92.0 11.7 %collective-permute-start.15 = (bf16[8,128,128]{2,1,0:T(8,128)(2,1)S(1)}, bf16[8,128,128]{2,1,0:T(8,128)(2,1)S(1)}, u32[]{:S(2)}, u32[]{:S(2)}) collective-permute-start(bf16[8,128,128]{2,1,0:T(8,128)(2,1)S(1)} %all_to_all.11.refs_0_), channel_id=1, source_target_pairs={{0,32},{32,64},{64,96},{96,0},{1,33},{33,65},{65,97},{97,1},{2,34}... | collective-permute-start | bytes 786440 | tf_op jit(solution)/shard_map/ppermute | solution.py:351
  92.0 12.7 %collective-permute-start.18 = (bf16[8,128,128]{2,1,0:T(8,128)(2,1)S(1)}, bf16[8,128,128]{2,1,0:T(8,128)(2,1)S(1)}, u32[]{:S(2)}, u32[]{:S(2)}) collective-permute-start(bf16[8,128,128]{2,1,0:T(8,128)(2,1)S(1)} %all_to_all.11.refs_0_), channel_id=1, source_target_pairs={{0,128},{128,0},{1,129},{129,1},{2,130},{130,2},{3,131},{131,3},{4... | collective-permute-start | bytes 786440 | tf_op jit(solution)/shard_map/ppermute | solution.py:355
  96.1 8.6 %collective-permute-start.21 = (bf16[8,128,128]{2,1,0:T(8,128)(2,1)S(1)}, bf16[8,128,128]{2,1,0:T(8,128)(2,1)S(1)}, u32[]{:S(2)}, u32[]{:S(2)}) collective-permute-start(bf16[8,128,128]{2,1,0:T(8,128)(2,1)S(1)} %collective-permute-done.17.refs_3_), channel_id=1, source_target_pairs={{0,128},{128,0},{1,129},{129,1},{2,130},{130,2},{3,131},{131,3},{4... | collective-permute-start | bytes 786440 | tf_op jit(solution)/shard_map/ppermute | solution.py:355
  100.9 4.0 %collective-permute-start.20 = (bf16[8,128,128]{2,1,0:T(8,128)(2,1)S(1)}, bf16[8,128,128]{2,1,0:T(8,128)(2,1)S(1)}, u32[]{:S(2)}, u32[]{:S(2)}) collective-permute-start(bf16[8,128,128]{2,1,0:T(8,128)(2,1)S(1)} %collective-permute-done.16.refs_2_), channel_id=1, source_target_pairs={{0,128},{128,0},{1,129},{129,1},{2,130},{130,2},{3,131},{131,3},{4... | collective-permute-start | bytes 786440 | tf_op jit(solution)/shard_map/ppermute | solution.py:355
  107.7 2.6 %collective-permute-start.22 = (bf16[16,128,128]{2,1,0:T(8,128)(2,1)S(1)}, bf16[16,128,128]{2,1,0:T(8,128)(2,1)S(1)}, u32[]{:S(2)}, u32[]{:S(2)}) collective-permute-start(bf16[16,128,128]{2,1,0:T(8,128)(2,1)S(1)} %get-tuple-element.51), channel_id=1, source_target_pairs={{0,128},{128,0},{1,129},{129,1},{2,130},{130,2},{3,131},{131,3},{4... | collective-permute-start | bytes 1572872 | tf_op jit(solution)/shard_map/ppermute | solution.py:355
  111.1 7.2 %collective-permute-start.23 = (bf16[528,128]{1,0:T(8,128)(2,1)S(1)}, bf16[528,128]{1,0:T(8,128)(2,1)S(1)}, u32[]{:S(2)}, u32[]{:S(2)}) collective-permute-start(bf16[528,128]{1,0:T(8,128)(2,1)S(1)} %get-tuple-element.55), channel_id=1, source_target_pairs={{0,2},{1,3},{2,0},{3,1},{4,6},{5,7},{6,4},{7,5},{8,10},{9,11},{10,... | collective-permute-start | bytes 405512 | tf_op jit(solution)/shard_map/ppermute | solution.py:351
  114.3 6.6 %collective-permute-start.24 = (bf16[528,128]{1,0:T(8,128)(2,1)S(1)}, bf16[528,128]{1,0:T(8,128)(2,1)S(1)}, u32[]{:S(2)}, u32[]{:S(2)}) collective-permute-start(bf16[528,128]{1,0:T(8,128)(2,1)S(1)} %get-tuple-element.56), channel_id=1, source_target_pairs={{0,1},{1,2},{2,3},{3,0},{4,5},{5,6},{6,7},{7,4},{8,9},{9,10},{10,1... | collective-permute-start | bytes 405512 | tf_op jit(solution)/shard_map/ppermute | solution.py:351
  115.4 7.0 %collective-permute-start.25 = (bf16[528,128]{1,0:T(8,128)(2,1)S(1)}, bf16[528,128]{1,0:T(8,128)(2,1)S(1)}, u32[]{:S(2)}, u32[]{:S(2)}) collective-permute-start(bf16[528,128]{1,0:T(8,128)(2,1)S(1)} %get-tuple-element.57), channel_id=1, source_target_pairs={{0,3},{1,0},{2,1},{3,2},{4,7},{5,4},{6,5},{7,6},{8,11},{9,8},{10,9... | collective-permute-start | bytes 405512 | tf_op jit(solution)/shard_map/ppermute | solution.py:351
  (4 other events, 20.4 us)

commit v3 on v2

--- a/solution.py
+++ b/solution.py
@@ -107,23 +107,23 @@
     return lax.fori_loop(0, size // SORT_STEP, several, counts)
 
 
-def sort_kernel(rows, cols, count, ids, after, order, numbers):
+def sort_kernel(rows, cols, count, ids, after, order, numbers, *, by_row):
     live = count[0]
-    counts = sort_slots(0, N_SLOTS, rows, cols, live, ids[CORE], order, False, (0, 0))
+    counts = sort_slots(0, N_SLOTS, rows, cols, live, ids[CORE], order, by_row, (0, 0))
     numbers[0] = live - counts[1]
     numbers[1] = counts[1]
 
 
-def sort_by_col(rows, cols, count, ids, after):
+def sort_list(rows, cols, count, ids, after, by_row, name):
     words = lambda k: jax.ShapeDtypeStruct((k,), jnp.int32)
     return pl.pallas_call(
-        sort_kernel,
+        functools.partial(sort_kernel, by_row=by_row),
         in_specs=[SMEM] * 4 + [pl.BlockSpec(memory_space=pl.ANY)],
         out_specs=[SMEM, SMEM],
         out_shape=[words(N_SLOTS), words(2)],
         cost_estimate=pl.CostEstimate(flops=2 * 10**9, bytes_accessed=4096, transcendentals=0),
         compiler_params=PARAMS,
-        name="sort_by_col",
+        name=name,
     )(rows, cols, count, ids, after)
 
 
@@ -141,61 +141,73 @@
             each(per, one)
 
 
-def first_send_kernel(
-    rows_hbm, cols_hbm, count, ids, tiles_hbm, panel_hbm, send, by_row, numbers, tiles, panel, rows, cols, acc, sems
-):
+def accumulate_slots(first, size, dst, src, count, tiles, panel, acc):
+    live = count[0]
+    left = jnp.clip(live - first, 0, size)
+
+    def group(g, carry):
+        for j in range(UNROLL):
+            t = first + g * UNROLL + j
+            d = jnp.where(t < live, dst[t], CTILES)
+            acc[d] += jnp.dot(tiles[t], panel[src[t]], preferred_element_type=F32)
+        return carry
+
+    lax.fori_loop(0, (left + UNROLL - 1) // UNROLL, group, 0)
+
+
+def split(ids, acc, keep, send, half):
+    core = ids[CORE]
+
+    def one(i):
+        keep[i] = acc[core * half + i]
+        send[i] = acc[(1 - core) * half + i].astype(BF16)
+
+    each(half, one)
+
+
+def first_kernel(dst_hbm, src_hbm, count, ids, tiles_hbm, panel_hbm, keep, send, tiles, dst, src, panel, acc, sems):
+    n_blocks = tiles.shape[0] // BLOCK
     lists = [
-        pltpu.make_async_copy(rows_hbm, rows, sems.at[0]),
-        pltpu.make_async_copy(cols_hbm, cols, sems.at[1]),
+        pltpu.make_async_copy(dst_hbm, dst, sems.at[0]),
+        pltpu.make_async_copy(src_hbm, src, sems.at[1]),
+        pltpu.make_async_copy(panel_hbm, panel, sems.at[2]),
     ]
-    start = pltpu.make_async_copy(panel_hbm, panel, sems.at[2])
     blocks = [
         pltpu.make_async_copy(
             tiles_hbm.at[pl.ds(i * BLOCK, BLOCK)], tiles.at[pl.ds(i * BLOCK, BLOCK)], sems.at[3 + i]
         )
-        for i in range(N_SLOTS // BLOCK)
+        for i in range(n_blocks)
     ]
-    for copy in lists + [start] + blocks:
+    for copy in lists + blocks:
         copy.start()
     zero(acc)
     for copy in lists:
         copy.wait()
-    live, core = count[0], ids[CORE]
-    counts, done, last = (0, 0), 0, N_SLOTS // BLOCK - 1
-    for i in range(last + 1):
-        counts = sort_slots(i * BLOCK, BLOCK, rows, cols, live, core, by_row, True, counts)
-        sends = jnp.minimum(live, (i + 1) * BLOCK) - counts[1]
-        if i == 0:
-            start.wait()
+    for i in range(n_blocks):
         blocks[i].wait()
-        until = groups(sends) if i == last else sends // UNROLL
-        accumulate(done, until, sends, by_row, tiles, panel, acc, True, False)
-        done = until
-    numbers[0] = live - counts[1]
-    numbers[1] = counts[1]
-    narrow(acc, send)
+        accumulate_slots(i * BLOCK, BLOCK, dst, src, count, tiles, panel, acc)
+    split(ids, acc, keep, send, CTILES // 2)
 
 
 def in_hbm(value):
     return pltpu.with_memory_space_constraint(value, pltpu.HBM)
 
 
-def first_send(rows, cols, count, ids, tiles, start):
-    n = rows.shape[0]
-    words = lambda k: jax.ShapeDtypeStruct((k,), jnp.int32)
-    return pl.pallas_call(
-        first_send_kernel,
+def first_pass(rows, cols, count, ids, tiles, start):
+    return pl.pallas_call(
+        first_kernel,
         in_specs=[HBM, HBM, SMEM, SMEM, HBM, HBM],
-        out_specs=[VMEM, SMEM, SMEM, VMEM, VMEM],
-        out_shape=[tiles_of(CTILES // 2, BF16), words(n), words(2), tiles_of(n, BF16), tiles_of(DTILES, BF16)],
+        out_specs=[VMEM] * 3,
+        out_shape=[tiles_of(CTILES // 2, F32), tiles_of(CTILES // 2, BF16), tiles_of(tiles.shape[0], BF16)],
         scratch_shapes=[
-            pltpu.SMEM((n,), jnp.int32),
-            pltpu.SMEM((n,), jnp.int32),
-            pltpu.VMEM((CTILES // 2 + 1, TILE, RANK), F32),
-            pltpu.SemaphoreType.DMA((3 + n // BLOCK,)),
+            pltpu.SMEM(rows.shape, jnp.int32),
+            pltpu.SMEM(cols.shape, jnp.int32),
+            pltpu.VMEM(start.shape, BF16),
+            pltpu.VMEM((CTILES + 1, TILE, RANK), F32),
+            pltpu.SemaphoreType.DMA((3 + tiles.shape[0] // BLOCK,)),
         ],
-        compiler_params=PARAMS,
-        name="first_send",
+        compiler_params=pltpu.CompilerParams(vmem_limit_bytes=40 * 2**20),
+        name="first_pass",
     )(*(in_hbm(v) for v in (rows, cols)), count, ids, *(in_hbm(v) for v in (tiles, start)))
 
 
@@ -284,7 +296,7 @@
     each(own.shape[0], one)
 
 
-def row_kernel(own, a, b, c, out):
+def row_kernel(sorted_first, own, a, b, c, out):
     def one(i):
         total = own[i] + a[i].astype(F32) + b[i].astype(F32) + c[i].astype(F32)
         out[i] = total.astype(BF16)
@@ -292,15 +304,15 @@
     each(own.shape[0], one)
 
 
-def four_sum(kernel, own, got, name):
+def four_sum(kernel, sorted_first, own, got, name):
     return pl.pallas_call(
         kernel,
-        in_specs=[VMEM] * 4,
+        in_specs=[SMEM] + [VMEM] * 4,
         out_specs=VMEM,
         out_shape=tiles_of(own.shape[0], BF16),
         compiler_params=PARAMS,
         name=name,
-    )(own, *got)
+    )(sorted_first, own, *got)
 
 
 def share_kernel(got, share, copies):
@@ -373,26 +385,18 @@
     start = start_panel.reshape(DTILES, TILE, RANK)
     quarter = CTILES // 2 // NCOL
 
-    send, by_row, row_numbers, tiles, panel = first_send(rows, cols, count, ids, tiles, start)
-    got = swap(send)
-    [keep] = keep_part(by_row, row_numbers, tiles, panel, True, [], "first_keep")
-    own, *sends = pair_sum(ids, keep, got, COL, NCOL, quarter, "first_pair")
-    by_col, col_numbers = sort_by_col(rows, cols, count, ids, own)
-    part = pl.pallas_call(
-        caller_kernel,
-        in_specs=[SMEM] + [VMEM] * NCOL,
-        out_specs=VMEM,
-        out_shape=tiles_of(quarter, BF16),
-        compiler_params=PARAMS,
-        name="first_sum",
-    )(col_numbers, own, *exchange(sends, "col", NCOL))
+    keep, send, tiles = first_pass(rows, cols, count, ids, tiles, start)
+    own, *sends = pair_sum(ids, keep, swap(send), COL, NCOL, quarter, "first_pair")
+    by_col, col_numbers = sort_list(rows, cols, count, ids, own, False, "sort_by_col")
+    part = four_sum(caller_kernel, col_numbers, own, exchange(sends, "col", NCOL), "first_sum")
     parts = gather(part, "col", NCOL)
 
     send, panel = send_part(by_col, col_numbers, ids, tiles, parts, False, COL, "back_send")
     got = swap(send)
     [keep] = keep_part(by_col, col_numbers, tiles, panel, False, [], "back_keep")
     own, *sends = pair_sum(ids, keep, got, XPOS, NX, NZ, "back_pair")
-    part = four_sum(row_kernel, own, exchange(sends, "x", NX), "back_sum")
+    by_row, row_numbers = sort_list(rows, cols, count, ids, own, True, "sort_by_row")
+    part = four_sum(row_kernel, row_numbers, own, exchange(sends, "x", NX), "back_sum")
     got = lax.all_to_all(part, "z", split_axis=0, concat_axis=0, tiled=True)
     share, copies = pl.pallas_call(
         share_kernel,

time: 124 us -> 123 us (level)
  starting transfers between devices: 49 us -> 41.9 us
  waiting for transfers between devices: 21.1 us -> 26.5 us
    ppermute x15, starting transfers between devices: 26.3 us -> 16 us  [shifted(): return lax.ppermute(value, axis, [(i, (i + k) % n) for i in range(n)])]
    ppermute x15, waiting for transfers between devices: 18.3 us -> 22.3 us  [shifted(): return lax.ppermute(value, axis, [(i, (i + k) % n) for i in range(n)])]
    ppermute x11, starting transfers between devices: 22.7 us -> 25.9 us  [swap(): return lax.ppermute(value, 'layer', [(0, 1), (1, 0)])]
    pallas_call x4 -> x5, Pallas kernels: 9.86 us -> 12.4 us  [the longest x2 6.24 us: sort_list(): pl.pallas_call(functools.partial(sort_kernel, by_row=by_row), in_specs=[S...]
    pallas_call x3 -> x2, Pallas kernels: 5.45 us -> 3.88 us  [keep_part(): pl.pallas_call(functools.partial(keep_kernel, by_row=by_row), in_specs=[S...]
    ppermute x11, waiting for transfers between devices: 2.75 us -> 4.29 us  [swap(): return lax.ppermute(value, 'layer', [(0, 1), (1, 0)])]
  transfers between devices with their start and end apart: 26 -> 26, of which waited for: 12 -> 12; matrix products, arithmetic and copies ran while one was open for 0% -> 0% of each run, Pallas kernels for 7% -> 8%
where the time goes in v3:
time: 123 us; the launch traced here: 122 us
  starting transfers between devices  41.9 us (34%)
  blocking collectives  29.1 us (24%)
  waiting for transfers between devices  26.5 us (22%)
  Pallas kernels  23 us (19%)
  between operations  1.41 us (1%)
    ppermute x11, starting transfers between devices, swap(): return lax.ppermute(value, 'layer', [(0, 1), (1, 0)])  25.9 us
    ppermute x15, waiting for transfers between devices, shifted(): return lax.ppermute(value, axis, [(i, (i + k) % n) for i in range(n)])  22.3 us
    all_to_all x1, blocking collectives, on_device(): got = lax.all_to_all(part, 'z', split_axis=0, concat_axis=0, tiled=True)  17.4 us
    ppermute x15, starting transfers between devices, shifted(): return lax.ppermute(value, axis, [(i, (i + k) % n) for i in range(n)])  16 us
    all_to_all x1, blocking collectives, on_device(): part = lax.all_to_all(copies, 'z', split_axis=0, concat_axis=0, tiled=True)  11.7 us
    pallas_call x2, Pallas kernels, sort_list(): pl.pallas_call(functools.partial(sort_kernel, by_row=by_row), in_specs=[S...  6.24 us
    pallas_call x1, Pallas kernels, first_pass(): pl.pallas_call(first_kernel, in_specs=[HBM, HBM, SMEM, SMEM, HBM, HBM], o...  4.8 us
    ppermute x11, waiting for transfers between devices, swap(): return lax.ppermute(value, 'layer', [(0, 1), (1, 0)])  4.29 us
  transfers between devices with their start and end apart: 26, of which 12 were waited for; matrix products, arithmetic and copies ran while one was open for 0% of the time, Pallas kernels for 8%

profile of v3, /device:TPU:1, one launch (start us, length us, event | category | flops | bytes accessed | tf_op | source)
XLA Modules:
  0.0 122.0 jit_solution(8903139652707973004)
XLA Ops:
  1.4 4.8 %first_pass.1 = (f32[16,128,128]{2,1,0:T(8,128)S(1)}, bf16[16,128,128]{2,1,0:T(8,128)(2,1)S(1)}, bf16[256,128,128]{2,1,0:T(8,128)(2,1)S(1)}) custom-call(s32[256]{0:T(256)} %bitcast.13, s32[256]{0:T(256)} %bitcast.16, s32[1]{0:T(128)} %bitcast.10.count, s32[3]{0:T(128)S(1)} %pad_add_fusion.ids, bf16[256,128,128]{2,1,0:T(8,128)(2,1)} %bitcast.19, ...), custom_call_target="tpu_custom_call" | custom-call | tf_op jit(solution)/shard_map/first_pass/pallas_call | solution.py:197
  6.2 5.5 %collective-permute-start = (bf16[16,128,128]{2,1,0:T(8,128)(2,1)S(1)}, bf16[16,128,128]{2,1,0:T(8,128)(2,1)S(1)}, u32[]{:S(2)}, u32[]{:S(2)}) collective-permute-start(bf16[16,128,128]{2,1,0:T(8,128)(2,1)S(1)} %get-tuple-element.32), channel_id=1, source_target_pairs={{0,128},{128,0},{1,129},{129,1},{2,130},{130,2},{3,131},{131,3},{4... | collective-permute-start | bytes 1572872 | tf_op jit(solution)/shard_map/ppermute | solution.py:367
  14.3 2.7 %collective-permute-start.3 = (bf16[4,128,128]{2,1,0:T(8,128)(2,1)S(1)}, bf16[4,128,128]{2,1,0:T(8,128)(2,1)S(1)}, u32[]{:S(2)}, u32[]{:S(2)}) collective-permute-start(bf16[4,128,128]{2,1,0:T(8,128)(2,1)S(1)} %get-tuple-element.39), channel_id=1, source_target_pairs={{0,3},{1,0},{2,1},{3,2},{4,7},{5,4},{6,5},{7,6},{8,11},{9,8},{10,9... | collective-permute-start | bytes 393224 | tf_op jit(solution)/shard_map/ppermute | solution.py:363
  17.0 3.1 %sort_by_col.1 = (s32[256]{0:T(256)S(1)}, s32[2]{0:T(128)S(1)}) custom-call(s32[256]{0:T(256)S(1)} %bitcast.14, s32[256]{0:T(256)S(1)} %bitcast.17, s32[1]{0:T(128)} %bitcast.11.count, s32[3]{0:T(128)S(1)} %pad_add_fusion.ids, f32[4,128,128]{2,1,0:T(8,128)S(1)} %get-tuple-element.33.after.own), custom_call_target="tpu_custom_call" | custom-call | flops 2000000000 | bytes 4096 | tf_op jit(solution)/shard_map/sort_by_col/pallas_call | solution.py:119
  20.2 3.5 %collective-permute-done.2.b = bf16[4,128,128]{2,1,0:T(8,128)(2,1)S(1)} collective-permute-done((bf16[4,128,128]{2,1,0:T(8,128)(2,1)S(1)}, bf16[4,128,128]{2,1,0:T(8,128)(2,1)S(1)}, u32[]{:S(2)}, u32[]{:S(2)}) %collective-permute-start.2) | collective-permute-done | bytes 131104 | tf_op jit(solution)/shard_map/ppermute | solution.py:363
  27.6 2.9 %collective-permute-done.6.refs_3_ = bf16[4,128,128]{2,1,0:T(8,128)(2,1)S(1)} collective-permute-done((bf16[4,128,128]{2,1,0:T(8,128)(2,1)S(1)}, bf16[4,128,128]{2,1,0:T(8,128)(2,1)S(1)}, u32[]{:S(2)}, u32[]{:S(2)}) %collective-permute-start.6) | collective-permute-done | bytes 131104 | tf_op jit(solution)/shard_map/ppermute | solution.py:363
  30.6 2.3 %collective-permute-start.10 = (bf16[4,128,128]{2,1,0:T(8,128)(2,1)S(1)}, bf16[4,128,128]{2,1,0:T(8,128)(2,1)S(1)}, u32[]{:S(2)}, u32[]{:S(2)}) collective-permute-start(bf16[4,128,128]{2,1,0:T(8,128)(2,1)S(1)} %collective-permute-done.6.refs_3_), channel_id=1, source_target_pairs={{0,128},{128,0},{1,129},{129,1},{2,130},{130,2},{3,131},{131,3},{4... | collective-permute-start | bytes 393224 | tf_op jit(solution)/shard_map/ppermute | solution.py:367
  35.7 1.9 %back_send.1 = (bf16[32,128,128]{2,1,0:T(8,128)(2,1)S(1)}, bf16[32,128,128]{2,1,0:T(8,128)(2,1)S(1)}) custom-call(s32[256]{0:T(256)S(1)} %get-tuple-element.34.order, s32[2]{0:T(128)S(1)} %get-tuple-element.35.sorted_first.numbers, s32[3]{0:T(128)S(1)} %pad_add_fusion.ids, bf16[256,128,128]{2,1,0:T(8,128)(2,1)S(1)} %get-tuple-element.36.tiles, ...), custom_call_target="tpu_custom_call" | custom-call | tf_op jit(solution)/shard_map/back_send/pallas_call | solution.py:227
  37.6 1.9 %collective-permute-start.11 = (bf16[32,128,128]{2,1,0:T(8,128)(2,1)S(1)}, bf16[32,128,128]{2,1,0:T(8,128)(2,1)S(1)}, u32[]{:S(2)}, u32[]{:S(2)}) collective-permute-start(bf16[32,128,128]{2,1,0:T(8,128)(2,1)S(1)} %get-tuple-element.41), channel_id=1, source_target_pairs={{0,128},{128,0},{1,129},{129,1},{2,130},{130,2},{3,131},{131,3},{4... | collective-permute-start | bytes 3145736 | tf_op jit(solution)/shard_map/ppermute | solution.py:367
  43.6 2.7 %collective-permute-start.14 = (bf16[8,128,128]{2,1,0:T(8,128)(2,1)S(1)}, bf16[8,128,128]{2,1,0:T(8,128)(2,1)S(1)}, u32[]{:S(2)}, u32[]{:S(2)}) collective-permute-start(bf16[8,128,128]{2,1,0:T(8,128)(2,1)S(1)} %get-tuple-element.47), channel_id=1, source_target_pairs={{0,96},{32,0},{64,32},{96,64},{1,97},{33,1},{65,33},{97,65},{2,98}... | collective-permute-start | bytes 786440 | tf_op jit(solution)/shard_map/ppermute | solution.py:363
  46.2 3.1 %sort_by_row.1 = (s32[256]{0:T(256)S(1)}, s32[2]{0:T(128)S(1)}) custom-call(s32[256]{0:T(256)S(1)} %bitcast.15, s32[256]{0:T(256)S(1)} %bitcast.18, s32[1]{0:T(128)} %bitcast.12.count, s32[3]{0:T(128)S(1)} %pad_add_fusion.ids, f32[8,128,128]{2,1,0:T(8,128)S(1)} %get-tuple-element.42.after.own), custom_call_target="tpu_custom_call" | custom-call | flops 2000000000 | bytes 4096 | tf_op jit(solution)/shard_map/sort_by_row/pallas_call | solution.py:119
  49.3 2.4 %collective-permute-done.12.a = bf16[8,128,128]{2,1,0:T(8,128)(2,1)S(1)} collective-permute-done((bf16[8,128,128]{2,1,0:T(8,128)(2,1)S(1)}, bf16[8,128,128]{2,1,0:T(8,128)(2,1)S(1)}, u32[]{:S(2)}, u32[]{:S(2)}) %collective-permute-start.12) | collective-permute-done | bytes 262176 | tf_op jit(solution)/shard_map/ppermute | solution.py:363
  51.7 6.3 %collective-permute-done.13.b = bf16[8,128,128]{2,1,0:T(8,128)(2,1)S(1)} collective-permute-done((bf16[8,128,128]{2,1,0:T(8,128)(2,1)S(1)}, bf16[8,128,128]{2,1,0:T(8,128)(2,1)S(1)}, u32[]{:S(2)}, u32[]{:S(2)}) %collective-permute-start.13) | collective-permute-done | bytes 262176 | tf_op jit(solution)/shard_map/ppermute | solution.py:363
  58.7 17.4 %all_to_all.10.got = bf16[8,128,128]{2,1,0:T(8,128)(2,1)S(1)} all-to-all(bf16[8,128,128]{2,1,0:T(8,128)(2,1)S(1)} %back_sum.1), channel_id=1, replica_groups=mesh['layer'=2,'x'=4,'z'=8,'col'=4] {'z'}, dimensions={0} | all-to-all | bytes 524288 | tf_op jit(solution)/shard_map/all_to_all | solution.py:400
  76.2 11.7 %all_to_all.11.refs_0_ = bf16[8,128,128]{2,1,0:T(8,128)(2,1)S(1)} all-to-all(bf16[8,128,128]{2,1,0:T(8,128)(2,1)S(1)} %get-tuple-element.48), channel_id=1, replica_groups=mesh['layer'=2,'x'=4,'z'=8,'col'=4] {'z'}, dimensions={0} | all-to-all | bytes 524288 | tf_op jit(solution)/shard_map/all_to_all | solution.py:409
  87.9 1.9 %collective-permute-start.17 = (bf16[8,128,128]{2,1,0:T(8,128)(2,1)S(1)}, bf16[8,128,128]{2,1,0:T(8,128)(2,1)S(1)}, u32[]{:S(2)}, u32[]{:S(2)}) collective-permute-start(bf16[8,128,128]{2,1,0:T(8,128)(2,1)S(1)} %all_to_all.11.refs_0_), channel_id=1, source_target_pairs={{0,64},{32,96},{64,0},{96,32},{1,65},{33,97},{65,1},{97,33},{2,66}... | collective-permute-start | bytes 786440 | tf_op jit(solution)/shard_map/ppermute | solution.py:363
  91.5 4.2 %collective-permute-start.18 = (bf16[8,128,128]{2,1,0:T(8,128)(2,1)S(1)}, bf16[8,128,128]{2,1,0:T(8,128)(2,1)S(1)}, u32[]{:S(2)}, u32[]{:S(2)}) collective-permute-start(bf16[8,128,128]{2,1,0:T(8,128)(2,1)S(1)} %all_to_all.11.refs_0_), channel_id=1, source_target_pairs={{0,128},{128,0},{1,129},{129,1},{2,130},{130,2},{3,131},{131,3},{4... | collective-permute-start | bytes 786440 | tf_op jit(solution)/shard_map/ppermute | solution.py:367
  95.7 5.4 %collective-permute-start.21 = (bf16[8,128,128]{2,1,0:T(8,128)(2,1)S(1)}, bf16[8,128,128]{2,1,0:T(8,128)(2,1)S(1)}, u32[]{:S(2)}, u32[]{:S(2)}) collective-permute-start(bf16[8,128,128]{2,1,0:T(8,128)(2,1)S(1)} %collective-permute-done.17.refs_3_), channel_id=1, source_target_pairs={{0,128},{128,0},{1,129},{129,1},{2,130},{130,2},{3,131},{131,3},{4... | collective-permute-start | bytes 786440 | tf_op jit(solution)/shard_map/ppermute | solution.py:367
  101.0 1.9 %collective-permute-start.20 = (bf16[8,128,128]{2,1,0:T(8,128)(2,1)S(1)}, bf16[8,128,128]{2,1,0:T(8,128)(2,1)S(1)}, u32[]{:S(2)}, u32[]{:S(2)}) collective-permute-start(bf16[8,128,128]{2,1,0:T(8,128)(2,1)S(1)} %collective-permute-done.16.refs_2_), channel_id=1, source_target_pairs={{0,128},{128,0},{1,129},{129,1},{2,130},{130,2},{3,131},{131,3},{4... | collective-permute-start | bytes 786440 | tf_op jit(solution)/shard_map/ppermute | solution.py:367
  105.4 1.9 %last_send.1 = (bf16[16,128,128]{2,1,0:T(8,128)(2,1)S(1)}, bf16[64,128,128]{2,1,0:T(8,128)(2,1)S(1)}) custom-call(s32[256]{0:T(256)S(1)} %get-tuple-element.43.order, s32[2]{0:T(128)S(1)} %get-tuple-element.44.sorted_first.numbers, s32[3]{0:T(128)S(1)} %pad_add_fusion.ids, bf16[256,128,128]{2,1,0:T(8,128)(2,1)S(1)} %get-tuple-element.36.tiles, ...), custom_call_target="tpu_custom_call" | custom-call | tf_op jit(solution)/shard_map/last_send/pallas_call | solution.py:227
  108.8 2.2 %last_keep.1 = (f32[17,128,128]{2,1,0:T(8,128)S(1)}, f32[32,128]{1,0:T(8,128)S(1)}) custom-call(s32[256]{0:T(256)S(1)} %get-tuple-element.43.order, s32[2]{0:T(128)S(1)} %get-tuple-element.44.sorted_first.numbers, bf16[256,128,128]{2,1,0:T(8,128)(2,1)S(1)} %get-tuple-element.36.tiles, bf16[64,128,128]{2,1,0:T(8,128)(2,1)S(1)} %get-tuple-element.49.panel), custom_call_target="tpu_custom_call" | custom-call | flops 1073741824 | bytes 10485760 | tf_op jit(solution)/shard_map/last_keep/pallas_call | solution.py:254
  113.4 2.0 %collective-permute-start.25 = (bf16[528,128]{1,0:T(8,128)(2,1)S(1)}, bf16[528,128]{1,0:T(8,128)(2,1)S(1)}, u32[]{:S(2)}, u32[]{:S(2)}) collective-permute-start(bf16[528,128]{1,0:T(8,128)(2,1)S(1)} %get-tuple-element.57), channel_id=1, source_target_pairs={{0,3},{1,0},{2,1},{3,2},{4,7},{5,4},{6,5},{7,6},{8,11},{9,8},{10,9... | collective-permute-start | bytes 405512 | tf_op jit(solution)/shard_map/ppermute | solution.py:363
  115.4 1.8 %collective-permute-done.23.a = bf16[528,128]{1,0:T(8,128)(2,1)S(1)} collective-permute-done((bf16[528,128]{1,0:T(8,128)(2,1)S(1)}, bf16[528,128]{1,0:T(8,128)(2,1)S(1)}, u32[]{:S(2)}, u32[]{:S(2)}) %collective-permute-start.23) | collective-permute-done | bytes 135200 | tf_op jit(solution)/shard_map/ppermute | solution.py:363
  117.2 4.1 %collective-permute-done.24.b = bf16[528,128]{1,0:T(8,128)(2,1)S(1)} collective-permute-done((bf16[528,128]{1,0:T(8,128)(2,1)S(1)}, bf16[528,128]{1,0:T(8,128)(2,1)S(1)}, u32[]{:S(2)}, u32[]{:S(2)}) %collective-permute-start.24) | collective-permute-done | bytes 135200 | tf_op jit(solution)/shard_map/ppermute | solution.py:363
  (49 shorter events, 23.2 us)
Async XLA Ops:
  6.2 7.1 %collective-permute-start = (bf16[16,128,128]{2,1,0:T(8,128)(2,1)S(1)}, bf16[16,128,128]{2,1,0:T(8,128)(2,1)S(1)}, u32[]{:S(2)}, u32[]{:S(2)}) collective-permute-start(bf16[16,128,128]{2,1,0:T(8,128)(2,1)S(1)} %get-tuple-element.32), channel_id=1, source_target_pairs={{0,128},{128,0},{1,129},{129,1},{2,130},{130,2},{3,131},{131,3},{4... | collective-permute-start | bytes 1572872 | tf_op jit(solution)/shard_map/ppermute | solution.py:367
  13.9 6.3 %collective-permute-start.1 = (bf16[4,128,128]{2,1,0:T(8,128)(2,1)S(1)}, bf16[4,128,128]{2,1,0:T(8,128)(2,1)S(1)}, u32[]{:S(2)}, u32[]{:S(2)}) collective-permute-start(bf16[4,128,128]{2,1,0:T(8,128)(2,1)S(1)} %get-tuple-element.37), channel_id=1, source_target_pairs={{0,2},{1,3},{2,0},{3,1},{4,6},{5,7},{6,4},{7,5},{8,10},{9,11},{10,... | collective-permute-start | bytes 393224 | tf_op jit(solution)/shard_map/ppermute | solution.py:363
  14.3 9.4 %collective-permute-start.2 = (bf16[4,128,128]{2,1,0:T(8,128)(2,1)S(1)}, bf16[4,128,128]{2,1,0:T(8,128)(2,1)S(1)}, u32[]{:S(2)}, u32[]{:S(2)}) collective-permute-start(bf16[4,128,128]{2,1,0:T(8,128)(2,1)S(1)} %get-tuple-element.38), channel_id=1, source_target_pairs={{0,1},{1,2},{2,3},{3,0},{4,5},{5,6},{6,7},{7,4},{8,9},{9,10},{10,1... | collective-permute-start | bytes 393224 | tf_op jit(solution)/shard_map/ppermute | solution.py:363
  14.3 9.4 %collective-permute-start.3 = (bf16[4,128,128]{2,1,0:T(8,128)(2,1)S(1)}, bf16[4,128,128]{2,1,0:T(8,128)(2,1)S(1)}, u32[]{:S(2)}, u32[]{:S(2)}) collective-permute-start(bf16[4,128,128]{2,1,0:T(8,128)(2,1)S(1)} %get-tuple-element.39), channel_id=1, source_target_pairs={{0,3},{1,0},{2,1},{3,2},{4,7},{5,4},{6,5},{7,6},{8,11},{9,8},{10,9... | collective-permute-start | bytes 393224 | tf_op jit(solution)/shard_map/ppermute | solution.py:363
  24.4 6.2 %collective-permute-start.6 = (bf16[4,128,128]{2,1,0:T(8,128)(2,1)S(1)}, bf16[4,128,128]{2,1,0:T(8,128)(2,1)S(1)}, u32[]{:S(2)}, u32[]{:S(2)}) collective-permute-start(bf16[4,128,128]{2,1,0:T(8,128)(2,1)S(1)} %first_sum.1.refs_0_), channel_id=1, source_target_pairs={{0,2},{1,3},{2,0},{3,1},{4,6},{5,7},{6,4},{7,5},{8,10},{9,11},{10,... | collective-permute-start | bytes 393224 | tf_op jit(solution)/shard_map/ppermute | solution.py:363
  24.8 8.0 %collective-permute-start.5 = (bf16[4,128,128]{2,1,0:T(8,128)(2,1)S(1)}, bf16[4,128,128]{2,1,0:T(8,128)(2,1)S(1)}, u32[]{:S(2)}, u32[]{:S(2)}) collective-permute-start(bf16[4,128,128]{2,1,0:T(8,128)(2,1)S(1)} %first_sum.1.refs_0_), channel_id=1, source_target_pairs={{0,3},{1,0},{2,1},{3,2},{4,7},{5,4},{6,5},{7,6},{8,11},{9,8},{10,9... | collective-permute-start | bytes 393224 | tf_op jit(solution)/shard_map/ppermute | solution.py:363
  25.3 8.8 %collective-permute-start.4 = (bf16[4,128,128]{2,1,0:T(8,128)(2,1)S(1)}, bf16[4,128,128]{2,1,0:T(8,128)(2,1)S(1)}, u32[]{:S(2)}, u32[]{:S(2)}) collective-permute-start(bf16[4,128,128]{2,1,0:T(8,128)(2,1)S(1)} %first_sum.1.refs_0_), channel_id=1, source_target_pairs={{0,1},{1,2},{2,3},{3,0},{4,5},{5,6},{6,7},{7,4},{8,9},{9,10},{10,1... | collective-permute-start | bytes 393224 | tf_op jit(solution)/shard_map/ppermute | solution.py:363
  26.3 8.4 %collective-permute-start.7 = (bf16[4,128,128]{2,1,0:T(8,128)(2,1)S(1)}, bf16[4,128,128]{2,1,0:T(8,128)(2,1)S(1)}, u32[]{:S(2)}, u32[]{:S(2)}) collective-permute-start(bf16[4,128,128]{2,1,0:T(8,128)(2,1)S(1)} %first_sum.1.refs_0_), channel_id=1, source_target_pairs={{0,128},{128,0},{1,129},{129,1},{2,130},{130,2},{3,131},{131,3},{4... | collective-permute-start | bytes 393224 | tf_op jit(solution)/shard_map/ppermute | solution.py:367
  30.6 4.1 %collective-permute-start.10 = (bf16[4,128,128]{2,1,0:T(8,128)(2,1)S(1)}, bf16[4,128,128]{2,1,0:T(8,128)(2,1)S(1)}, u32[]{:S(2)}, u32[]{:S(2)}) collective-permute-start(bf16[4,128,128]{2,1,0:T(8,128)(2,1)S(1)} %collective-permute-done.6.refs_3_), channel_id=1, source_target_pairs={{0,128},{128,0},{1,129},{129,1},{2,130},{130,2},{3,131},{131,3},{4... | collective-permute-start | bytes 393224 | tf_op jit(solution)/shard_map/ppermute | solution.py:367
  37.6 4.2 %collective-permute-start.11 = (bf16[32,128,128]{2,1,0:T(8,128)(2,1)S(1)}, bf16[32,128,128]{2,1,0:T(8,128)(2,1)S(1)}, u32[]{:S(2)}, u32[]{:S(2)}) collective-permute-start(bf16[32,128,128]{2,1,0:T(8,128)(2,1)S(1)} %get-tuple-element.41), channel_id=1, source_target_pairs={{0,128},{128,0},{1,129},{129,1},{2,130},{130,2},{3,131},{131,3},{4... | collective-permute-start | bytes 3145736 | tf_op jit(solution)/shard_map/ppermute | solution.py:367
  42.6 9.1 %collective-permute-start.12 = (bf16[8,128,128]{2,1,0:T(8,128)(2,1)S(1)}, bf16[8,128,128]{2,1,0:T(8,128)(2,1)S(1)}, u32[]{:S(2)}, u32[]{:S(2)}) collective-permute-start(bf16[8,128,128]{2,1,0:T(8,128)(2,1)S(1)} %get-tuple-element.45), channel_id=1, source_target_pairs={{0,64},{32,96},{64,0},{96,32},{1,65},{33,97},{65,1},{97,33},{2,66}... | collective-permute-start | bytes 786440 | tf_op jit(solution)/shard_map/ppermute | solution.py:363
  43.5 14.5 %collective-permute-start.13 = (bf16[8,128,128]{2,1,0:T(8,128)(2,1)S(1)}, bf16[8,128,128]{2,1,0:T(8,128)(2,1)S(1)}, u32[]{:S(2)}, u32[]{:S(2)}) collective-permute-start(bf16[8,128,128]{2,1,0:T(8,128)(2,1)S(1)} %get-tuple-element.46), channel_id=1, source_target_pairs={{0,32},{32,64},{64,96},{96,0},{1,33},{33,65},{65,97},{97,1},{2,34}... | collective-permute-start | bytes 786440 | tf_op jit(solution)/shard_map/ppermute | solution.py:363
  43.6 14.5 %collective-permute-start.14 = (bf16[8,128,128]{2,1,0:T(8,128)(2,1)S(1)}, bf16[8,128,128]{2,1,0:T(8,128)(2,1)S(1)}, u32[]{:S(2)}, u32[]{:S(2)}) collective-permute-start(bf16[8,128,128]{2,1,0:T(8,128)(2,1)S(1)} %get-tuple-element.47), channel_id=1, source_target_pairs={{0,96},{32,0},{64,32},{96,64},{1,97},{33,1},{65,33},{97,65},{2,98}... | collective-permute-start | bytes 786440 | tf_op jit(solution)/shard_map/ppermute | solution.py:363
  87.9 7.8 %collective-permute-start.17 = (bf16[8,128,128]{2,1,0:T(8,128)(2,1)S(1)}, bf16[8,128,128]{2,1,0:T(8,128)(2,1)S(1)}, u32[]{:S(2)}, u32[]{:S(2)}) collective-permute-start(bf16[8,128,128]{2,1,0:T(8,128)(2,1)S(1)} %all_to_all.11.refs_0_), channel_id=1, source_target_pairs={{0,64},{32,96},{64,0},{96,32},{1,65},{33,97},{65,1},{97,33},{2,66}... | collective-permute-start | bytes 786440 | tf_op jit(solution)/shard_map/ppermute | solution.py:363
  89.8 11.3 %collective-permute-start.16 = (bf16[8,128,128]{2,1,0:T(8,128)(2,1)S(1)}, bf16[8,128,128]{2,1,0:T(8,128)(2,1)S(1)}, u32[]{:S(2)}, u32[]{:S(2)}) collective-permute-start(bf16[8,128,128]{2,1,0:T(8,128)(2,1)S(1)} %all_to_all.11.refs_0_), channel_id=1, source_target_pairs={{0,96},{32,0},{64,32},{96,64},{1,97},{33,1},{65,33},{97,65},{2,98}... | collective-permute-start | bytes 786440 | tf_op jit(solution)/shard_map/ppermute | solution.py:363
  91.5 11.4 %collective-permute-start.15 = (bf16[8,128,128]{2,1,0:T(8,128)(2,1)S(1)}, bf16[8,128,128]{2,1,0:T(8,128)(2,1)S(1)}, u32[]{:S(2)}, u32[]{:S(2)}) collective-permute-start(bf16[8,128,128]{2,1,0:T(8,128)(2,1)S(1)} %all_to_all.11.refs_0_), channel_id=1, source_target_pairs={{0,32},{32,64},{64,96},{96,0},{1,33},{33,65},{65,97},{97,1},{2,34}... | collective-permute-start | bytes 786440 | tf_op jit(solution)/shard_map/ppermute | solution.py:363
  91.5 12.7 %collective-permute-start.18 = (bf16[8,128,128]{2,1,0:T(8,128)(2,1)S(1)}, bf16[8,128,128]{2,1,0:T(8,128)(2,1)S(1)}, u32[]{:S(2)}, u32[]{:S(2)}) collective-permute-start(bf16[8,128,128]{2,1,0:T(8,128)(2,1)S(1)} %all_to_all.11.refs_0_), channel_id=1, source_target_pairs={{0,128},{128,0},{1,129},{129,1},{2,130},{130,2},{3,131},{131,3},{4... | collective-permute-start | bytes 786440 | tf_op jit(solution)/shard_map/ppermute | solution.py:367
  95.7 8.6 %collective-permute-start.21 = (bf16[8,128,128]{2,1,0:T(8,128)(2,1)S(1)}, bf16[8,128,128]{2,1,0:T(8,128)(2,1)S(1)}, u32[]{:S(2)}, u32[]{:S(2)}) collective-permute-start(bf16[8,128,128]{2,1,0:T(8,128)(2,1)S(1)} %collective-permute-done.17.refs_3_), channel_id=1, source_target_pairs={{0,128},{128,0},{1,129},{129,1},{2,130},{130,2},{3,131},{131,3},{4... | collective-permute-start | bytes 786440 | tf_op jit(solution)/shard_map/ppermute | solution.py:367
  101.0 3.2 %collective-permute-start.20 = (bf16[8,128,128]{2,1,0:T(8,128)(2,1)S(1)}, bf16[8,128,128]{2,1,0:T(8,128)(2,1)S(1)}, u32[]{:S(2)}, u32[]{:S(2)}) collective-permute-start(bf16[8,128,128]{2,1,0:T(8,128)(2,1)S(1)} %collective-permute-done.16.refs_2_), channel_id=1, source_target_pairs={{0,128},{128,0},{1,129},{129,1},{2,130},{130,2},{3,131},{131,3},{4... | collective-permute-start | bytes 786440 | tf_op jit(solution)/shard_map/ppermute | solution.py:367
  103.0 2.5 %collective-permute-start.19 = (bf16[8,128,128]{2,1,0:T(8,128)(2,1)S(1)}, bf16[8,128,128]{2,1,0:T(8,128)(2,1)S(1)}, u32[]{:S(2)}, u32[]{:S(2)}) collective-permute-start(bf16[8,128,128]{2,1,0:T(8,128)(2,1)S(1)} %collective-permute-done.15.refs_1_), channel_id=1, source_target_pairs={{0,128},{128,0},{1,129},{129,1},{2,130},{130,2},{3,131},{131,3},{4... | collective-permute-start | bytes 786440 | tf_op jit(solution)/shard_map/ppermute | solution.py:367
  107.3 3.7 %collective-permute-start.22 = (bf16[16,128,128]{2,1,0:T(8,128)(2,1)S(1)}, bf16[16,128,128]{2,1,0:T(8,128)(2,1)S(1)}, u32[]{:S(2)}, u32[]{:S(2)}) collective-permute-start(bf16[16,128,128]{2,1,0:T(8,128)(2,1)S(1)} %get-tuple-element.51), channel_id=1, source_target_pairs={{0,128},{128,0},{1,129},{129,1},{2,130},{130,2},{3,131},{131,3},{4... | collective-permute-start | bytes 1572872 | tf_op jit(solution)/shard_map/ppermute | solution.py:367
  111.6 5.5 %collective-permute-start.23 = (bf16[528,128]{1,0:T(8,128)(2,1)S(1)}, bf16[528,128]{1,0:T(8,128)(2,1)S(1)}, u32[]{:S(2)}, u32[]{:S(2)}) collective-permute-start(bf16[528,128]{1,0:T(8,128)(2,1)S(1)} %get-tuple-element.55), channel_id=1, source_target_pairs={{0,2},{1,3},{2,0},{3,1},{4,6},{5,7},{6,4},{7,5},{8,10},{9,11},{10,... | collective-permute-start | bytes 405512 | tf_op jit(solution)/shard_map/ppermute | solution.py:363
  112.7 8.6 %collective-permute-start.24 = (bf16[528,128]{1,0:T(8,128)(2,1)S(1)}, bf16[528,128]{1,0:T(8,128)(2,1)S(1)}, u32[]{:S(2)}, u32[]{:S(2)}) collective-permute-start(bf16[528,128]{1,0:T(8,128)(2,1)S(1)} %get-tuple-element.56), channel_id=1, source_target_pairs={{0,1},{1,2},{2,3},{3,0},{4,5},{5,6},{6,7},{7,4},{8,9},{9,10},{10,1... | collective-permute-start | bytes 405512 | tf_op jit(solution)/shard_map/ppermute | solution.py:363
  113.4 7.9 %collective-permute-start.25 = (bf16[528,128]{1,0:T(8,128)(2,1)S(1)}, bf16[528,128]{1,0:T(8,128)(2,1)S(1)}, u32[]{:S(2)}, u32[]{:S(2)}) collective-permute-start(bf16[528,128]{1,0:T(8,128)(2,1)S(1)} %get-tuple-element.57), channel_id=1, source_target_pairs={{0,3},{1,0},{2,1},{3,2},{4,7},{5,4},{6,5},{7,6},{8,11},{9,8},{10,9... | collective-permute-start | bytes 405512 | tf_op jit(solution)/shard_map/ppermute | solution.py:363
  (4 other events, 34.9 us)

commit v4 on v3

--- a/solution.py
+++ b/solution.py
@@ -18,7 +18,7 @@
 NDST = 32768
 N_SLOTS = 256
 SLOT_BITS, ROW_BITS, COL_BITS = 8, 5, 6
-BLOCK = 64
+BLOCK = 32
 UNROLL = 32
 STEPS = 4
 SORT_STEP = 16
@@ -33,6 +33,7 @@
 SMEM = pl.BlockSpec(memory_space=pltpu.SMEM)
 VMEM = pl.BlockSpec(memory_space=pltpu.VMEM)
 HBM = pl.BlockSpec(memory_space=pltpu.HBM)
+ANY = pl.BlockSpec(memory_space=pl.ANY)
 PARAMS = pltpu.CompilerParams(vmem_limit_bytes=40 * 2**20)
 
 
@@ -118,7 +119,7 @@
     words = lambda k: jax.ShapeDtypeStruct((k,), jnp.int32)
     return pl.pallas_call(
         functools.partial(sort_kernel, by_row=by_row),
-        in_specs=[SMEM] * 4 + [pl.BlockSpec(memory_space=pl.ANY)],
+        in_specs=[SMEM] * 4 + [ANY],
         out_specs=[SMEM, SMEM],
         out_shape=[words(N_SLOTS), words(2)],
         cost_estimate=pl.CostEstimate(flops=2 * 10**9, bytes_accessed=4096, transcendentals=0),
@@ -307,7 +308,7 @@
 def four_sum(kernel, sorted_first, own, got, name):
     return pl.pallas_call(
         kernel,
-        in_specs=[SMEM] + [VMEM] * 4,
+        in_specs=[ANY] + [VMEM] * 4,
         out_specs=VMEM,
         out_shape=tiles_of(own.shape[0], BF16),
         compiler_params=PARAMS,

time: 123 us -> 121 us (0.984); the launches traced: 122 us -> 122 us
  Pallas kernels: 23 us -> 24.8 us
  waiting for transfers between devices: 26.5 us -> 24.7 us
    ppermute x11, starting transfers between devices: 25.9 us -> 24.1 us  [swap(): return lax.ppermute(value, 'layer', [(0, 1), (1, 0)])]
    ppermute x15, waiting for transfers between devices: 22.3 us -> 20.9 us  [shifted(): return lax.ppermute(value, axis, [(i, (i + k) % n) for i in range(n)])]
  transfers between devices with their start and end apart: 26 -> 26, of which waited for: 12 -> 12; matrix products, arithmetic and copies ran while one was open for 0% -> 0% of each run, Pallas kernels for 8% -> 9%
where the time goes in v4:
time: 121 us; the launch traced here: 122 us
  starting transfers between devices  40.7 us (34%)
  blocking collectives  30.2 us (25%)
  Pallas kernels  24.8 us (20%)
  waiting for transfers between devices  24.7 us (20%)
  between operations  1.42 us (1%)
    ppermute x11, starting transfers between devices, swap(): return lax.ppermute(value, 'layer', [(0, 1), (1, 0)])  24.1 us
    ppermute x15, waiting for transfers between devices, shifted(): return lax.ppermute(value, axis, [(i, (i + k) % n) for i in range(n)])  20.9 us
    all_to_all x1, blocking collectives, on_device(): got = lax.all_to_all(part, 'z', split_axis=0, concat_axis=0, tiled=True)  18.6 us
    ppermute x15, starting transfers between devices, shifted(): return lax.ppermute(value, axis, [(i, (i + k) % n) for i in range(n)])  16.7 us
    all_to_all x1, blocking collectives, on_device(): part = lax.all_to_all(copies, 'z', split_axis=0, concat_axis=0, tiled=True)  11.7 us
    pallas_call x2, Pallas kernels, sort_list(): pl.pallas_call(functools.partial(sort_kernel, by_row=by_row), in_specs=[S...  6.24 us
    pallas_call x1, Pallas kernels, first_pass(): pl.pallas_call(first_kernel, in_specs=[HBM, HBM, SMEM, SMEM, HBM, HBM], o...  5.74 us
    pallas_call x2, Pallas kernels, keep_part(): pl.pallas_call(functools.partial(keep_kernel, by_row=by_row), in_specs=[S...  4.86 us
  transfers between devices with their start and end apart: 26, of which 12 were waited for; matrix products, arithmetic and copies ran while one was open for 0% of the time, Pallas kernels for 9%

profile of v4, /device:TPU:1, one launch (start us, length us, event | category | flops | bytes accessed | tf_op | source)
XLA Modules:
  0.0 121.9 jit_solution(6593263312042625607)
XLA Ops:
  1.4 5.7 %first_pass.1 = (f32[16,128,128]{2,1,0:T(8,128)S(1)}, bf16[16,128,128]{2,1,0:T(8,128)(2,1)S(1)}, bf16[256,128,128]{2,1,0:T(8,128)(2,1)S(1)}) custom-call(s32[256]{0:T(256)} %bitcast.13, s32[256]{0:T(256)} %bitcast.16, s32[1]{0:T(128)} %bitcast.10.count, s32[3]{0:T(128)S(1)} %pad_add_fusion.ids, bf16[256,128,128]{2,1,0:T(8,128)(2,1)} %bitcast.19, ...), custom_call_target="tpu_custom_call" | custom-call | tf_op jit(solution)/shard_map/first_pass/pallas_call | solution.py:198
  7.1 4.3 %collective-permute-start = (bf16[16,128,128]{2,1,0:T(8,128)(2,1)S(1)}, bf16[16,128,128]{2,1,0:T(8,128)(2,1)S(1)}, u32[]{:S(2)}, u32[]{:S(2)}) collective-permute-start(bf16[16,128,128]{2,1,0:T(8,128)(2,1)S(1)} %get-tuple-element.32), channel_id=1, source_target_pairs={{0,128},{128,0},{1,129},{129,1},{2,130},{130,2},{3,131},{131,3},{4... | collective-permute-start | bytes 1572872 | tf_op jit(solution)/shard_map/ppermute | solution.py:368
  14.6 2.7 %collective-permute-start.3 = (bf16[4,128,128]{2,1,0:T(8,128)(2,1)S(1)}, bf16[4,128,128]{2,1,0:T(8,128)(2,1)S(1)}, u32[]{:S(2)}, u32[]{:S(2)}) collective-permute-start(bf16[4,128,128]{2,1,0:T(8,128)(2,1)S(1)} %get-tuple-element.39), channel_id=1, source_target_pairs={{0,3},{1,0},{2,1},{3,2},{4,7},{5,4},{6,5},{7,6},{8,11},{9,8},{10,9... | collective-permute-start | bytes 393224 | tf_op jit(solution)/shard_map/ppermute | solution.py:364
  17.3 3.1 %sort_by_col.1 = (s32[256]{0:T(256)S(1)}, s32[2]{0:T(128)S(1)}) custom-call(s32[256]{0:T(256)S(1)} %bitcast.14, s32[256]{0:T(256)S(1)} %bitcast.17, s32[1]{0:T(128)} %bitcast.11.count, s32[3]{0:T(128)S(1)} %pad_add_fusion.ids, f32[4,128,128]{2,1,0:T(8,128)S(1)} %get-tuple-element.33.after.own), custom_call_target="tpu_custom_call" | custom-call | flops 2000000000 | bytes 4096 | tf_op jit(solution)/shard_map/sort_by_col/pallas_call | solution.py:120
  20.4 3.0 %collective-permute-done.2.b = bf16[4,128,128]{2,1,0:T(8,128)(2,1)S(1)} collective-permute-done((bf16[4,128,128]{2,1,0:T(8,128)(2,1)S(1)}, bf16[4,128,128]{2,1,0:T(8,128)(2,1)S(1)}, u32[]{:S(2)}, u32[]{:S(2)}) %collective-permute-start.2) | collective-permute-done | bytes 131104 | tf_op jit(solution)/shard_map/ppermute | solution.py:364
  27.3 2.4 %collective-permute-done.6.refs_3_ = bf16[4,128,128]{2,1,0:T(8,128)(2,1)S(1)} collective-permute-done((bf16[4,128,128]{2,1,0:T(8,128)(2,1)S(1)}, bf16[4,128,128]{2,1,0:T(8,128)(2,1)S(1)}, u32[]{:S(2)}, u32[]{:S(2)}) %collective-permute-start.6) | collective-permute-done | bytes 131104 | tf_op jit(solution)/shard_map/ppermute | solution.py:364
  29.8 2.3 %collective-permute-start.10 = (bf16[4,128,128]{2,1,0:T(8,128)(2,1)S(1)}, bf16[4,128,128]{2,1,0:T(8,128)(2,1)S(1)}, u32[]{:S(2)}, u32[]{:S(2)}) collective-permute-start(bf16[4,128,128]{2,1,0:T(8,128)(2,1)S(1)} %collective-permute-done.6.refs_3_), channel_id=1, source_target_pairs={{0,128},{128,0},{1,129},{129,1},{2,130},{130,2},{3,131},{131,3},{4... | collective-permute-start | bytes 393224 | tf_op jit(solution)/shard_map/ppermute | solution.py:368
  34.9 2.4 %back_send.1 = (bf16[32,128,128]{2,1,0:T(8,128)(2,1)S(1)}, bf16[32,128,128]{2,1,0:T(8,128)(2,1)S(1)}) custom-call(s32[256]{0:T(256)S(1)} %get-tuple-element.34.order, s32[2]{0:T(128)S(1)} %get-tuple-element.35.sorted_first.numbers, s32[3]{0:T(128)S(1)} %pad_add_fusion.ids, bf16[256,128,128]{2,1,0:T(8,128)(2,1)S(1)} %get-tuple-element.36.tiles, ...), custom_call_target="tpu_custom_call" | custom-call | tf_op jit(solution)/shard_map/back_send/pallas_call | solution.py:228
  38.3 2.2 %back_keep.1.keep = f32[33,128,128]{2,1,0:T(8,128)S(1)} custom-call(s32[256]{0:T(256)S(1)} %get-tuple-element.34.order, s32[2]{0:T(128)S(1)} %get-tuple-element.35.sorted_first.numbers, bf16[256,128,128]{2,1,0:T(8,128)(2,1)S(1)} %get-tuple-element.36.tiles, bf16[32,128,128]{2,1,0:T(8,128)(2,1)S(1)} %get-tuple-element.40.panel), custom_call_target="tpu_custom_call" | custom-call | flops 1073741824 | bytes 10485760 | tf_op jit(solution)/shard_map/back_keep/pallas_call | solution.py:255
  42.5 2.4 %collective-permute-start.14 = (bf16[8,128,128]{2,1,0:T(8,128)(2,1)S(1)}, bf16[8,128,128]{2,1,0:T(8,128)(2,1)S(1)}, u32[]{:S(2)}, u32[]{:S(2)}) collective-permute-start(bf16[8,128,128]{2,1,0:T(8,128)(2,1)S(1)} %get-tuple-element.47), channel_id=1, source_target_pairs={{0,96},{32,0},{64,32},{96,64},{1,97},{33,1},{65,33},{97,65},{2,98}... | collective-permute-start | bytes 786440 | tf_op jit(solution)/shard_map/ppermute | solution.py:364
  45.0 3.1 %sort_by_row.1 = (s32[256]{0:T(256)S(1)}, s32[2]{0:T(128)S(1)}) custom-call(s32[256]{0:T(256)S(1)} %bitcast.15, s32[256]{0:T(256)S(1)} %bitcast.18, s32[1]{0:T(128)} %bitcast.12.count, s32[3]{0:T(128)S(1)} %pad_add_fusion.ids, f32[8,128,128]{2,1,0:T(8,128)S(1)} %get-tuple-element.42.after.own), custom_call_target="tpu_custom_call" | custom-call | flops 2000000000 | bytes 4096 | tf_op jit(solution)/shard_map/sort_by_row/pallas_call | solution.py:120
  48.1 2.5 %collective-permute-done.12.a = bf16[8,128,128]{2,1,0:T(8,128)(2,1)S(1)} collective-permute-done((bf16[8,128,128]{2,1,0:T(8,128)(2,1)S(1)}, bf16[8,128,128]{2,1,0:T(8,128)(2,1)S(1)}, u32[]{:S(2)}, u32[]{:S(2)}) %collective-permute-start.12) | collective-permute-done | bytes 262176 | tf_op jit(solution)/shard_map/ppermute | solution.py:364
  50.6 6.3 %collective-permute-done.13.b = bf16[8,128,128]{2,1,0:T(8,128)(2,1)S(1)} collective-permute-done((bf16[8,128,128]{2,1,0:T(8,128)(2,1)S(1)}, bf16[8,128,128]{2,1,0:T(8,128)(2,1)S(1)}, u32[]{:S(2)}, u32[]{:S(2)}) %collective-permute-start.13) | collective-permute-done | bytes 262176 | tf_op jit(solution)/shard_map/ppermute | solution.py:364
  57.0 18.6 %all_to_all.10.got = bf16[8,128,128]{2,1,0:T(8,128)(2,1)S(1)} all-to-all(bf16[8,128,128]{2,1,0:T(8,128)(2,1)S(1)} %back_sum.1), channel_id=1, replica_groups=mesh['layer'=2,'x'=4,'z'=8,'col'=4] {'z'}, dimensions={0} | all-to-all | bytes 524288 | tf_op jit(solution)/shard_map/all_to_all | solution.py:401
  75.7 11.7 %all_to_all.11.refs_0_ = bf16[8,128,128]{2,1,0:T(8,128)(2,1)S(1)} all-to-all(bf16[8,128,128]{2,1,0:T(8,128)(2,1)S(1)} %get-tuple-element.48), channel_id=1, replica_groups=mesh['layer'=2,'x'=4,'z'=8,'col'=4] {'z'}, dimensions={0} | all-to-all | bytes 524288 | tf_op jit(solution)/shard_map/all_to_all | solution.py:410
  90.2 4.2 %collective-permute-start.18 = (bf16[8,128,128]{2,1,0:T(8,128)(2,1)S(1)}, bf16[8,128,128]{2,1,0:T(8,128)(2,1)S(1)}, u32[]{:S(2)}, u32[]{:S(2)}) collective-permute-start(bf16[8,128,128]{2,1,0:T(8,128)(2,1)S(1)} %all_to_all.11.refs_0_), channel_id=1, source_target_pairs={{0,128},{128,0},{1,129},{129,1},{2,130},{130,2},{3,131},{131,3},{4... | collective-permute-start | bytes 786440 | tf_op jit(solution)/shard_map/ppermute | solution.py:368
  94.4 6.2 %collective-permute-start.21 = (bf16[8,128,128]{2,1,0:T(8,128)(2,1)S(1)}, bf16[8,128,128]{2,1,0:T(8,128)(2,1)S(1)}, u32[]{:S(2)}, u32[]{:S(2)}) collective-permute-start(bf16[8,128,128]{2,1,0:T(8,128)(2,1)S(1)} %collective-permute-done.17.refs_3_), channel_id=1, source_target_pairs={{0,128},{128,0},{1,129},{129,1},{2,130},{130,2},{3,131},{131,3},{4... | collective-permute-start | bytes 786440 | tf_op jit(solution)/shard_map/ppermute | solution.py:368
  100.5 2.1 %collective-permute-start.20 = (bf16[8,128,128]{2,1,0:T(8,128)(2,1)S(1)}, bf16[8,128,128]{2,1,0:T(8,128)(2,1)S(1)}, u32[]{:S(2)}, u32[]{:S(2)}) collective-permute-start(bf16[8,128,128]{2,1,0:T(8,128)(2,1)S(1)} %collective-permute-done.16.refs_2_), channel_id=1, source_target_pairs={{0,128},{128,0},{1,129},{129,1},{2,130},{130,2},{3,131},{131,3},{4... | collective-permute-start | bytes 786440 | tf_op jit(solution)/shard_map/ppermute | solution.py:368
  104.4 2.4 %last_send.1 = (bf16[16,128,128]{2,1,0:T(8,128)(2,1)S(1)}, bf16[64,128,128]{2,1,0:T(8,128)(2,1)S(1)}) custom-call(s32[256]{0:T(256)S(1)} %get-tuple-element.43.order, s32[2]{0:T(128)S(1)} %get-tuple-element.44.sorted_first.numbers, s32[3]{0:T(128)S(1)} %pad_add_fusion.ids, bf16[256,128,128]{2,1,0:T(8,128)(2,1)S(1)} %get-tuple-element.36.tiles, ...), custom_call_target="tpu_custom_call" | custom-call | tf_op jit(solution)/shard_map/last_send/pallas_call | solution.py:228
  107.7 2.7 %last_keep.1 = (f32[17,128,128]{2,1,0:T(8,128)S(1)}, f32[32,128]{1,0:T(8,128)S(1)}) custom-call(s32[256]{0:T(256)S(1)} %get-tuple-element.43.order, s32[2]{0:T(128)S(1)} %get-tuple-element.44.sorted_first.numbers, bf16[256,128,128]{2,1,0:T(8,128)(2,1)S(1)} %get-tuple-element.36.tiles, bf16[64,128,128]{2,1,0:T(8,128)(2,1)S(1)} %get-tuple-element.49.panel), custom_call_target="tpu_custom_call" | custom-call | flops 1073741824 | bytes 10485760 | tf_op jit(solution)/shard_map/last_keep/pallas_call | solution.py:255
  111.1 1.6 %collective-permute-start.23 = (bf16[528,128]{1,0:T(8,128)(2,1)S(1)}, bf16[528,128]{1,0:T(8,128)(2,1)S(1)}, u32[]{:S(2)}, u32[]{:S(2)}) collective-permute-start(bf16[528,128]{1,0:T(8,128)(2,1)S(1)} %get-tuple-element.55), channel_id=1, source_target_pairs={{0,2},{1,3},{2,0},{3,1},{4,6},{5,7},{6,4},{7,5},{8,10},{9,11},{10,... | collective-permute-start | bytes 405512 | tf_op jit(solution)/shard_map/ppermute | solution.py:364
  112.8 2.7 %collective-permute-start.25 = (bf16[528,128]{1,0:T(8,128)(2,1)S(1)}, bf16[528,128]{1,0:T(8,128)(2,1)S(1)}, u32[]{:S(2)}, u32[]{:S(2)}) collective-permute-start(bf16[528,128]{1,0:T(8,128)(2,1)S(1)} %get-tuple-element.57), channel_id=1, source_target_pairs={{0,3},{1,0},{2,1},{3,2},{4,7},{5,4},{6,5},{7,6},{8,11},{9,8},{10,9... | collective-permute-start | bytes 405512 | tf_op jit(solution)/shard_map/ppermute | solution.py:364
  115.4 1.9 %collective-permute-done.23.a = bf16[528,128]{1,0:T(8,128)(2,1)S(1)} collective-permute-done((bf16[528,128]{1,0:T(8,128)(2,1)S(1)}, bf16[528,128]{1,0:T(8,128)(2,1)S(1)}, u32[]{:S(2)}, u32[]{:S(2)}) %collective-permute-start.23) | collective-permute-done | bytes 135200 | tf_op jit(solution)/shard_map/ppermute | solution.py:364
  117.3 3.8 %collective-permute-done.24.b = bf16[528,128]{1,0:T(8,128)(2,1)S(1)} collective-permute-done((bf16[528,128]{1,0:T(8,128)(2,1)S(1)}, bf16[528,128]{1,0:T(8,128)(2,1)S(1)}, u32[]{:S(2)}, u32[]{:S(2)}) %collective-permute-start.24) | collective-permute-done | bytes 135200 | tf_op jit(solution)/shard_map/ppermute | solution.py:364
  (49 shorter events, 20.3 us)
Async XLA Ops:
  7.1 5.9 %collective-permute-start = (bf16[16,128,128]{2,1,0:T(8,128)(2,1)S(1)}, bf16[16,128,128]{2,1,0:T(8,128)(2,1)S(1)}, u32[]{:S(2)}, u32[]{:S(2)}) collective-permute-start(bf16[16,128,128]{2,1,0:T(8,128)(2,1)S(1)} %get-tuple-element.32), channel_id=1, source_target_pairs={{0,128},{128,0},{1,129},{129,1},{2,130},{130,2},{3,131},{131,3},{4... | collective-permute-start | bytes 1572872 | tf_op jit(solution)/shard_map/ppermute | solution.py:368
  13.6 6.8 %collective-permute-start.1 = (bf16[4,128,128]{2,1,0:T(8,128)(2,1)S(1)}, bf16[4,128,128]{2,1,0:T(8,128)(2,1)S(1)}, u32[]{:S(2)}, u32[]{:S(2)}) collective-permute-start(bf16[4,128,128]{2,1,0:T(8,128)(2,1)S(1)} %get-tuple-element.37), channel_id=1, source_target_pairs={{0,2},{1,3},{2,0},{3,1},{4,6},{5,7},{6,4},{7,5},{8,10},{9,11},{10,... | collective-permute-start | bytes 393224 | tf_op jit(solution)/shard_map/ppermute | solution.py:364
  14.6 8.9 %collective-permute-start.2 = (bf16[4,128,128]{2,1,0:T(8,128)(2,1)S(1)}, bf16[4,128,128]{2,1,0:T(8,128)(2,1)S(1)}, u32[]{:S(2)}, u32[]{:S(2)}) collective-permute-start(bf16[4,128,128]{2,1,0:T(8,128)(2,1)S(1)} %get-tuple-element.38), channel_id=1, source_target_pairs={{0,1},{1,2},{2,3},{3,0},{4,5},{5,6},{6,7},{7,4},{8,9},{9,10},{10,1... | collective-permute-start | bytes 393224 | tf_op jit(solution)/shard_map/ppermute | solution.py:364
  14.6 8.9 %collective-permute-start.3 = (bf16[4,128,128]{2,1,0:T(8,128)(2,1)S(1)}, bf16[4,128,128]{2,1,0:T(8,128)(2,1)S(1)}, u32[]{:S(2)}, u32[]{:S(2)}) collective-permute-start(bf16[4,128,128]{2,1,0:T(8,128)(2,1)S(1)} %get-tuple-element.39), channel_id=1, source_target_pairs={{0,3},{1,0},{2,1},{3,2},{4,7},{5,4},{6,5},{7,6},{8,11},{9,8},{10,9... | collective-permute-start | bytes 393224 | tf_op jit(solution)/shard_map/ppermute | solution.py:364
  23.6 6.2 %collective-permute-start.6 = (bf16[4,128,128]{2,1,0:T(8,128)(2,1)S(1)}, bf16[4,128,128]{2,1,0:T(8,128)(2,1)S(1)}, u32[]{:S(2)}, u32[]{:S(2)}) collective-permute-start(bf16[4,128,128]{2,1,0:T(8,128)(2,1)S(1)} %first_sum.1.refs_0_), channel_id=1, source_target_pairs={{0,2},{1,3},{2,0},{3,1},{4,6},{5,7},{6,4},{7,5},{8,10},{9,11},{10,... | collective-permute-start | bytes 393224 | tf_op jit(solution)/shard_map/ppermute | solution.py:364
  24.5 7.5 %collective-permute-start.5 = (bf16[4,128,128]{2,1,0:T(8,128)(2,1)S(1)}, bf16[4,128,128]{2,1,0:T(8,128)(2,1)S(1)}, u32[]{:S(2)}, u32[]{:S(2)}) collective-permute-start(bf16[4,128,128]{2,1,0:T(8,128)(2,1)S(1)} %first_sum.1.refs_0_), channel_id=1, source_target_pairs={{0,3},{1,0},{2,1},{3,2},{4,7},{5,4},{6,5},{7,6},{8,11},{9,8},{10,9... | collective-permute-start | bytes 393224 | tf_op jit(solution)/shard_map/ppermute | solution.py:364
  25.0 7.9 %collective-permute-start.4 = (bf16[4,128,128]{2,1,0:T(8,128)(2,1)S(1)}, bf16[4,128,128]{2,1,0:T(8,128)(2,1)S(1)}, u32[]{:S(2)}, u32[]{:S(2)}) collective-permute-start(bf16[4,128,128]{2,1,0:T(8,128)(2,1)S(1)} %first_sum.1.refs_0_), channel_id=1, source_target_pairs={{0,1},{1,2},{2,3},{3,0},{4,5},{5,6},{6,7},{7,4},{8,9},{9,10},{10,1... | collective-permute-start | bytes 393224 | tf_op jit(solution)/shard_map/ppermute | solution.py:364
  26.0 7.9 %collective-permute-start.7 = (bf16[4,128,128]{2,1,0:T(8,128)(2,1)S(1)}, bf16[4,128,128]{2,1,0:T(8,128)(2,1)S(1)}, u32[]{:S(2)}, u32[]{:S(2)}) collective-permute-start(bf16[4,128,128]{2,1,0:T(8,128)(2,1)S(1)} %first_sum.1.refs_0_), channel_id=1, source_target_pairs={{0,128},{128,0},{1,129},{129,1},{2,130},{130,2},{3,131},{131,3},{4... | collective-permute-start | bytes 393224 | tf_op jit(solution)/shard_map/ppermute | solution.py:368
  29.8 4.1 %collective-permute-start.10 = (bf16[4,128,128]{2,1,0:T(8,128)(2,1)S(1)}, bf16[4,128,128]{2,1,0:T(8,128)(2,1)S(1)}, u32[]{:S(2)}, u32[]{:S(2)}) collective-permute-start(bf16[4,128,128]{2,1,0:T(8,128)(2,1)S(1)} %collective-permute-done.6.refs_3_), channel_id=1, source_target_pairs={{0,128},{128,0},{1,129},{129,1},{2,130},{130,2},{3,131},{131,3},{4... | collective-permute-start | bytes 393224 | tf_op jit(solution)/shard_map/ppermute | solution.py:368
  32.9 2.0 %collective-permute-start.8 = (bf16[4,128,128]{2,1,0:T(8,128)(2,1)S(1)}, bf16[4,128,128]{2,1,0:T(8,128)(2,1)S(1)}, u32[]{:S(2)}, u32[]{:S(2)}) collective-permute-start(bf16[4,128,128]{2,1,0:T(8,128)(2,1)S(1)} %collective-permute-done.4.refs_1_), channel_id=1, source_target_pairs={{0,128},{128,0},{1,129},{129,1},{2,130},{130,2},{3,131},{131,3},{4... | collective-permute-start | bytes 393224 | tf_op jit(solution)/shard_map/ppermute | solution.py:368
  37.2 3.4 %collective-permute-start.11 = (bf16[32,128,128]{2,1,0:T(8,128)(2,1)S(1)}, bf16[32,128,128]{2,1,0:T(8,128)(2,1)S(1)}, u32[]{:S(2)}, u32[]{:S(2)}) collective-permute-start(bf16[32,128,128]{2,1,0:T(8,128)(2,1)S(1)} %get-tuple-element.41), channel_id=1, source_target_pairs={{0,128},{128,0},{1,129},{129,1},{2,130},{130,2},{3,131},{131,3},{4... | collective-permute-start | bytes 3145736 | tf_op jit(solution)/shard_map/ppermute | solution.py:368
  41.5 9.2 %collective-permute-start.12 = (bf16[8,128,128]{2,1,0:T(8,128)(2,1)S(1)}, bf16[8,128,128]{2,1,0:T(8,128)(2,1)S(1)}, u32[]{:S(2)}, u32[]{:S(2)}) collective-permute-start(bf16[8,128,128]{2,1,0:T(8,128)(2,1)S(1)} %get-tuple-element.45), channel_id=1, source_target_pairs={{0,64},{32,96},{64,0},{96,32},{1,65},{33,97},{65,1},{97,33},{2,66}... | collective-permute-start | bytes 786440 | tf_op jit(solution)/shard_map/ppermute | solution.py:364
  42.3 14.6 %collective-permute-start.13 = (bf16[8,128,128]{2,1,0:T(8,128)(2,1)S(1)}, bf16[8,128,128]{2,1,0:T(8,128)(2,1)S(1)}, u32[]{:S(2)}, u32[]{:S(2)}) collective-permute-start(bf16[8,128,128]{2,1,0:T(8,128)(2,1)S(1)} %get-tuple-element.46), channel_id=1, source_target_pairs={{0,32},{32,64},{64,96},{96,0},{1,33},{33,65},{65,97},{97,1},{2,34}... | collective-permute-start | bytes 786440 | tf_op jit(solution)/shard_map/ppermute | solution.py:364
  42.5 14.4 %collective-permute-start.14 = (bf16[8,128,128]{2,1,0:T(8,128)(2,1)S(1)}, bf16[8,128,128]{2,1,0:T(8,128)(2,1)S(1)}, u32[]{:S(2)}, u32[]{:S(2)}) collective-permute-start(bf16[8,128,128]{2,1,0:T(8,128)(2,1)S(1)} %get-tuple-element.47), channel_id=1, source_target_pairs={{0,96},{32,0},{64,32},{96,64},{1,97},{33,1},{65,33},{97,65},{2,98}... | collective-permute-start | bytes 786440 | tf_op jit(solution)/shard_map/ppermute | solution.py:364
  87.4 7.0 %collective-permute-start.17 = (bf16[8,128,128]{2,1,0:T(8,128)(2,1)S(1)}, bf16[8,128,128]{2,1,0:T(8,128)(2,1)S(1)}, u32[]{:S(2)}, u32[]{:S(2)}) collective-permute-start(bf16[8,128,128]{2,1,0:T(8,128)(2,1)S(1)} %all_to_all.11.refs_0_), channel_id=1, source_target_pairs={{0,64},{32,96},{64,0},{96,32},{1,65},{33,97},{65,1},{97,33},{2,66}... | collective-permute-start | bytes 786440 | tf_op jit(solution)/shard_map/ppermute | solution.py:364
  88.7 11.8 %collective-permute-start.16 = (bf16[8,128,128]{2,1,0:T(8,128)(2,1)S(1)}, bf16[8,128,128]{2,1,0:T(8,128)(2,1)S(1)}, u32[]{:S(2)}, u32[]{:S(2)}) collective-permute-start(bf16[8,128,128]{2,1,0:T(8,128)(2,1)S(1)} %all_to_all.11.refs_0_), channel_id=1, source_target_pairs={{0,96},{32,0},{64,32},{96,64},{1,97},{33,1},{65,33},{97,65},{2,98}... | collective-permute-start | bytes 786440 | tf_op jit(solution)/shard_map/ppermute | solution.py:364
  89.6 13.0 %collective-permute-start.15 = (bf16[8,128,128]{2,1,0:T(8,128)(2,1)S(1)}, bf16[8,128,128]{2,1,0:T(8,128)(2,1)S(1)}, u32[]{:S(2)}, u32[]{:S(2)}) collective-permute-start(bf16[8,128,128]{2,1,0:T(8,128)(2,1)S(1)} %all_to_all.11.refs_0_), channel_id=1, source_target_pairs={{0,32},{32,64},{64,96},{96,0},{1,33},{33,65},{65,97},{97,1},{2,34}... | collective-permute-start | bytes 786440 | tf_op jit(solution)/shard_map/ppermute | solution.py:364
  90.2 13.1 %collective-permute-start.18 = (bf16[8,128,128]{2,1,0:T(8,128)(2,1)S(1)}, bf16[8,128,128]{2,1,0:T(8,128)(2,1)S(1)}, u32[]{:S(2)}, u32[]{:S(2)}) collective-permute-start(bf16[8,128,128]{2,1,0:T(8,128)(2,1)S(1)} %all_to_all.11.refs_0_), channel_id=1, source_target_pairs={{0,128},{128,0},{1,129},{129,1},{2,130},{130,2},{3,131},{131,3},{4... | collective-permute-start | bytes 786440 | tf_op jit(solution)/shard_map/ppermute | solution.py:368
  94.4 8.9 %collective-permute-start.21 = (bf16[8,128,128]{2,1,0:T(8,128)(2,1)S(1)}, bf16[8,128,128]{2,1,0:T(8,128)(2,1)S(1)}, u32[]{:S(2)}, u32[]{:S(2)}) collective-permute-start(bf16[8,128,128]{2,1,0:T(8,128)(2,1)S(1)} %collective-permute-done.17.refs_3_), channel_id=1, source_target_pairs={{0,128},{128,0},{1,129},{129,1},{2,130},{130,2},{3,131},{131,3},{4... | collective-permute-start | bytes 786440 | tf_op jit(solution)/shard_map/ppermute | solution.py:368
  100.5 3.2 %collective-permute-start.20 = (bf16[8,128,128]{2,1,0:T(8,128)(2,1)S(1)}, bf16[8,128,128]{2,1,0:T(8,128)(2,1)S(1)}, u32[]{:S(2)}, u32[]{:S(2)}) collective-permute-start(bf16[8,128,128]{2,1,0:T(8,128)(2,1)S(1)} %collective-permute-done.16.refs_2_), channel_id=1, source_target_pairs={{0,128},{128,0},{1,129},{129,1},{2,130},{130,2},{3,131},{131,3},{4... | collective-permute-start | bytes 786440 | tf_op jit(solution)/shard_map/ppermute | solution.py:368
  106.8 3.7 %collective-permute-start.22 = (bf16[16,128,128]{2,1,0:T(8,128)(2,1)S(1)}, bf16[16,128,128]{2,1,0:T(8,128)(2,1)S(1)}, u32[]{:S(2)}, u32[]{:S(2)}) collective-permute-start(bf16[16,128,128]{2,1,0:T(8,128)(2,1)S(1)} %get-tuple-element.51), channel_id=1, source_target_pairs={{0,128},{128,0},{1,129},{129,1},{2,130},{130,2},{3,131},{131,3},{4... | collective-permute-start | bytes 1572872 | tf_op jit(solution)/shard_map/ppermute | solution.py:368
  111.1 6.2 %collective-permute-start.23 = (bf16[528,128]{1,0:T(8,128)(2,1)S(1)}, bf16[528,128]{1,0:T(8,128)(2,1)S(1)}, u32[]{:S(2)}, u32[]{:S(2)}) collective-permute-start(bf16[528,128]{1,0:T(8,128)(2,1)S(1)} %get-tuple-element.55), channel_id=1, source_target_pairs={{0,2},{1,3},{2,0},{3,1},{4,6},{5,7},{6,4},{7,5},{8,10},{9,11},{10,... | collective-permute-start | bytes 405512 | tf_op jit(solution)/shard_map/ppermute | solution.py:364
  112.8 8.4 %collective-permute-start.24 = (bf16[528,128]{1,0:T(8,128)(2,1)S(1)}, bf16[528,128]{1,0:T(8,128)(2,1)S(1)}, u32[]{:S(2)}, u32[]{:S(2)}) collective-permute-start(bf16[528,128]{1,0:T(8,128)(2,1)S(1)} %get-tuple-element.56), channel_id=1, source_target_pairs={{0,1},{1,2},{2,3},{3,0},{4,5},{5,6},{6,7},{7,4},{8,9},{9,10},{10,1... | collective-permute-start | bytes 405512 | tf_op jit(solution)/shard_map/ppermute | solution.py:364
  112.8 8.4 %collective-permute-start.25 = (bf16[528,128]{1,0:T(8,128)(2,1)S(1)}, bf16[528,128]{1,0:T(8,128)(2,1)S(1)}, u32[]{:S(2)}, u32[]{:S(2)}) collective-permute-start(bf16[528,128]{1,0:T(8,128)(2,1)S(1)} %get-tuple-element.57), channel_id=1, source_target_pairs={{0,3},{1,0},{2,1},{3,2},{4,7},{5,4},{6,5},{7,6},{8,11},{9,8},{10,9... | collective-permute-start | bytes 405512 | tf_op jit(solution)/shard_map/ppermute | solution.py:364
  (4 other events, 35.5 us)

commit v5 on v4

--- a/solution.py
+++ b/solution.py
@@ -20,7 +20,7 @@
 SLOT_BITS, ROW_BITS, COL_BITS = 8, 5, 6
 BLOCK = 32
 UNROLL = 32
-STEPS = 4
+STEPS = 8
 SORT_STEP = 16
 SHIFTS = (0, 2, 1, 3)
 GATHER_SHIFTS = (0, 1, 3, 2)

time: 121 us -> 122 us (level)
  starting transfers between devices: 40.7 us -> 39.4 us
    ppermute x15, starting transfers between devices: 16.7 us -> 14.9 us  [shifted(): return lax.ppermute(value, axis, [(i, (i + k) % n) for i in range(n)])]
  transfers between devices with their start and end apart: 26 -> 26, of which waited for: 12 -> 12; matrix products, arithmetic and copies ran while one was open for 0% -> 0% of each run, Pallas kernels for 9% -> 10%
where the time goes in v5:
time: 122 us
  starting transfers between devices  39.4 us (32%)
  blocking collectives  30.1 us (25%)
  waiting for transfers between devices  25.8 us (21%)
  Pallas kernels  25.1 us (21%)
  between operations  1.42 us (1%)
    ppermute x11, starting transfers between devices, swap(): return lax.ppermute(value, 'layer', [(0, 1), (1, 0)])  24.6 us
    ppermute x15, waiting for transfers between devices, shifted(): return lax.ppermute(value, axis, [(i, (i + k) % n) for i in range(n)])  22 us
    all_to_all x1, blocking collectives, on_device(): got = lax.all_to_all(part, 'z', split_axis=0, concat_axis=0, tiled=True)  18.5 us
    ppermute x15, starting transfers between devices, shifted(): return lax.ppermute(value, axis, [(i, (i + k) % n) for i in range(n)])  14.9 us
    all_to_all x1, blocking collectives, on_device(): part = lax.all_to_all(copies, 'z', split_axis=0, concat_axis=0, tiled=True)  11.6 us
    pallas_call x2, Pallas kernels, sort_list(): pl.pallas_call(functools.partial(sort_kernel, by_row=by_row), in_specs=[S...  6.24 us
    pallas_call x1, Pallas kernels, first_pass(): pl.pallas_call(first_kernel, in_specs=[HBM, HBM, SMEM, SMEM, HBM, HBM], o...  5.73 us
    pallas_call x2, Pallas kernels, keep_part(): pl.pallas_call(functools.partial(keep_kernel, by_row=by_row), in_specs=[S...  5.36 us
  transfers between devices with their start and end apart: 26, of which 12 were waited for; matrix products, arithmetic and copies ran while one was open for 0% of the time, Pallas kernels for 10%

profile of v5, /device:TPU:1, one launch (start us, length us, event | category | flops | bytes accessed | tf_op | source)
XLA Modules:
  0.0 122.0 jit_solution(4510537923973958275)
XLA Ops:
  1.4 5.7 %first_pass.1 = (f32[16,128,128]{2,1,0:T(8,128)S(1)}, bf16[16,128,128]{2,1,0:T(8,128)(2,1)S(1)}, bf16[256,128,128]{2,1,0:T(8,128)(2,1)S(1)}) custom-call(s32[256]{0:T(256)} %bitcast.13, s32[256]{0:T(256)} %bitcast.16, s32[1]{0:T(128)} %bitcast.10.count, s32[3]{0:T(128)S(1)} %pad_add_fusion.ids, bf16[256,128,128]{2,1,0:T(8,128)(2,1)} %bitcast.19, ...), custom_call_target="tpu_custom_call" | custom-call | tf_op jit(solution)/shard_map/first_pass/pallas_call | solution.py:198
  7.1 4.3 %collective-permute-start = (bf16[16,128,128]{2,1,0:T(8,128)(2,1)S(1)}, bf16[16,128,128]{2,1,0:T(8,128)(2,1)S(1)}, u32[]{:S(2)}, u32[]{:S(2)}) collective-permute-start(bf16[16,128,128]{2,1,0:T(8,128)(2,1)S(1)} %get-tuple-element.32), channel_id=1, source_target_pairs={{0,128},{128,0},{1,129},{129,1},{2,130},{130,2},{3,131},{131,3},{4... | collective-permute-start | bytes 1572872 | tf_op jit(solution)/shard_map/ppermute | solution.py:368
  13.9 2.7 %collective-permute-start.3 = (bf16[4,128,128]{2,1,0:T(8,128)(2,1)S(1)}, bf16[4,128,128]{2,1,0:T(8,128)(2,1)S(1)}, u32[]{:S(2)}, u32[]{:S(2)}) collective-permute-start(bf16[4,128,128]{2,1,0:T(8,128)(2,1)S(1)} %get-tuple-element.39), channel_id=1, source_target_pairs={{0,3},{1,0},{2,1},{3,2},{4,7},{5,4},{6,5},{7,6},{8,11},{9,8},{10,9... | collective-permute-start | bytes 393224 | tf_op jit(solution)/shard_map/ppermute | solution.py:364
  16.5 3.1 %sort_by_col.1 = (s32[256]{0:T(256)S(1)}, s32[2]{0:T(128)S(1)}) custom-call(s32[256]{0:T(256)S(1)} %bitcast.14, s32[256]{0:T(256)S(1)} %bitcast.17, s32[1]{0:T(128)} %bitcast.11.count, s32[3]{0:T(128)S(1)} %pad_add_fusion.ids, f32[4,128,128]{2,1,0:T(8,128)S(1)} %get-tuple-element.33.after.own), custom_call_target="tpu_custom_call" | custom-call | flops 2000000000 | bytes 4096 | tf_op jit(solution)/shard_map/sort_by_col/pallas_call | solution.py:120
  19.9 3.2 %collective-permute-done.2.b = bf16[4,128,128]{2,1,0:T(8,128)(2,1)S(1)} collective-permute-done((bf16[4,128,128]{2,1,0:T(8,128)(2,1)S(1)}, bf16[4,128,128]{2,1,0:T(8,128)(2,1)S(1)}, u32[]{:S(2)}, u32[]{:S(2)}) %collective-permute-start.2) | collective-permute-done | bytes 131104 | tf_op jit(solution)/shard_map/ppermute | solution.py:364
  26.6 2.7 %collective-permute-done.6.refs_3_ = bf16[4,128,128]{2,1,0:T(8,128)(2,1)S(1)} collective-permute-done((bf16[4,128,128]{2,1,0:T(8,128)(2,1)S(1)}, bf16[4,128,128]{2,1,0:T(8,128)(2,1)S(1)}, u32[]{:S(2)}, u32[]{:S(2)}) %collective-permute-start.6) | collective-permute-done | bytes 131104 | tf_op jit(solution)/shard_map/ppermute | solution.py:364
  29.4 2.5 %collective-permute-start.10 = (bf16[4,128,128]{2,1,0:T(8,128)(2,1)S(1)}, bf16[4,128,128]{2,1,0:T(8,128)(2,1)S(1)}, u32[]{:S(2)}, u32[]{:S(2)}) collective-permute-start(bf16[4,128,128]{2,1,0:T(8,128)(2,1)S(1)} %collective-permute-done.6.refs_3_), channel_id=1, source_target_pairs={{0,128},{128,0},{1,129},{129,1},{2,130},{130,2},{3,131},{131,3},{4... | collective-permute-start | bytes 393224 | tf_op jit(solution)/shard_map/ppermute | solution.py:368
  34.6 2.3 %back_send.1 = (bf16[32,128,128]{2,1,0:T(8,128)(2,1)S(1)}, bf16[32,128,128]{2,1,0:T(8,128)(2,1)S(1)}) custom-call(s32[256]{0:T(256)S(1)} %get-tuple-element.34.order, s32[2]{0:T(128)S(1)} %get-tuple-element.35.sorted_first.numbers, s32[3]{0:T(128)S(1)} %pad_add_fusion.ids, bf16[256,128,128]{2,1,0:T(8,128)(2,1)S(1)} %get-tuple-element.36.tiles, ...), custom_call_target="tpu_custom_call" | custom-call | tf_op jit(solution)/shard_map/back_send/pallas_call | solution.py:228
  38.1 2.2 %back_keep.1.keep = f32[33,128,128]{2,1,0:T(8,128)S(1)} custom-call(s32[256]{0:T(256)S(1)} %get-tuple-element.34.order, s32[2]{0:T(128)S(1)} %get-tuple-element.35.sorted_first.numbers, bf16[256,128,128]{2,1,0:T(8,128)(2,1)S(1)} %get-tuple-element.36.tiles, bf16[32,128,128]{2,1,0:T(8,128)(2,1)S(1)} %get-tuple-element.40.panel), custom_call_target="tpu_custom_call" | custom-call | flops 1073741824 | bytes 10485760 | tf_op jit(solution)/shard_map/back_keep/pallas_call | solution.py:255
  42.7 2.7 %collective-permute-start.14 = (bf16[8,128,128]{2,1,0:T(8,128)(2,1)S(1)}, bf16[8,128,128]{2,1,0:T(8,128)(2,1)S(1)}, u32[]{:S(2)}, u32[]{:S(2)}) collective-permute-start(bf16[8,128,128]{2,1,0:T(8,128)(2,1)S(1)} %get-tuple-element.47), channel_id=1, source_target_pairs={{0,96},{32,0},{64,32},{96,64},{1,97},{33,1},{65,33},{97,65},{2,98}... | collective-permute-start | bytes 786440 | tf_op jit(solution)/shard_map/ppermute | solution.py:364
  45.4 3.1 %sort_by_row.1 = (s32[256]{0:T(256)S(1)}, s32[2]{0:T(128)S(1)}) custom-call(s32[256]{0:T(256)S(1)} %bitcast.15, s32[256]{0:T(256)S(1)} %bitcast.18, s32[1]{0:T(128)} %bitcast.12.count, s32[3]{0:T(128)S(1)} %pad_add_fusion.ids, f32[8,128,128]{2,1,0:T(8,128)S(1)} %get-tuple-element.42.after.own), custom_call_target="tpu_custom_call" | custom-call | flops 2000000000 | bytes 4096 | tf_op jit(solution)/shard_map/sort_by_row/pallas_call | solution.py:120
  48.5 1.8 %collective-permute-done.12.a = bf16[8,128,128]{2,1,0:T(8,128)(2,1)S(1)} collective-permute-done((bf16[8,128,128]{2,1,0:T(8,128)(2,1)S(1)}, bf16[8,128,128]{2,1,0:T(8,128)(2,1)S(1)}, u32[]{:S(2)}, u32[]{:S(2)}) %collective-permute-start.12) | collective-permute-done | bytes 262176 | tf_op jit(solution)/shard_map/ppermute | solution.py:364
  50.3 6.3 %collective-permute-done.13.b = bf16[8,128,128]{2,1,0:T(8,128)(2,1)S(1)} collective-permute-done((bf16[8,128,128]{2,1,0:T(8,128)(2,1)S(1)}, bf16[8,128,128]{2,1,0:T(8,128)(2,1)S(1)}, u32[]{:S(2)}, u32[]{:S(2)}) %collective-permute-start.13) | collective-permute-done | bytes 262176 | tf_op jit(solution)/shard_map/ppermute | solution.py:364
  56.7 18.5 %all_to_all.10.got = bf16[8,128,128]{2,1,0:T(8,128)(2,1)S(1)} all-to-all(bf16[8,128,128]{2,1,0:T(8,128)(2,1)S(1)} %back_sum.1), channel_id=1, replica_groups=mesh['layer'=2,'x'=4,'z'=8,'col'=4] {'z'}, dimensions={0} | all-to-all | bytes 524288 | tf_op jit(solution)/shard_map/all_to_all | solution.py:401
  75.3 11.6 %all_to_all.11.refs_0_ = bf16[8,128,128]{2,1,0:T(8,128)(2,1)S(1)} all-to-all(bf16[8,128,128]{2,1,0:T(8,128)(2,1)S(1)} %get-tuple-element.48), channel_id=1, replica_groups=mesh['layer'=2,'x'=4,'z'=8,'col'=4] {'z'}, dimensions={0} | all-to-all | bytes 524288 | tf_op jit(solution)/shard_map/all_to_all | solution.py:410
  87.8 2.2 %collective-permute-start.16 = (bf16[8,128,128]{2,1,0:T(8,128)(2,1)S(1)}, bf16[8,128,128]{2,1,0:T(8,128)(2,1)S(1)}, u32[]{:S(2)}, u32[]{:S(2)}) collective-permute-start(bf16[8,128,128]{2,1,0:T(8,128)(2,1)S(1)} %all_to_all.11.refs_0_), channel_id=1, source_target_pairs={{0,96},{32,0},{64,32},{96,64},{1,97},{33,1},{65,33},{97,65},{2,98}... | collective-permute-start | bytes 786440 | tf_op jit(solution)/shard_map/ppermute | solution.py:364
  90.0 3.9 %collective-permute-start.18 = (bf16[8,128,128]{2,1,0:T(8,128)(2,1)S(1)}, bf16[8,128,128]{2,1,0:T(8,128)(2,1)S(1)}, u32[]{:S(2)}, u32[]{:S(2)}) collective-permute-start(bf16[8,128,128]{2,1,0:T(8,128)(2,1)S(1)} %all_to_all.11.refs_0_), channel_id=1, source_target_pairs={{0,128},{128,0},{1,129},{129,1},{2,130},{130,2},{3,131},{131,3},{4... | collective-permute-start | bytes 786440 | tf_op jit(solution)/shard_map/ppermute | solution.py:368
  93.9 6.2 %collective-permute-start.21 = (bf16[8,128,128]{2,1,0:T(8,128)(2,1)S(1)}, bf16[8,128,128]{2,1,0:T(8,128)(2,1)S(1)}, u32[]{:S(2)}, u32[]{:S(2)}) collective-permute-start(bf16[8,128,128]{2,1,0:T(8,128)(2,1)S(1)} %collective-permute-done.17.refs_3_), channel_id=1, source_target_pairs={{0,128},{128,0},{1,129},{129,1},{2,130},{130,2},{3,131},{131,3},{4... | collective-permute-start | bytes 786440 | tf_op jit(solution)/shard_map/ppermute | solution.py:368
  101.2 1.6 %collective-permute-start.19 = (bf16[8,128,128]{2,1,0:T(8,128)(2,1)S(1)}, bf16[8,128,128]{2,1,0:T(8,128)(2,1)S(1)}, u32[]{:S(2)}, u32[]{:S(2)}) collective-permute-start(bf16[8,128,128]{2,1,0:T(8,128)(2,1)S(1)} %collective-permute-done.15.refs_1_), channel_id=1, source_target_pairs={{0,128},{128,0},{1,129},{129,1},{2,130},{130,2},{3,131},{131,3},{4... | collective-permute-start | bytes 786440 | tf_op jit(solution)/shard_map/ppermute | solution.py:368
  104.0 2.3 %last_send.1 = (bf16[16,128,128]{2,1,0:T(8,128)(2,1)S(1)}, bf16[64,128,128]{2,1,0:T(8,128)(2,1)S(1)}) custom-call(s32[256]{0:T(256)S(1)} %get-tuple-element.43.order, s32[2]{0:T(128)S(1)} %get-tuple-element.44.sorted_first.numbers, s32[3]{0:T(128)S(1)} %pad_add_fusion.ids, bf16[256,128,128]{2,1,0:T(8,128)(2,1)S(1)} %get-tuple-element.36.tiles, ...), custom_call_target="tpu_custom_call" | custom-call | tf_op jit(solution)/shard_map/last_send/pallas_call | solution.py:228
  107.8 3.2 %last_keep.1 = (f32[17,128,128]{2,1,0:T(8,128)S(1)}, f32[32,128]{1,0:T(8,128)S(1)}) custom-call(s32[256]{0:T(256)S(1)} %get-tuple-element.43.order, s32[2]{0:T(128)S(1)} %get-tuple-element.44.sorted_first.numbers, bf16[256,128,128]{2,1,0:T(8,128)(2,1)S(1)} %get-tuple-element.36.tiles, bf16[64,128,128]{2,1,0:T(8,128)(2,1)S(1)} %get-tuple-element.49.panel), custom_call_target="tpu_custom_call" | custom-call | flops 1073741824 | bytes 10485760 | tf_op jit(solution)/shard_map/last_keep/pallas_call | solution.py:255
  112.8 1.7 %collective-permute-start.25 = (bf16[528,128]{1,0:T(8,128)(2,1)S(1)}, bf16[528,128]{1,0:T(8,128)(2,1)S(1)}, u32[]{:S(2)}, u32[]{:S(2)}) collective-permute-start(bf16[528,128]{1,0:T(8,128)(2,1)S(1)} %get-tuple-element.57), channel_id=1, source_target_pairs={{0,3},{1,0},{2,1},{3,2},{4,7},{5,4},{6,5},{7,6},{8,11},{9,8},{10,9... | collective-permute-start | bytes 405512 | tf_op jit(solution)/shard_map/ppermute | solution.py:364
  114.5 4.3 %collective-permute-done.23.a = bf16[528,128]{1,0:T(8,128)(2,1)S(1)} collective-permute-done((bf16[528,128]{1,0:T(8,128)(2,1)S(1)}, bf16[528,128]{1,0:T(8,128)(2,1)S(1)}, u32[]{:S(2)}, u32[]{:S(2)}) %collective-permute-start.23) | collective-permute-done | bytes 135200 | tf_op jit(solution)/shard_map/ppermute | solution.py:364
  118.8 2.4 %collective-permute-done.24.b = bf16[528,128]{1,0:T(8,128)(2,1)S(1)} collective-permute-done((bf16[528,128]{1,0:T(8,128)(2,1)S(1)}, bf16[528,128]{1,0:T(8,128)(2,1)S(1)}, u32[]{:S(2)}, u32[]{:S(2)}) %collective-permute-start.24) | collective-permute-done | bytes 135200 | tf_op jit(solution)/shard_map/ppermute | solution.py:364
  (49 shorter events, 19.8 us)
Async XLA Ops:
  7.1 5.9 %collective-permute-start = (bf16[16,128,128]{2,1,0:T(8,128)(2,1)S(1)}, bf16[16,128,128]{2,1,0:T(8,128)(2,1)S(1)}, u32[]{:S(2)}, u32[]{:S(2)}) collective-permute-start(bf16[16,128,128]{2,1,0:T(8,128)(2,1)S(1)} %get-tuple-element.32), channel_id=1, source_target_pairs={{0,128},{128,0},{1,129},{129,1},{2,130},{130,2},{3,131},{131,3},{4... | collective-permute-start | bytes 1572872 | tf_op jit(solution)/shard_map/ppermute | solution.py:368
  13.6 6.3 %collective-permute-start.1 = (bf16[4,128,128]{2,1,0:T(8,128)(2,1)S(1)}, bf16[4,128,128]{2,1,0:T(8,128)(2,1)S(1)}, u32[]{:S(2)}, u32[]{:S(2)}) collective-permute-start(bf16[4,128,128]{2,1,0:T(8,128)(2,1)S(1)} %get-tuple-element.37), channel_id=1, source_target_pairs={{0,2},{1,3},{2,0},{3,1},{4,6},{5,7},{6,4},{7,5},{8,10},{9,11},{10,... | collective-permute-start | bytes 393224 | tf_op jit(solution)/shard_map/ppermute | solution.py:364
  13.9 9.3 %collective-permute-start.2 = (bf16[4,128,128]{2,1,0:T(8,128)(2,1)S(1)}, bf16[4,128,128]{2,1,0:T(8,128)(2,1)S(1)}, u32[]{:S(2)}, u32[]{:S(2)}) collective-permute-start(bf16[4,128,128]{2,1,0:T(8,128)(2,1)S(1)} %get-tuple-element.38), channel_id=1, source_target_pairs={{0,1},{1,2},{2,3},{3,0},{4,5},{5,6},{6,7},{7,4},{8,9},{9,10},{10,1... | collective-permute-start | bytes 393224 | tf_op jit(solution)/shard_map/ppermute | solution.py:364
  13.9 9.3 %collective-permute-start.3 = (bf16[4,128,128]{2,1,0:T(8,128)(2,1)S(1)}, bf16[4,128,128]{2,1,0:T(8,128)(2,1)S(1)}, u32[]{:S(2)}, u32[]{:S(2)}) collective-permute-start(bf16[4,128,128]{2,1,0:T(8,128)(2,1)S(1)} %get-tuple-element.39), channel_id=1, source_target_pairs={{0,3},{1,0},{2,1},{3,2},{4,7},{5,4},{6,5},{7,6},{8,11},{9,8},{10,9... | collective-permute-start | bytes 393224 | tf_op jit(solution)/shard_map/ppermute | solution.py:364
  23.3 6.0 %collective-permute-start.6 = (bf16[4,128,128]{2,1,0:T(8,128)(2,1)S(1)}, bf16[4,128,128]{2,1,0:T(8,128)(2,1)S(1)}, u32[]{:S(2)}, u32[]{:S(2)}) collective-permute-start(bf16[4,128,128]{2,1,0:T(8,128)(2,1)S(1)} %first_sum.1.refs_0_), channel_id=1, source_target_pairs={{0,2},{1,3},{2,0},{3,1},{4,6},{5,7},{6,4},{7,5},{8,10},{9,11},{10,... | collective-permute-start | bytes 393224 | tf_op jit(solution)/shard_map/ppermute | solution.py:364
  23.7 8.2 %collective-permute-start.5 = (bf16[4,128,128]{2,1,0:T(8,128)(2,1)S(1)}, bf16[4,128,128]{2,1,0:T(8,128)(2,1)S(1)}, u32[]{:S(2)}, u32[]{:S(2)}) collective-permute-start(bf16[4,128,128]{2,1,0:T(8,128)(2,1)S(1)} %first_sum.1.refs_0_), channel_id=1, source_target_pairs={{0,3},{1,0},{2,1},{3,2},{4,7},{5,4},{6,5},{7,6},{8,11},{9,8},{10,9... | collective-permute-start | bytes 393224 | tf_op jit(solution)/shard_map/ppermute | solution.py:364
  24.0 8.8 %collective-permute-start.4 = (bf16[4,128,128]{2,1,0:T(8,128)(2,1)S(1)}, bf16[4,128,128]{2,1,0:T(8,128)(2,1)S(1)}, u32[]{:S(2)}, u32[]{:S(2)}) collective-permute-start(bf16[4,128,128]{2,1,0:T(8,128)(2,1)S(1)} %first_sum.1.refs_0_), channel_id=1, source_target_pairs={{0,1},{1,2},{2,3},{3,0},{4,5},{5,6},{6,7},{7,4},{8,9},{9,10},{10,1... | collective-permute-start | bytes 393224 | tf_op jit(solution)/shard_map/ppermute | solution.py:364
  25.2 8.5 %collective-permute-start.7 = (bf16[4,128,128]{2,1,0:T(8,128)(2,1)S(1)}, bf16[4,128,128]{2,1,0:T(8,128)(2,1)S(1)}, u32[]{:S(2)}, u32[]{:S(2)}) collective-permute-start(bf16[4,128,128]{2,1,0:T(8,128)(2,1)S(1)} %first_sum.1.refs_0_), channel_id=1, source_target_pairs={{0,128},{128,0},{1,129},{129,1},{2,130},{130,2},{3,131},{131,3},{4... | collective-permute-start | bytes 393224 | tf_op jit(solution)/shard_map/ppermute | solution.py:368
  29.4 4.3 %collective-permute-start.10 = (bf16[4,128,128]{2,1,0:T(8,128)(2,1)S(1)}, bf16[4,128,128]{2,1,0:T(8,128)(2,1)S(1)}, u32[]{:S(2)}, u32[]{:S(2)}) collective-permute-start(bf16[4,128,128]{2,1,0:T(8,128)(2,1)S(1)} %collective-permute-done.6.refs_3_), channel_id=1, source_target_pairs={{0,128},{128,0},{1,129},{129,1},{2,130},{130,2},{3,131},{131,3},{4... | collective-permute-start | bytes 393224 | tf_op jit(solution)/shard_map/ppermute | solution.py:368
  37.0 3.4 %collective-permute-start.11 = (bf16[32,128,128]{2,1,0:T(8,128)(2,1)S(1)}, bf16[32,128,128]{2,1,0:T(8,128)(2,1)S(1)}, u32[]{:S(2)}, u32[]{:S(2)}) collective-permute-start(bf16[32,128,128]{2,1,0:T(8,128)(2,1)S(1)} %get-tuple-element.41), channel_id=1, source_target_pairs={{0,128},{128,0},{1,129},{129,1},{2,130},{130,2},{3,131},{131,3},{4... | collective-permute-start | bytes 3145736 | tf_op jit(solution)/shard_map/ppermute | solution.py:368
  41.1 9.1 %collective-permute-start.12 = (bf16[8,128,128]{2,1,0:T(8,128)(2,1)S(1)}, bf16[8,128,128]{2,1,0:T(8,128)(2,1)S(1)}, u32[]{:S(2)}, u32[]{:S(2)}) collective-permute-start(bf16[8,128,128]{2,1,0:T(8,128)(2,1)S(1)} %get-tuple-element.45), channel_id=1, source_target_pairs={{0,64},{32,96},{64,0},{96,32},{1,65},{33,97},{65,1},{97,33},{2,66}... | collective-permute-start | bytes 786440 | tf_op jit(solution)/shard_map/ppermute | solution.py:364
  42.7 13.9 %collective-permute-start.13 = (bf16[8,128,128]{2,1,0:T(8,128)(2,1)S(1)}, bf16[8,128,128]{2,1,0:T(8,128)(2,1)S(1)}, u32[]{:S(2)}, u32[]{:S(2)}) collective-permute-start(bf16[8,128,128]{2,1,0:T(8,128)(2,1)S(1)} %get-tuple-element.46), channel_id=1, source_target_pairs={{0,32},{32,64},{64,96},{96,0},{1,33},{33,65},{65,97},{97,1},{2,34}... | collective-permute-start | bytes 786440 | tf_op jit(solution)/shard_map/ppermute | solution.py:364
  42.7 13.9 %collective-permute-start.14 = (bf16[8,128,128]{2,1,0:T(8,128)(2,1)S(1)}, bf16[8,128,128]{2,1,0:T(8,128)(2,1)S(1)}, u32[]{:S(2)}, u32[]{:S(2)}) collective-permute-start(bf16[8,128,128]{2,1,0:T(8,128)(2,1)S(1)} %get-tuple-element.47), channel_id=1, source_target_pairs={{0,96},{32,0},{64,32},{96,64},{1,97},{33,1},{65,33},{97,65},{2,98}... | collective-permute-start | bytes 786440 | tf_op jit(solution)/shard_map/ppermute | solution.py:364
  87.0 6.9 %collective-permute-start.17 = (bf16[8,128,128]{2,1,0:T(8,128)(2,1)S(1)}, bf16[8,128,128]{2,1,0:T(8,128)(2,1)S(1)}, u32[]{:S(2)}, u32[]{:S(2)}) collective-permute-start(bf16[8,128,128]{2,1,0:T(8,128)(2,1)S(1)} %all_to_all.11.refs_0_), channel_id=1, source_target_pairs={{0,64},{32,96},{64,0},{96,32},{1,65},{33,97},{65,1},{97,33},{2,66}... | collective-permute-start | bytes 786440 | tf_op jit(solution)/shard_map/ppermute | solution.py:364
  87.8 12.3 %collective-permute-start.16 = (bf16[8,128,128]{2,1,0:T(8,128)(2,1)S(1)}, bf16[8,128,128]{2,1,0:T(8,128)(2,1)S(1)}, u32[]{:S(2)}, u32[]{:S(2)}) collective-permute-start(bf16[8,128,128]{2,1,0:T(8,128)(2,1)S(1)} %all_to_all.11.refs_0_), channel_id=1, source_target_pairs={{0,96},{32,0},{64,32},{96,64},{1,97},{33,1},{65,33},{97,65},{2,98}... | collective-permute-start | bytes 786440 | tf_op jit(solution)/shard_map/ppermute | solution.py:364
  90.0 11.3 %collective-permute-start.15 = (bf16[8,128,128]{2,1,0:T(8,128)(2,1)S(1)}, bf16[8,128,128]{2,1,0:T(8,128)(2,1)S(1)}, u32[]{:S(2)}, u32[]{:S(2)}) collective-permute-start(bf16[8,128,128]{2,1,0:T(8,128)(2,1)S(1)} %all_to_all.11.refs_0_), channel_id=1, source_target_pairs={{0,32},{32,64},{64,96},{96,0},{1,33},{33,65},{65,97},{97,1},{2,34}... | collective-permute-start | bytes 786440 | tf_op jit(solution)/shard_map/ppermute | solution.py:364
  90.0 12.9 %collective-permute-start.18 = (bf16[8,128,128]{2,1,0:T(8,128)(2,1)S(1)}, bf16[8,128,128]{2,1,0:T(8,128)(2,1)S(1)}, u32[]{:S(2)}, u32[]{:S(2)}) collective-permute-start(bf16[8,128,128]{2,1,0:T(8,128)(2,1)S(1)} %all_to_all.11.refs_0_), channel_id=1, source_target_pairs={{0,128},{128,0},{1,129},{129,1},{2,130},{130,2},{3,131},{131,3},{4... | collective-permute-start | bytes 786440 | tf_op jit(solution)/shard_map/ppermute | solution.py:368
  93.9 9.0 %collective-permute-start.21 = (bf16[8,128,128]{2,1,0:T(8,128)(2,1)S(1)}, bf16[8,128,128]{2,1,0:T(8,128)(2,1)S(1)}, u32[]{:S(2)}, u32[]{:S(2)}) collective-permute-start(bf16[8,128,128]{2,1,0:T(8,128)(2,1)S(1)} %collective-permute-done.17.refs_3_), channel_id=1, source_target_pairs={{0,128},{128,0},{1,129},{129,1},{2,130},{130,2},{3,131},{131,3},{4... | collective-permute-start | bytes 786440 | tf_op jit(solution)/shard_map/ppermute | solution.py:368
  100.1 2.7 %collective-permute-start.20 = (bf16[8,128,128]{2,1,0:T(8,128)(2,1)S(1)}, bf16[8,128,128]{2,1,0:T(8,128)(2,1)S(1)}, u32[]{:S(2)}, u32[]{:S(2)}) collective-permute-start(bf16[8,128,128]{2,1,0:T(8,128)(2,1)S(1)} %collective-permute-done.16.refs_2_), channel_id=1, source_target_pairs={{0,128},{128,0},{1,129},{129,1},{2,130},{130,2},{3,131},{131,3},{4... | collective-permute-start | bytes 786440 | tf_op jit(solution)/shard_map/ppermute | solution.py:368
  101.2 2.7 %collective-permute-start.19 = (bf16[8,128,128]{2,1,0:T(8,128)(2,1)S(1)}, bf16[8,128,128]{2,1,0:T(8,128)(2,1)S(1)}, u32[]{:S(2)}, u32[]{:S(2)}) collective-permute-start(bf16[8,128,128]{2,1,0:T(8,128)(2,1)S(1)} %collective-permute-done.15.refs_1_), channel_id=1, source_target_pairs={{0,128},{128,0},{1,129},{129,1},{2,130},{130,2},{3,131},{131,3},{4... | collective-permute-start | bytes 786440 | tf_op jit(solution)/shard_map/ppermute | solution.py:368
  106.3 4.7 %collective-permute-start.22 = (bf16[16,128,128]{2,1,0:T(8,128)(2,1)S(1)}, bf16[16,128,128]{2,1,0:T(8,128)(2,1)S(1)}, u32[]{:S(2)}, u32[]{:S(2)}) collective-permute-start(bf16[16,128,128]{2,1,0:T(8,128)(2,1)S(1)} %get-tuple-element.51), channel_id=1, source_target_pairs={{0,128},{128,0},{1,129},{129,1},{2,130},{130,2},{3,131},{131,3},{4... | collective-permute-start | bytes 1572872 | tf_op jit(solution)/shard_map/ppermute | solution.py:368
  111.6 7.2 %collective-permute-start.23 = (bf16[528,128]{1,0:T(8,128)(2,1)S(1)}, bf16[528,128]{1,0:T(8,128)(2,1)S(1)}, u32[]{:S(2)}, u32[]{:S(2)}) collective-permute-start(bf16[528,128]{1,0:T(8,128)(2,1)S(1)} %get-tuple-element.55), channel_id=1, source_target_pairs={{0,2},{1,3},{2,0},{3,1},{4,6},{5,7},{6,4},{7,5},{8,10},{9,11},{10,... | collective-permute-start | bytes 405512 | tf_op jit(solution)/shard_map/ppermute | solution.py:364
  111.7 9.5 %collective-permute-start.24 = (bf16[528,128]{1,0:T(8,128)(2,1)S(1)}, bf16[528,128]{1,0:T(8,128)(2,1)S(1)}, u32[]{:S(2)}, u32[]{:S(2)}) collective-permute-start(bf16[528,128]{1,0:T(8,128)(2,1)S(1)} %get-tuple-element.56), channel_id=1, source_target_pairs={{0,1},{1,2},{2,3},{3,0},{4,5},{5,6},{6,7},{7,4},{8,9},{9,10},{10,1... | collective-permute-start | bytes 405512 | tf_op jit(solution)/shard_map/ppermute | solution.py:364
  112.8 8.5 %collective-permute-start.25 = (bf16[528,128]{1,0:T(8,128)(2,1)S(1)}, bf16[528,128]{1,0:T(8,128)(2,1)S(1)}, u32[]{:S(2)}, u32[]{:S(2)}) collective-permute-start(bf16[528,128]{1,0:T(8,128)(2,1)S(1)} %get-tuple-element.57), channel_id=1, source_target_pairs={{0,3},{1,0},{2,1},{3,2},{4,7},{5,4},{6,5},{7,6},{8,11},{9,8},{10,9... | collective-permute-start | bytes 405512 | tf_op jit(solution)/shard_map/ppermute | solution.py:364
  (4 other events, 34.0 us)
